TPU v7x, 32 devices: a whole 2x2x4 slice. The times are simulated.
32 devices in a mesh: dp: 16 (over z, x, core), head: 2 (over y).
Axes of the slice: x: 2, y: 2, z: 4, core: 2. Of those that a mesh axis runs over, the one named last changes fastest.
Arguments:
- inputs: float32 [32, 1024, 1152], P('dp', 'head'), may hold values from -6 to 6
- cond: float32 [32, 1152], P(('dp', 'head')), may hold values from -6 to 6
- order: int32 [32], P('dp'), may hold values from 0 to 31, each once
- grid_kind: int32 [32], P('dp'), may hold values from 0 to 1
- weight_ada: float32 [1152, 6912], P('dp', 'head'), may hold values from -0.1875 to 0.1875
- bias_ada: float32 [6912], replicated, may hold values from -3 to 3
- weight_qkv: float32 [1152, 3456], P('dp', 'head'), may hold values from -0.1875 to 0.1875
- bias_query: float32 [1152], replicated, may hold values from -3 to 3
- bias_value: float32 [1152], replicated, may hold values from -2 to 2
- weight_out: float32 [1152, 1152], P('dp', 'head'), may hold values from -0.75 to 0.75
- bias_out: float32 [1152], replicated, may hold values from -2 to 2
- weight_up: float32 [1152, 4608], P('dp', 'head'), may hold values from -0.1875 to 0.1875
- bias_up: float32 [4608], replicated, may hold values from -3 to 3
- weight_down: float32 [4608, 1152], P('dp', 'head'), may hold values from -0.09375 to 0.09375
- bias_down: float32 [1152], replicated, may hold values from -2 to 2
- cotangent: float32 [32, 1024, 1152], P('dp', 'head'), may hold values from -6 to 6
Outputs:
- out_act: float32 [32, 1024, 1152], P('dp', 'head')
- input_grad: float32 [32, 1024, 1152], P('dp', 'head')
- cond_grad: float32 [32, 1152], P(('dp', 'head'))
- weight_ada_grad: float32 [1152, 6912], P('dp', 'head')
- weight_qkv_grad: float32 [1152, 3456], P('dp', 'head')
- weight_out_grad: float32 [1152, 1152], P('dp', 'head')
- weight_up_grad: float32 [1152, 4608], P('dp', 'head')
- weight_down_grad: float32 [4608, 1152], P('dp', 'head')
- bias_ada_grad: float32 [6912], replicated
- bias_query_grad: float32 [1152], replicated
- bias_value_grad: float32 [1152], replicated
- bias_out_grad: float32 [1152], replicated
- bias_up_grad: float32 [4608], replicated
- bias_down_grad: float32 [1152], replicated
Inputs may be any that keep to these rules, and one draw needn't show every extreme that they name: order lists every initial image exactly once.
All inputs are finite; a program needn't handle non-finite values.
Results may differ from a plain program's by a relative error of at most 0.02.
The roundings to bfloat16 on the way count: a program that leaves them out, or rounds other values in their place, can miss the bound.
Values may be sent and summed in bfloat16 or wider, within the bound.
A program may use at most 320 MiB of HBM per device.

v0:
```python
import jax
import jax.numpy as jnp
from jax import lax
from jax.sharding import PartitionSpec as P

H = 16


norm_eps = 1e-06
mask_fill = -1000000000.0


def layer_norm(values):
    center = values - jnp.mean(values, axis=-1, keepdims=True)
    spread = jnp.mean(center * center, axis=-1, keepdims=True)
    return center * lax.rsqrt(spread + norm_eps)


def modulate(values, offset, factor):
    return layer_norm(values) * (1.0 + factor[:, None, :]) + offset[:, None, :]


def gelu_tanh(values):
    inner_arg = 0.7978845608028654 * (values + 0.044715 * values * values * values)
    return 0.5 * values * (1.0 + jnp.tanh(inner_arg))


def silu_act(values):
    return values * jax.nn.sigmoid(values)


def fetch_weights(weight_ada, weight_qkv, weight_out, weight_up, weight_down):
    widened = (
        lax.all_gather(weight_ada.astype(jnp.bfloat16), "head", axis=1, tiled=True),
        lax.all_gather(weight_qkv.astype(jnp.bfloat16), "head", axis=1, tiled=True),
        lax.all_gather(weight_out.astype(jnp.bfloat16), "head", axis=1, tiled=True),
        lax.all_gather(weight_up.astype(jnp.bfloat16), "head", axis=1, tiled=True),
        lax.all_gather(weight_down.astype(jnp.bfloat16), "head", axis=1, tiled=True),
    )
    return (
        lax.all_gather(widened[0], "dp", axis=0, tiled=True),
        lax.all_gather(widened[1], "dp", axis=0, tiled=True),
        lax.all_gather(widened[2], "dp", axis=0, tiled=True),
        lax.all_gather(widened[3], "dp", axis=0, tiled=True),
        lax.all_gather(widened[4], "dp", axis=0, tiled=True),
    )


def masked_scores(queries, keys_in, valid_keys):
    score_scale = queries.shape[-1] ** (-0.5)
    scores = (
        jnp.einsum("bshd,bthd->bhst", queries, keys_in, preferred_element_type=jnp.float32)
        * score_scale
    )
    return jnp.where(valid_keys[:, None, None, :], scores, mask_fill)


def attend_block(operands):
    queries, keys_in, values_in, valid_keys = operands
    scores = masked_scores(queries, keys_in, valid_keys)
    row_peak = jnp.max(scores, axis=-1, keepdims=True)
    exponent = jnp.exp(scores - row_peak)
    row_total = jnp.sum(exponent, axis=-1, keepdims=True)
    soft_weights = (exponent / row_total).astype(jnp.bfloat16)
    attn_mix = jnp.einsum(
        "bhst,bthd->bshd", soft_weights, values_in, preferred_element_type=jnp.float32
    )
    return (attn_mix.astype(jnp.bfloat16), row_peak + jnp.log(row_total))


def attend_back(operands):
    queries, keys_in, values_in, valid_keys, log_total, grad_mix = operands
    score_scale = queries.shape[-1] ** (-0.5)
    soft_weights = jnp.exp(masked_scores(queries, keys_in, valid_keys) - log_total)
    grad_values = jnp.einsum(
        "bhst,bshd->bthd",
        soft_weights.astype(jnp.bfloat16),
        grad_mix,
        preferred_element_type=jnp.float32,
    )
    grad_soft = jnp.einsum(
        "bshd,bthd->bhst", grad_mix, values_in, preferred_element_type=jnp.float32
    )
    inner_term = jnp.sum(grad_soft * soft_weights, axis=-1, keepdims=True)
    grad_scores = (soft_weights * (grad_soft - inner_term)).astype(jnp.bfloat16)
    grad_queries = (
        jnp.einsum("bhst,bthd->bshd", grad_scores, keys_in, preferred_element_type=jnp.float32)
        * score_scale
    )
    grad_keys = (
        jnp.einsum("bhst,bshd->bthd", grad_scores, queries, preferred_element_type=jnp.float32)
        * score_scale
    )
    return (grad_queries, grad_keys, grad_values)


def block_layout(image_total, query_rows):
    block_images = max(1, 512 // query_rows)
    block_images = min(block_images, image_total)
    while image_total % block_images:
        block_images = block_images - 1
    return (image_total // block_images, block_images)


def body(
    inputs,
    cond,
    order,
    grid_kind,
    weight_ada,
    bias_ada,
    weight_qkv,
    bias_query,
    bias_value,
    weight_out,
    bias_out,
    weight_up,
    bias_up,
    weight_down,
    bias_down,
    cotangent,
):
    group_count, slot_local, model_width = inputs.shape
    head_count = lax.axis_size("head")
    head_index = lax.axis_index("head")
    unit_count = group_count // head_count
    slot_total = slot_local * head_count
    head_size = model_width // H
    head_local = H // head_count
    token_rows = group_count * slot_local
    counts = jnp.where(grid_kind == 0, slot_total, slot_total - slot_total // 16)
    full_weights = fetch_weights(weight_ada, weight_qkv, weight_out, weight_up, weight_down)
    ada_full, qkv_full, out_full, up_full, down_full = full_weights
    own_silu, silu_pull = jax.vjp(silu_act, cond)
    all_silu = lax.all_gather(own_silu.astype(jnp.bfloat16), ("dp", "head"), axis=0, tiled=True)
    image_silu = jnp.take(all_silu, order, axis=0)
    modulation = jnp.dot(image_silu, ada_full, preferred_element_type=jnp.float32) + bias_ada
    mod_parts = modulation.reshape(group_count, 6, model_width)
    gate_attn = mod_parts[:, 2][:, None, :]
    gate_mlp = mod_parts[:, 5][:, None, :]
    normed, first_pull = jax.vjp(modulate, inputs, mod_parts[:, 0], mod_parts[:, 1])
    normed_low = normed.astype(jnp.bfloat16).reshape(token_rows, model_width)
    bias_qkv = jnp.concatenate([bias_query, jnp.zeros_like(bias_query), bias_value])
    projected = (
        jnp.dot(normed_low, qkv_full, preferred_element_type=jnp.float32) + bias_qkv
    ).astype(jnp.bfloat16)
    valid_all = jnp.arange(slot_total, dtype=jnp.int32)[None, :] < counts[:, None]
    by_heads = lax.all_to_all(
        projected.reshape(group_count, slot_local, 3, head_count, model_width // head_count),
        "head",
        split_axis=3,
        concat_axis=1,
        tiled=True,
    )
    by_heads = by_heads.reshape(group_count, slot_total, 3, head_local, head_size)
    queries_flat = by_heads[:, :, 0]
    keys_flat = by_heads[:, :, 1]
    values_flat = by_heads[:, :, 2]
    block_total, block_images = block_layout(group_count, slot_total)

    def split_blocks(array):
        return array.reshape((block_total, block_images) + array.shape[1:])

    valid_keys = split_blocks(valid_all)
    queries = split_blocks(queries_flat)
    keys_in = split_blocks(keys_flat)
    values_in = split_blocks(values_flat)
    attn_mix, log_total = lax.map(attend_block, (queries, keys_in, values_in, valid_keys))
    attn_mix = attn_mix.reshape(group_count, slot_total, 1, head_local * head_size)
    attended = lax.all_to_all(attn_mix, "head", split_axis=1, concat_axis=2, tiled=True).reshape(
        token_rows, model_width
    )
    branch = (jnp.dot(attended, out_full, preferred_element_type=jnp.float32) + bias_out).reshape(
        group_count, slot_local, model_width
    )
    middle = inputs + gate_attn * branch
    second, second_pull = jax.vjp(modulate, middle, mod_parts[:, 3], mod_parts[:, 4])
    second_low = second.astype(jnp.bfloat16).reshape(token_rows, model_width)
    hidden_pre = jnp.dot(second_low, up_full, preferred_element_type=jnp.float32) + bias_up
    activ, gelu_pull = jax.vjp(gelu_tanh, hidden_pre)
    activ_low = activ.astype(jnp.bfloat16)
    mlp_out = (
        jnp.dot(activ_low, down_full, preferred_element_type=jnp.float32) + bias_down
    ).reshape(group_count, slot_local, model_width)
    result = middle + gate_mlp * mlp_out
    back_weights = fetch_weights(weight_ada, weight_qkv, weight_out, weight_up, weight_down)
    ada_back, qkv_back, out_back, up_back, down_back = back_weights
    grad_gate_mlp = jnp.sum(cotangent * mlp_out, axis=1)
    grad_mlp = (gate_mlp * cotangent).reshape(token_rows, model_width)
    grad_bias_down = jnp.sum(grad_mlp, axis=0)
    grad_mlp_low = grad_mlp.astype(jnp.bfloat16)
    grad_weight_down = jnp.dot(activ_low.T, grad_mlp_low, preferred_element_type=jnp.float32)
    grad_activ = jnp.dot(grad_mlp_low, down_back.T, preferred_element_type=jnp.float32)
    grad_hidden = gelu_pull(grad_activ)[0]
    grad_bias_up = jnp.sum(grad_hidden, axis=0)
    grad_hidden_low = grad_hidden.astype(jnp.bfloat16)
    grad_weight_up = jnp.dot(second_low.T, grad_hidden_low, preferred_element_type=jnp.float32)
    grad_second = jnp.dot(grad_hidden_low, up_back.T, preferred_element_type=jnp.float32).reshape(
        group_count, slot_local, model_width
    )
    grad_mid_norm, grad_shift_mlp, grad_scale_mlp = second_pull(grad_second)
    grad_middle = cotangent + grad_mid_norm
    grad_gate_attn = jnp.sum(grad_middle * branch, axis=1)
    grad_branch = (gate_attn * grad_middle).reshape(token_rows, model_width)
    grad_bias_out = jnp.sum(grad_branch, axis=0)
    grad_branch_low = grad_branch.astype(jnp.bfloat16)
    grad_weight_out = jnp.dot(attended.T, grad_branch_low, preferred_element_type=jnp.float32)
    grad_attended = jnp.dot(grad_branch_low, out_back.T, preferred_element_type=jnp.float32).astype(
        jnp.bfloat16
    )
    grad_attended = grad_attended.reshape(
        group_count, slot_local, head_count, model_width // head_count
    )
    grad_heads = lax.all_to_all(grad_attended, "head", split_axis=2, concat_axis=1, tiled=True)
    grad_heads = grad_heads.reshape(group_count, slot_total, head_local, head_size)
    grad_q, grad_k, grad_v = lax.map(
        attend_back, (queries, keys_in, values_in, valid_keys, log_total, split_blocks(grad_heads))
    )
    grad_stack = jnp.stack(
        [grad_q.astype(jnp.bfloat16), grad_k.astype(jnp.bfloat16), grad_v.astype(jnp.bfloat16)],
        axis=3,
    )
    grad_stack = grad_stack.reshape(group_count, slot_total, 3, 1, head_local * head_size)
    grad_proj = lax.all_to_all(grad_stack, "head", split_axis=1, concat_axis=3, tiled=True).reshape(
        token_rows, 3 * model_width
    )
    grad_bias_query = jnp.sum(grad_proj[:, :model_width].astype(jnp.float32), axis=0)
    grad_bias_value = jnp.sum(grad_proj[:, 2 * model_width :].astype(jnp.float32), axis=0)
    grad_weight_qkv = jnp.dot(normed_low.T, grad_proj, preferred_element_type=jnp.float32)
    grad_normed = jnp.dot(grad_proj, qkv_back.T, preferred_element_type=jnp.float32).reshape(
        group_count, slot_local, model_width
    )
    grad_in_norm, grad_shift_attn, grad_scale_attn = first_pull(grad_normed)
    grad_inputs = grad_middle + grad_in_norm
    grad_mod = jnp.stack(
        [
            grad_shift_attn,
            grad_scale_attn,
            grad_gate_attn,
            grad_shift_mlp,
            grad_scale_mlp,
            grad_gate_mlp,
        ],
        axis=1,
    )
    grad_mod = grad_mod.reshape(group_count, 6 * model_width)
    own_mod = lax.psum_scatter(
        grad_mod.astype(jnp.bfloat16), "head", scatter_dimension=0, tiled=True
    ).astype(jnp.float32)
    grad_bias_ada = jnp.sum(own_mod, axis=0)
    mod_low = own_mod.astype(jnp.bfloat16)
    first_unit = head_index * unit_count
    own_image_silu = lax.dynamic_slice_in_dim(image_silu, first_unit, unit_count, 0)
    own_order = lax.dynamic_slice_in_dim(order, first_unit, unit_count, 0)
    grad_weight_ada = jnp.dot(own_image_silu.T, mod_low, preferred_element_type=jnp.float32)
    grad_silu = jnp.dot(mod_low, ada_back.T, preferred_element_type=jnp.float32)
    placed = jnp.zeros((all_silu.shape[0], model_width), jnp.float32).at[own_order].set(grad_silu)
    grad_silu_own = lax.psum_scatter(placed, ("dp", "head"), scatter_dimension=0, tiled=True)
    grad_cond = silu_pull(grad_silu_own)[0]
    row_sums = (
        lax.psum_scatter(
            grad_weight_ada.astype(jnp.bfloat16), "dp", scatter_dimension=0, tiled=True
        ).astype(jnp.float32),
        lax.psum_scatter(
            grad_weight_qkv.astype(jnp.bfloat16), "dp", scatter_dimension=0, tiled=True
        ).astype(jnp.float32),
        lax.psum_scatter(
            grad_weight_out.astype(jnp.bfloat16), "dp", scatter_dimension=0, tiled=True
        ).astype(jnp.float32),
        lax.psum_scatter(
            grad_weight_up.astype(jnp.bfloat16), "dp", scatter_dimension=0, tiled=True
        ).astype(jnp.float32),
        lax.psum_scatter(
            grad_weight_down.astype(jnp.bfloat16), "dp", scatter_dimension=0, tiled=True
        ).astype(jnp.float32),
    )
    weight_sums = (
        lax.psum_scatter(
            row_sums[0].astype(jnp.bfloat16), "head", scatter_dimension=1, tiled=True
        ).astype(jnp.float32),
        lax.psum_scatter(
            row_sums[1].astype(jnp.bfloat16), "head", scatter_dimension=1, tiled=True
        ).astype(jnp.float32),
        lax.psum_scatter(
            row_sums[2].astype(jnp.bfloat16), "head", scatter_dimension=1, tiled=True
        ).astype(jnp.float32),
        lax.psum_scatter(
            row_sums[3].astype(jnp.bfloat16), "head", scatter_dimension=1, tiled=True
        ).astype(jnp.float32),
        lax.psum_scatter(
            row_sums[4].astype(jnp.bfloat16), "head", scatter_dimension=1, tiled=True
        ).astype(jnp.float32),
    )
    bias_sums = lax.psum(
        (
            grad_bias_ada,
            grad_bias_query,
            grad_bias_value,
            grad_bias_out,
            grad_bias_up,
            grad_bias_down,
        ),
        ("dp", "head"),
    )
    return (
        result,
        grad_inputs,
        grad_cond,
        weight_sums[0],
        weight_sums[1],
        weight_sums[2],
        weight_sums[3],
        weight_sums[4],
        bias_sums[0],
        bias_sums[1],
        bias_sums[2],
        bias_sums[3],
        bias_sums[4],
        bias_sums[5],
    )


def solution(mesh):
    in_specs = (
        P("dp", "head", None),
        P(("dp", "head"), None),
        P("dp"),
        P("dp"),
        P("dp", "head"),
        P(),
        P("dp", "head"),
        P(),
        P(),
        P("dp", "head"),
        P(),
        P("dp", "head"),
        P(),
        P("dp", "head"),
        P(),
        P("dp", "head", None),
    )
    out_specs = (
        P("dp", "head", None),
        P("dp", "head", None),
        P(("dp", "head"), None),
        P("dp", "head"),
        P("dp", "head"),
        P("dp", "head"),
        P("dp", "head"),
        P("dp", "head"),
        P(),
        P(),
        P(),
        P(),
        P(),
        P(),
    )
    return jax.shard_map(body, mesh=mesh, in_specs=in_specs, out_specs=out_specs, check_vma=False)
```

profile of v0, /device:TPU:0, one launch (start us, length us, event | category | flops | bytes accessed | tf_op | source)
XLA Modules:
  0.0 1709.4 jit_solution(11590966451635481693)
XLA Ops:
  49.7 67.9 %all-gather = bf16[32,1,1152]{2,1,0:T(2,128)(2,1)S(1)} all-gather(bf16[1,1,1152]{2,1,0:T(2,128)(2,1)S(1)} %get-tuple-element.248), channel_id=1, replica_groups=mesh['dp'=16,'head'=2] {'dp','head'}, dimensions={0}, use_global_device_ids=true | all-gather | bytes 76032 | tf_op jit(solution)/shard_map/all_gather | solution.py:135
  125.0 22.5 %all-gather.10.cloned.1.call-done = bf16[1152,6912]{1,0:T(8,128)(2,1)} async-done(((bf16[72,6912]{1,0:T(8,128)(2,1)}), bf16[1152,6912]{1,0:T(8,128)(2,1)}) %all-gather.10.cloned.1.call-update) | async-done | bytes 15925264 | tf_op jit(solution)/shard_map/all_gather | solution.py:41
  159.9 60.8 %all-gather.12.cloned.1.call-done = bf16[1152,3456]{1,0:T(8,128)(2,1)} async-done(((bf16[72,3456]{1,0:T(8,128)(2,1)}), bf16[1152,3456]{1,0:T(8,128)(2,1)}) %all-gather.12.cloned.1.call-update) | async-done | bytes 7962640 | tf_op jit(solution)/shard_map/all_gather | solution.py:42
  252.4 36.5 %copy.139 = bf16[2,512,3,2,576]{1,0,4,2,3:T(2,128)(2,1)} copy(bf16[2,512,3,2,576]{4,3,2,1,0:T(2,128)(2,1)} %reshape.396) | data formatting | bytes 14155776 | tf_op jit(solution)/shard_map/reshape | solution.py:149
  295.7 86.7 %all-gather.3 = bf16[2,576,288]{1,2,0:T(8,128)(2,1)S(1)} all-gather(bf16[1,576,288]{1,2,0:T(8,128)(2,1)S(1)} %convert_bitcast_fusion), channel_id=1, replica_groups=mesh['dp'=16,'head'=2] {'head'}, dimensions={0}, use_global_device_ids=true | all-gather | bytes 995328 | tf_op jit(solution)/shard_map/all_gather | solution.py:38
  419.3 91.0 %while.27 = (s32[]{:T(128)}, bf16[2,1,1024,8,72]{2,4,3,1,0:T(8,128)(2,1)}, f32[2,1,8,1024,1]{3,2,4,1,0:T(8,128)S(1)}, bf16[2,1,1024,8,72]{2,4,3,1,0:T(8,128)(2,1...) while((s32[]{:T(128)}, ...), condition=%wide.region_5.6_spmd, body=%wide.region_2.5_spmd.sunk | while | flops 2517164032 | bytes 115088520 | solution.py:168
  523.8 29.6 %all-to-all-done.1 = bf16[2,1024,1,576]{3,0,2,1:T(2,128)(2,1)} async-done(((bf16[2,1024,1,576]{3,0,2,1:T(2,128)(2,1)}), bf16[2,1024,1,576]{3,0,2,1:T(2,128)(2,1)}, u32[]{:S(2)}, u32[]{:S(2)}) %all-to-all-start.1) | async-done | bytes 2359328 | tf_op jit(solution)/shard_map/all_to_all | solution.py:170
  600.1 24.1 %multiply_reduce_fusion.9 = (f32[1152]{0:T(1024)}, bf16[2,1152]{1,0:T(2,128)(2,1)}, bf16[2,512,1152]{2,1,0:T(8,128)(2,1)S(1)}, f32[1024,1152]{1,0:T(8,128)}) fusion(f32[2,512,1152]{2,1,0:T(8,128)} %param.37, f32[2,1152]{1,0:T(2,128)S(1)} %get-tuple-element.270, f32[1152]{0:T(1024)S(1)} %copy-done.59, bf16[4608,1152]{1,0:T(8,128)(2,1)} %all-gather.18.cloned.1.call-done, ...), kind=kOutput, calls=%fused_computation.105 | convolution fusion | flops 10925896704 | bytes 41329152 | tf_op jit(solution)/shard_map/dot_general | solution.py:183
  624.2 32.9 %fusion.70 = (f32[4608]{0:T(1024)}, bf16[1024,4608]{1,0:T(8,128)(2,1)}) fusion(f32[1024,4608]{1,0:T(8,128)} %fusion.74, f32[4608]{0:T(1024)S(1)} %copy-done.50, bf16[1024,1152]{1,0:T(8,128)(2,1)S(1)} %bitcast.286, bf16[4608,1152]{1,0:T(8,128)(2,1)} %all-gather.18.cloned.1.call-done), kind=kOutput, calls=%fused_computation.161 | convolution fusion | flops 10994315264 | bytes 41324544 | tf_op jit(solution)/shard_map/dot_general | solution.py:193
  693.7 22.7 %convolution_convert_fusion = bf16[4608,1152]{1,0:T(8,128)(2,1)} fusion(bf16[1024,1152]{1,0:T(8,128)(2,1)S(1)} %bitcast.287, f32[1024,4608]{1,0:T(8,128)} %fusion.74, f32[4608]{0:T(1024)S(1)} %copy-done.50), kind=kOutput, calls=%fused_computation.62 | convolution fusion | flops 10924130304 | bytes 31868928 | tf_op jit(solution)/shard_map/dot_general | solution.py:192
  783.7 218.0 %while.28 = (s32[]{:T(128)}, bf16[2,1,1024,8,72]{2,4,3,1,0:T(8,128)(2,1)}, bf16[2,1,1024,8,72]{2,4,3,1,0:T(8,128)(2,1)}, bf16[2,1,1024,8,72]{2,4,3,1,0:T(8,128)(...) while((s32[]{:T(128)}, ...), condition=%wide.region_12.13_spmd, body=%wide.region_10.12_spmd.sunk | while | flops 6166798336 | bytes 267233424 | solution.py:216
  815.1 24.9 %multiply_reduce_fusion.11 = (f32[8,1024]{1,0:T(8,128)S(1)}, f32[8,1024,1024]{1,2,0:T(8,128)}) fusion(f32[8,1024,1024]{1,2,0:T(8,128)} %fusion.126, f32[8,1024]{1,0:T(8,128)S(1)} %dynamic-slice_bitcast_fusion.2, pred[1024]{0:T(1024)(128)(4,1)S(1)} %dynamic-slice_reduce_fusion.6, bf16[2,1,1024,8,72]{2,4,3,1,0:T(8,128)(2,1)} %get-tuple-element.441, ...), kind=kOutput, calls=%fused_computation.24.clone.1 | convolution fusion | flops 1249894400 | bytes 69535744 | tf_op jit(solution)/shard_map/while/body/eval_jaxpr/bshd,bthd->bhst/dot_general | solution.py:81
  840.0 28.2 %multiply_convert_fusion.5 = bf16[8,1024,1024]{1,2,0:T(8,128)(2,1)} fusion(f32[8,1024,1024]{1,2,0:T(8,128)} %get-tuple-element.384, f32[8,1024,1024]{1,2,0:T(8,128)} %fusion.126, f32[8,1024]{1,0:T(8,128)S(1)} %get-tuple-element.385, f32[8,1024]{1,0:T(8,128)S(1)} %dynamic-slice_bitcast_fusion.2, pred[1024]{0:T(1024)(128)(4,1)S(1)} %dynamic-slice_reduce_fusion.6), kind=kLoop, calls=%fused_computation.23.clone.1 | loop fusion | flops 50331648 | bytes 83952640 | tf_op jit(solution)/shard_map/while/body/eval_jaxpr/convert_element_type | solution.py:85
  925.6 24.9 %multiply_reduce_fusion.11 = (f32[8,1024]{1,0:T(8,128)S(1)}, f32[8,1024,1024]{1,2,0:T(8,128)}) fusion(f32[8,1024,1024]{1,2,0:T(8,128)} %fusion.126, f32[8,1024]{1,0:T(8,128)S(1)} %dynamic-slice_bitcast_fusion.2, pred[1024]{0:T(1024)(128)(4,1)S(1)} %dynamic-slice_reduce_fusion.6, bf16[2,1,1024,8,72]{2,4,3,1,0:T(8,128)(2,1)} %get-tuple-element.441, ...), kind=kOutput, calls=%fused_computation.24.clone.1 | convolution fusion | flops 1249894400 | bytes 69535744 | tf_op jit(solution)/shard_map/while/body/eval_jaxpr/bshd,bthd->bhst/dot_general | solution.py:81
  950.5 28.5 %multiply_convert_fusion.5 = bf16[8,1024,1024]{1,2,0:T(8,128)(2,1)} fusion(f32[8,1024,1024]{1,2,0:T(8,128)} %get-tuple-element.384, f32[8,1024,1024]{1,2,0:T(8,128)} %fusion.126, f32[8,1024]{1,0:T(8,128)S(1)} %get-tuple-element.385, f32[8,1024]{1,0:T(8,128)S(1)} %dynamic-slice_bitcast_fusion.2, pred[1024]{0:T(1024)(128)(4,1)S(1)} %dynamic-slice_reduce_fusion.6), kind=kLoop, calls=%fused_computation.23.clone.1 | loop fusion | flops 50331648 | bytes 83952640 | tf_op jit(solution)/shard_map/while/body/eval_jaxpr/convert_element_type | solution.py:85
  1008.2 20.1 %copy.155 = bf16[2,1024,3,1,576]{4,0,3,2,1:T(2,128)(2,1)} copy(bf16[2,1024,3,1,576]{1,4,3,2,0:T(8,128)(2,1)} %pad_maximum_fusion) | data formatting | bytes 14155776 | tf_op jit(solution)/shard_map/stack | solution.py:219
  1028.3 97.0 %all_to_all.60 = bf16[2,1024,3,1,576]{4,0,3,2,1:T(2,128)(2,1)} all-to-all(bf16[2,1024,3,1,576]{4,0,3,2,1:T(2,128)(2,1)} %copy.155), channel_id=1, replica_groups=mesh['dp'=16,'head'=2] {'head'}, dimensions={1} | all-to-all | bytes 14155776 | tf_op jit(solution)/shard_map/all_to_all | solution.py:224
  1125.3 36.5 %copy.169 = bf16[2,2,512,3,1,576]{2,1,5,3,0,4:T(2,128)(2,1)} copy(bf16[2,2,512,3,1,576]{5,0,3,2,1,4:T(2,128)(2,1)} %bitcast.270) | data formatting | bytes 14155776 | tf_op jit(solution)/shard_map/all_to_all | solution.py:224
  1254.1 36.7 %reduce-scatter.39.cloned.1.call-done = bf16[72,3456]{1,0:T(8,128)(2,1)} async-done(((bf16[1152,3456]{1,0:T(8,128)(2,1)}), bf16[72,3456]{1,0:T(8,128)(2,1)}) %reduce-scatter.39.cloned.1.call-update) | async-done | bytes 497680
  1310.2 41.3 %all-reduce.4 = (f32[6912]{0:T(1024)}, f32[1152]{0:T(1024)}, f32[1152]{0:T(1024)}, f32[1152]{0:T(1024)}, f32[4608]{0:T(1024)}, /*index=5*/f32[1152]{0:T(1024)}) all-reduce(bf16[6912]{0:T(1024)(128)(2,1)S(1)} %dynamic-slice_reduce_fusion.2, f32[1152]{0:T(1024)S(1)} %get-tuple-element.194, ...), channel_id=1, replica_groups=mesh['dp'=16,'head'=2] {'dp','head'}, use_global_device_ids=true, to_apply=%region_34.35 | all-reduce | flops 16128 | bytes 115200 | tf_op jit(solution)/shard_map/psum | solution.py:294
  1351.5 130.0 %reduce-scatter.23.cloned.1.call-done = bf16[72,6912]{1,0:T(8,128)(2,1)} async-done(((bf16[1152,6912]{1,0:T(8,128)(2,1)}), bf16[72,6912]{1,0:T(8,128)(2,1)}) %reduce-scatter.23.cloned.1.call-update) | async-done | bytes 995344 | tf_op jit(solution)/shard_map/reduce_scatter | solution.py:261
  1492.0 115.3 %all-reduce.7.cloned.1.call-done = f32[32,1152]{1,0:T(8,128)} async-done(((f32[32,1152]{1,0:T(8,128)}), f32[32,1152]{1,0:T(8,128)}) %all-reduce.7.cloned.1.call-update) | async-done | bytes 147472
  1608.7 21.4 %reduce-scatter.37.cloned.1.call-done = bf16[576,288]{1,0:T(8,128)(2,1)} async-done(((bf16[1152,288]{1,0:T(8,128)(2,1)}), bf16[576,288]{1,0:T(8,128)(2,1)}) %reduce-scatter.37.cloned.1.call-update) | async-done | bytes 331792
  1671.7 28.5 %reduce-scatter.31.cloned.1.call-done = bf16[3456,72]{1,0:T(8,128)(2,1)} async-done(((bf16[6912,72]{1,0:T(8,128)(2,1)}), bf16[3456,72]{1,0:T(8,128)(2,1)}) %reduce-scatter.31.cloned.1.call-update) | async-done | bytes 497680
  (343 shorter events, 674.7 us)
Async XLA Ops:
  7.2 140.3 %all-gather.10.cloned.1.call-start = ((), (), s32[]{:S(2)}) async-start(), calls=%async_computation.14 | async-start | bytes 16920576 | tf_op jit(solution)/shard_map/all_gather | solution.py:41
  23.7 197.0 %all-gather.12.cloned.1.call-start = ((), (), s32[]{:S(2)}) async-start(), calls=%async_computation.15 | async-start | bytes 8460288 | tf_op jit(solution)/shard_map/all_gather | solution.py:42
  34.5 86.3 %copy-start.60 = (f32[1152]{0:T(1024)S(1)}, f32[1152]{0:T(1024)}, u32[]{:S(2)}) copy-start(f32[1152]{0:T(1024)} %param.30) | copy-start | bytes 13828
  34.5 86.3 %copy-start.61 = (f32[1152]{0:T(1024)S(1)}, f32[1152]{0:T(1024)}, u32[]{:S(2)}) copy-start(f32[1152]{0:T(1024)} %param.29) | copy-start | bytes 13828
  34.5 534.5 %all-gather.14.cloned.1.call-start = ((), (), s32[]{:S(2)}) async-start(), calls=%async_computation.16 | async-start | bytes 2820096 | tf_op jit(solution)/shard_map/all_gather | solution.py:43
  40.8 539.7 %all-gather.16.cloned.1.call-start = ((), (), s32[]{:S(2)}) async-start(), calls=%async_computation.17 | async-start | bytes 11280384 | tf_op jit(solution)/shard_map/all_gather | solution.py:44
  288.9 95.5 %all-to-all-start = ((bf16[2,512,3,2,576]{1,0,4,2,3:T(2,128)(2,1)}), bf16[2,512,3,2,576]{1,0,4,2,3:T(2,128)(2,1)}, u32[]{:S(2)}, u32[]{:S(2)}) async-start(bf16[2,512,3,2,576]{1,0,4,2,3:T(2,128)(2,1)} %copy.139), calls=%async_computation | async-start | bytes 14155776 | tf_op jit(solution)/shard_map/all_to_all | solution.py:148
  295.6 88.7 %copy-start.64 = (s32[2]{0:T(128)S(1)}, s32[2]{0:T(128)}, u32[]{:S(2)}) copy-start(s32[2]{0:T(128)} %param.25) | copy-start | bytes 28
  295.6 304.4 %all-gather.18.cloned.1.call-start = ((), (), s32[]{:S(2)}) async-start(), calls=%async_computation.18 | async-start | bytes 11280384 | tf_op jit(solution)/shard_map/all_gather | solution.py:45
  518.1 35.3 %all-to-all-start.1 = ((bf16[2,1024,1,576]{3,0,2,1:T(2,128)(2,1)}), bf16[2,1024,1,576]{3,0,2,1:T(2,128)(2,1)}, u32[]{:S(2)}, u32[]{:S(2)}) async-start(bf16[2,1024,1,576]{3,0,2,1:T(2,128)(2,1)} %copy.144), calls=%async_computation.1 | async-start | bytes 5242880 | tf_op jit(solution)/shard_map/all_to_all | solution.py:170
  523.1 669.1 %reduce-scatter.41.cloned.1.call-start = ((), (), s32[]{:S(2)}) async-start(), calls=%async_computation.29 | async-start | bytes 2820096
  693.7 557.4 %reduce-scatter.29.cloned.1.call-start = ((), (), s32[]{:S(2)}) async-start(), calls=%async_computation.22 | async-start | bytes 11280384 | tf_op jit(solution)/shard_map/reduce_scatter | solution.py:273
  739.7 29.8 %all-to-all-start.2 = ((bf16[2,512,2,576]{1,0,3,2:T(2,128)(2,1)}), bf16[2,512,2,576]{1,0,3,2:T(2,128)(2,1)S(1)}, u32[]{:S(2)}, u32[]{:S(2)}) async-start(bf16[2,512,2,576]{1,0,3,2:T(2,128)(2,1)} %copy.168), calls=%async_computation.2 | async-start | bytes 4718592 | tf_op jit(solution)/shard_map/all_to_all | solution.py:214
  743.6 509.9 %reduce-scatter.25.cloned.1.call-start = ((), (), s32[]{:S(2)}) async-start(), calls=%async_computation.20 | async-start | bytes 11280384 | tf_op jit(solution)/shard_map/reduce_scatter | solution.py:270
  761.1 529.8 %reduce-scatter.39.cloned.1.call-start = ((), (), s32[]{:S(2)}) async-start(), calls=%async_computation.28 | async-start | bytes 8460288
  1191.0 114.4 %reduce-scatter.35.cloned.1.call-start = ((), (), s32[]{:S(2)}) async-start(), calls=%async_computation.25 | async-start | bytes 442368
  1194.1 287.4 %reduce-scatter.23.cloned.1.call-start = ((), (), s32[]{:S(2)}) async-start(), calls=%async_computation.19 | async-start | bytes 16920576 | tf_op jit(solution)/shard_map/reduce_scatter | solution.py:261
  1235.0 372.3 %all-reduce.7.cloned.1.call-start = ((), (), s32[]{:S(2)}) async-start(), calls=%async_computation.27 | async-start | bytes 294912
  1251.0 379.1 %reduce-scatter.37.cloned.1.call-start = ((), (), s32[]{:S(2)}) async-start(), calls=%async_computation.26 | async-start | bytes 1327104
  1253.5 394.9 %reduce-scatter.27.cloned.1.call-start = ((), (), s32[]{:S(2)}) async-start(), calls=%async_computation.21 | async-start | bytes 995328 | tf_op jit(solution)/shard_map/reduce_scatter | solution.py:287
  1254.1 415.6 %reduce-scatter.33.cloned.1.call-start = ((), (), s32[]{:S(2)}) async-start(), calls=%async_computation.24 | async-start | bytes 1327104
  1293.1 407.0 %reduce-scatter.31.cloned.1.call-start = ((), (), s32[]{:S(2)}) async-start(), calls=%async_computation.23 | async-start | bytes 2654208
  1484.1 123.3 %copy-start.57 = (f32[1,1152]{1,0:T(1,128)S(1)}, f32[1,1152]{1,0:T(1,128)}, u32[]{:S(2)}) copy-start(f32[1,1152]{1,0:T(1,128)} %param.23) | copy-start | bytes 13828
  1484.1 123.2 %copy-start.58 = (f32[1,1152]{1,0:T(1,128)S(1)}, f32[1,1152]{1,0:T(1,128)}, u32[]{:S(2)}) copy-start(f32[1,1152]{1,0:T(1,128)} %get-tuple-element.249) | copy-start | bytes 13828
  (72 other events, 1206.8 us)
Sparse Core Ops, SparseCore 0:
  23.8 123.6 all-gather.9
  150.2 70.3 all-gather.11
  223.4 41.6 all-gather.13
  267.2 87.3 all-gather.15
  384.4 86.1 all-gather.17
  693.8 61.7 reduce-scatter.40
  760.2 119.1 reduce-scatter.28
  883.9 119.9 reduce-scatter.24
  1191.1 99.7 reduce-scatter.38
  1293.5 11.8 reduce-scatter.34
  1309.5 171.9 reduce-scatter.22
  1487.4 119.8 all-reduce.6
  1609.6 20.4 reduce-scatter.36
  1632.2 16.0 reduce-scatter.26
  1651.1 18.4 reduce-scatter.32
  1671.9 28.2 reduce-scatter.30
where the time goes:
time: 1720 us; the launch traced here: 1710 us
  waiting for transfers between devices  502 us (29%)
  matrix products  435 us (25%)
  blocking collectives  336 us (20%)
  local copies, waits for them, and re-layouts  254 us (15%)
  other arithmetic  147 us (9%)
  between operations  17.4 us (1%)
    unnamed x23, waiting for transfers between devices  234 us
    reduce_scatter x1, waiting for transfers between devices, body(): lax.psum_scatter(grad_weight_ada.astype(jnp.bfloat16), 'dp', scatter_dime...  130 us
    all_to_all x1, blocking collectives, body(): lax.all_to_all(grad_stack, 'head', split_axis=1, concat_axis=3, tiled=True)  97 us
    all_gather x1, blocking collectives, fetch_weights(): lax.all_gather(weight_down.astype(jnp.bfloat16), 'head', axis=1, tiled=True)  86.7 us
    all_gather x1, blocking collectives, body(): lax.all_gather(own_silu.astype(jnp.bfloat16), ('dp', 'head'), axis=0, til...  67.9 us
    dot_general x4, matrix products, masked_scores(): jnp.einsum('bshd,bthd->bhst', queries, keys_in, preferred_element_type=jn...  64.1 us
    all_gather x1, waiting for transfers between devices, fetch_weights(): lax.all_gather(widened[1], 'dp', axis=0, tiled=True)  60.8 us
    convert_element_type x2, other arithmetic, attend_back(): grad_scores = (soft_weights * (grad_soft - inner_term)).astype(jnp.bfloat16)  56.7 us
  transfers between devices with their start and end apart: 19, of which 12 were waited for; matrix products, arithmetic and copies ran while one was open for 43% of the time, Pallas kernels for 0%

commit v1 on v0

v1 whole, which is shorter than its diff:
```python
import functools
import math

import jax
import jax.numpy as jnp
from jax import lax
from jax.experimental import pallas as pl
from jax.experimental.pallas import tpu as pltpu
from jax.sharding import PartitionSpec as P

H = 16
norm_eps = 1e-06
log2_e = 1.4426950408889634
gelu_in = 0.7978845608028654
gelu_cube = 0.044715
f32 = jnp.float32
bf16 = jnp.bfloat16
VMEM_MOST = 60 * 1024 * 1024


def mm(left, right):
    return jnp.dot(left, right, preferred_element_type=f32)


def mm_nt(left, right):
    return lax.dot_general(left, right, (((1,), (1,)), ((), ())), preferred_element_type=f32)


def center_spread(values):
    center = values - jnp.mean(values, axis=-1, keepdims=True)
    spread = jnp.mean(center * center, axis=-1, keepdims=True)
    return center, lax.rsqrt(spread + norm_eps)


def norm_back(grad, unit, inv):
    return inv * (
        grad
        - jnp.mean(grad, axis=-1, keepdims=True)
        - unit * jnp.mean(grad * unit, axis=-1, keepdims=True)
    )


def whole_spec(shape):
    zeros = (0,) * len(shape)
    return pl.BlockSpec(shape, lambda *_: zeros)


def once_spec(shape):
    zeros = (0,) * len(shape)
    return pl.BlockSpec(shape, lambda *_: zeros, pipeline_mode=pl.Buffered(1))


def params(most=VMEM_MOST):
    return pltpu.CompilerParams(vmem_limit_bytes=most)


def place(quarter):
    return (quarter % 2) * 2 + quarter // 2


def qkv_kernel(tm, x_ref, mod_ref, w_ref, b_ref, qkv_ref, norm_ref):
    part = pl.program_id(0)
    rows = pl.ds(pl.multiple_of(pl.program_id(1) * tm, tm), tm)

    @pl.when(part == 0)
    def _():
        center, inv = center_spread(x_ref[...].astype(f32))
        norm_ref[rows, :] = (center * inv * (1.0 + mod_ref[1:2, :]) + mod_ref[0:1, :]).astype(bf16)

    groups, _, rows_each, width = w_ref.shape
    weight = w_ref[...].reshape(groups * rows_each, width)
    out = (mm(norm_ref[rows, :], weight) + b_ref[0]).astype(bf16)
    size = qkv_ref.shape[2]
    for j in range(qkv_ref.shape[0]):
        qkv_ref[j] = out[:, j * size : (j + 1) * size]


def qkv_call(x, mod, weight, bias):
    slots, width = x.shape
    tm = min(256, slots)
    groups, parts, rows_each, part_width = weight.shape
    size = width // H
    heads = part_width // size
    return pl.pallas_call(
        functools.partial(qkv_kernel, tm),
        grid=(parts, slots // tm),
        in_specs=[
            pl.BlockSpec((tm, width), lambda p, i: (i, 0)),
            whole_spec(mod.shape),
            pl.BlockSpec((groups, 1, rows_each, part_width), lambda p, i: (0, place(p), 0, 0)),
            pl.BlockSpec((1, 1, part_width), lambda p, i: (p, 0, 0)),
        ],
        out_specs=[
            pl.BlockSpec((heads, tm, size), lambda p, i: (p, i, 0)),
            whole_spec((slots, width)),
        ],
        out_shape=[
            jax.ShapeDtypeStruct((3 * H, slots, size), bf16),
            jax.ShapeDtypeStruct((slots, width), bf16),
        ],
        compiler_params=params(),
        name="qkv_forward",
    )(x, mod, weight, bias)


def masked(scores, full, kept):
    return jnp.concatenate(
        [scores[:kept], jnp.where(full, scores[kept:], -1e30)], axis=0
    )


def attn_kernel(ts, kind_ref, q_ref, k_ref, v_ref, o_ref, lse_ref):
    slots, size = q_ref.shape[1:]
    kept = slots - slots // 16
    factor = log2_e * size ** (-0.5)
    full = kind_ref[0] == 0
    keys = k_ref[0]
    values_t = v_ref[0].T
    for start in range(0, slots, ts):
        here = slice(start, start + ts)
        scores = masked(mm_nt(keys, q_ref[0, here, :]), full, kept)
        peak = jnp.max(scores, axis=0, keepdims=True) * factor
        exponent = jnp.exp2(scores * factor - peak)
        total = jnp.sum(exponent, axis=0, keepdims=True)
        mix = mm(values_t, exponent.astype(bf16)) * (1.0 / total)
        o_ref[0, here, :] = mix.T.astype(bf16)
        lse_ref[0, :, here] = peak + jnp.log2(total)


def attn_call(kind, qkv):
    _, slots, size = qkv.shape
    ts = min(256, slots)
    block = (1, slots, size)
    return pl.pallas_call(
        functools.partial(attn_kernel, ts),
        grid=(H,),
        in_specs=[
            pl.BlockSpec(memory_space=pltpu.SMEM),
            pl.BlockSpec(block, lambda h: (h, 0, 0)),
            pl.BlockSpec(block, lambda h: (h + H, 0, 0)),
            pl.BlockSpec(block, lambda h: (h + 2 * H, 0, 0)),
        ],
        out_specs=[
            pl.BlockSpec(block, lambda h: (h, 0, 0)),
            pl.BlockSpec((1, 1, slots), lambda h: (h, 0, 0)),
        ],
        out_shape=[
            jax.ShapeDtypeStruct((H, slots, size), bf16),
            jax.ShapeDtypeStruct((H, 1, slots), f32),
        ],
        compiler_params=params(),
        name="attention_forward",
    )(kind, qkv, qkv, qkv)


def attn_back_kernel(ts, kind_ref, q_ref, k_ref, v_ref, g_ref, lse_ref, out_ref, dk_s, dv_s):
    slots, size = q_ref.shape[1:]
    kept = slots - slots // 16
    scale = size ** (-0.5)
    factor = log2_e * scale
    full = kind_ref[0] == 0
    keys = k_ref[0]
    keys_t = keys.T
    values = v_ref[0]
    for start in range(0, slots, ts):
        here = slice(start, start + ts)
        queries = q_ref[0, here, :]
        grad = g_ref[0, here, :]
        scores = masked(mm_nt(keys, queries), full, kept)
        probs = jnp.exp2(scores * factor - lse_ref[0, :, here])
        grad_probs = mm_nt(values, grad)
        weighted = probs * grad_probs
        inner = jnp.sum(weighted, axis=0, keepdims=True)
        grad_scores = (weighted - probs * inner).astype(bf16)
        add_v = mm(probs.astype(bf16), grad)
        add_k = mm(grad_scores, queries)
        if start == 0:
            dv_s[...] = add_v
            dk_s[...] = add_k
        else:
            dv_s[...] += add_v
            dk_s[...] += add_k
        out_ref[0, 0, here, :] = (mm(keys_t, grad_scores) * scale).T.astype(bf16)
    out_ref[1, 0] = (dk_s[...] * scale).astype(bf16)
    out_ref[2, 0] = dv_s[...].astype(bf16)


def attn_back_call(kind, qkv, grad, lse):
    _, slots, size = qkv.shape
    ts = min(256, slots)
    block = (1, slots, size)
    return pl.pallas_call(
        functools.partial(attn_back_kernel, ts),
        grid=(H,),
        in_specs=[
            pl.BlockSpec(memory_space=pltpu.SMEM),
            pl.BlockSpec(block, lambda h: (h, 0, 0)),
            pl.BlockSpec(block, lambda h: (h + H, 0, 0)),
            pl.BlockSpec(block, lambda h: (h + 2 * H, 0, 0)),
            pl.BlockSpec(block, lambda h: (h, 0, 0)),
            pl.BlockSpec((1, 1, slots), lambda h: (h, 0, 0)),
        ],
        out_specs=pl.BlockSpec((3, 1, slots, size), lambda h: (0, h, 0, 0)),
        out_shape=jax.ShapeDtypeStruct((3, H, slots, size), bf16),
        scratch_shapes=[pltpu.VMEM((slots, size), f32), pltpu.VMEM((slots, size), f32)],
        compiler_params=params(),
        name="attention_backward",
    )(kind, qkv, qkv, qkv, grad, lse)


def columns_of(w_ref):
    groups, parts, rows_each, width = w_ref.shape
    return jnp.concatenate(
        [w_ref[:, place(n)].reshape(groups * rows_each, width) for n in range(parts)], axis=1
    )


def out_kernel(o_ref, x_ref, mod_ref, w_ref, b_ref, att_ref, branch_ref, second_ref, w_s):
    @pl.when(pl.program_id(0) == 0)
    def _():
        w_s[...] = columns_of(w_ref)

    attended = jnp.concatenate([o_ref[j] for j in range(o_ref.shape[0])], axis=1)
    att_ref[...] = attended
    branch = mm(attended, w_s[...]) + b_ref[...]
    branch_ref[...] = branch.astype(bf16)
    middle = x_ref[...].astype(f32) + mod_ref[2:3, :] * branch
    center, inv = center_spread(middle)
    second_ref[...] = (center * inv * (1.0 + mod_ref[4:5, :]) + mod_ref[3:4, :]).astype(bf16)


def out_call(mix, x, mod, weight, bias):
    slots, width = x.shape
    tm = min(256, slots)
    size = width // H
    tile = pl.BlockSpec((tm, width), lambda i: (i, 0))
    return pl.pallas_call(
        out_kernel,
        grid=(slots // tm,),
        in_specs=[
            pl.BlockSpec((H, tm, size), lambda i: (0, i, 0)),
            tile,
            whole_spec(mod.shape),
            whole_spec(weight.shape),
            whole_spec((1, width)),
        ],
        out_specs=[tile, tile, tile],
        out_shape=[jax.ShapeDtypeStruct((slots, width), bf16)] * 3,
        scratch_shapes=[pltpu.VMEM((width, width), bf16)],
        compiler_params=params(),
        name="out_projection",
    )(mix, x, mod, weight, bias.reshape(1, width))


def mlp_kernel(
    tm, second_ref, cot_ref, mod_ref, up_ref, down_ref, b_ref,
    mlp_ref, gsec_ref, dup_ref, ddown_ref, bias_ref,
    gm_s, sec_t, act_t, gh_s, down_s,
):
    part = pl.program_id(0)
    slots, width = second_ref.shape
    tiles = slots // tm

    @pl.when(part == 0)
    def _():
        sec_t[...] = second_ref[...].T
        gm_s[...] = (cot_ref[...].astype(f32) * mod_ref[5:6, :]).astype(bf16)
        mlp_ref[...] = jnp.zeros_like(mlp_ref)
        gsec_ref[...] = jnp.zeros_like(gsec_ref)

    groups, _, rows_each, hidden = up_ref.shape
    chunks, halves, chunk, half = down_ref.shape
    for j in range(chunks):
        down_s[j * chunk : (j + 1) * chunk, :] = jnp.concatenate(
            [down_ref[j, s] for s in range(halves)], axis=1
        )
    bias_ref[...] = jnp.zeros_like(bias_ref)

    def tile(i, carry):
        rows = pl.ds(pl.multiple_of(i * tm, tm), tm)
        up = up_ref[...].reshape(width, hidden)
        pre = mm(second_ref[rows, :], up) + b_ref[0]
        square = pre * pre
        tanh = jnp.tanh(gelu_in * (pre + gelu_cube * pre * square))
        act = (0.5 * pre * (1.0 + tanh)).astype(bf16)
        slope = 0.5 * (1.0 + tanh) + 0.5 * pre * (1.0 - tanh * tanh) * (
            gelu_in * (1.0 + 3.0 * gelu_cube * square)
        )
        grad = mm_nt(gm_s[rows, :], down_s[...]) * slope
        bias_ref[0] += jnp.sum(grad, axis=0, keepdims=True)
        grad_low = grad.astype(bf16)
        gh_s[rows, :] = grad_low
        act_t[:, rows] = act.T
        mlp_ref[rows, :] += mm(act, down_s[...])
        gsec_ref[rows, :] += mm_nt(grad_low, up)
        return carry

    lax.fori_loop(0, tiles, tile, 0)
    per = groups // 2
    for j in range(2):
        dup_ref[per * j : per * (j + 1), 0] = (
            mm(sec_t[per * j * rows_each : per * (j + 1) * rows_each, :], gh_s[...])
            .astype(bf16)
            .reshape(per, rows_each, hidden)
        )
    per = chunks // 2
    for j in range(2):
        grad = mm(act_t[per * j * chunk : per * (j + 1) * chunk, :], gm_s[...]).astype(bf16)
        for r in range(per):
            for s in range(halves):
                ddown_ref[per * j + r, s] = grad[
                    r * chunk : (r + 1) * chunk, s * half : (s + 1) * half
                ]


def mlp_call(second, cot, mod, up, down, bias):
    slots, width = second.shape
    tm = min(256, slots)
    groups, parts, rows_each, hidden = up.shape
    chunks, halves, chunk, half = down.shape
    per = chunks // parts
    up_spec = pl.BlockSpec((groups, 1, rows_each, hidden), lambda p: (0, place(p), 0, 0))
    down_spec = pl.BlockSpec((per, halves, chunk, half), lambda p: (p, 0, 0, 0))
    return pl.pallas_call(
        functools.partial(mlp_kernel, tm),
        grid=(parts,),
        in_specs=[
            once_spec((slots, width)),
            once_spec((slots, width)),
            whole_spec(mod.shape),
            up_spec,
            down_spec,
            pl.BlockSpec((1, 1, hidden), lambda p: (p, 0, 0)),
        ],
        out_specs=[
            once_spec((slots, width)),
            once_spec((slots, width)),
            up_spec,
            down_spec,
            pl.BlockSpec((1, 1, hidden), lambda p: (p, 0, 0)),
        ],
        out_shape=[
            jax.ShapeDtypeStruct((slots, width), f32),
            jax.ShapeDtypeStruct((slots, width), f32),
            jax.ShapeDtypeStruct(up.shape, bf16),
            jax.ShapeDtypeStruct(down.shape, bf16),
            jax.ShapeDtypeStruct((parts, 1, hidden), f32),
        ],
        scratch_shapes=[
            pltpu.VMEM((slots, width), bf16),
            pltpu.VMEM((width, slots), bf16),
            pltpu.VMEM((hidden, slots), bf16),
            pltpu.VMEM((slots, hidden), bf16),
            pltpu.VMEM((hidden, width), bf16),
        ],
        compiler_params=params(),
        name="feed_forward_both_ways",
    )(second, cot, mod, up, down, bias)


def mid_back_kernel(
    x_ref, branch_ref, mlp_ref, gsec_ref, cot_ref, att_ref, mod_ref, w_ref, b_ref,
    act_ref, gmid_ref, gatt_ref, dw_ref, sums_ref, w_s, dw_s,
):
    step = pl.program_id(0)

    @pl.when(step == 0)
    def _():
        w_s[...] = columns_of(w_ref)
        sums_ref[...] = jnp.zeros_like(sums_ref)
        dw_s[...] = jnp.zeros_like(dw_s)

    gate_a = mod_ref[2:3, :]
    gate_m = mod_ref[5:6, :]
    branch = branch_ref[...].astype(f32)
    middle = x_ref[...].astype(f32) + gate_a * branch
    mlp = mlp_ref[...] + b_ref[...]
    cot = cot_ref[...].astype(f32)
    act_ref[...] = (middle + gate_m * mlp).astype(act_ref.dtype)
    center, inv = center_spread(middle)
    unit = center * inv
    grad = gsec_ref[...]
    grad_mid = cot + norm_back(grad * (1.0 + mod_ref[4:5, :]), unit, inv)
    gmid_ref[...] = grad_mid
    grad_branch = gate_a * grad_mid

    def add(row, value):
        sums_ref[row : row + 1, :] += jnp.sum(value, axis=0, keepdims=True)

    add(0, grad_mid * branch)
    add(1, grad)
    add(2, grad * unit)
    add(3, cot * mlp)
    add(4, grad_branch)
    add(5, gate_m * cot)
    grad_low = grad_branch.astype(bf16)
    grad_att = mm_nt(grad_low, w_s[...]).astype(bf16)
    size = gatt_ref.shape[2]
    for j in range(gatt_ref.shape[0]):
        gatt_ref[j] = grad_att[:, j * size : (j + 1) * size]
    dw_s[...] += mm(att_ref[...].T, grad_low)

    @pl.when(step == pl.num_programs(0) - 1)
    def _():
        groups, parts, rows_each, width = dw_ref.shape
        low = dw_s[...].astype(bf16)
        for n in range(parts):
            dw_ref[:, place(n)] = low[:, n * width : (n + 1) * width].reshape(
                groups, rows_each, width
            )


def mid_back_call(x, branch, mlp, gsec, cot, attended, mod, weight, bias_down):
    slots, width = x.shape
    tm = min(256, slots)
    size = width // H
    tile = pl.BlockSpec((tm, width), lambda i: (i, 0))
    return pl.pallas_call(
        mid_back_kernel,
        grid=(slots // tm,),
        in_specs=[tile] * 6 + [whole_spec(mod.shape), whole_spec(weight.shape), whole_spec((1, width))],
        out_specs=[
            tile,
            tile,
            pl.BlockSpec((H, tm, size), lambda i: (0, i, 0)),
            whole_spec(weight.shape),
            whole_spec((8, width)),
        ],
        out_shape=[
            jax.ShapeDtypeStruct((slots, width), bf16),
            jax.ShapeDtypeStruct((slots, width), f32),
            jax.ShapeDtypeStruct((H, slots, size), bf16),
            jax.ShapeDtypeStruct(weight.shape, bf16),
            jax.ShapeDtypeStruct((8, width), f32),
        ],
        scratch_shapes=[pltpu.VMEM((width, width), bf16), pltpu.VMEM((width, width), f32)],
        compiler_params=params(),
        name="middle_backward",
    )(x, branch, mlp, gsec, cot, attended, mod, weight, bias_down.reshape(1, width))


def qkv_back_kernel(tm, g_ref, norm_ref, w_ref, x_ref, gmid_ref, mod_ref, gin_ref, dw_ref, bias_ref, sums_ref, norm_t, gp_s, gn_s):
    part = pl.program_id(0)
    slots, width = x_ref.shape
    tiles = slots // tm
    groups, _, rows_each, part_width = w_ref.shape
    heads = g_ref.shape[0]

    @pl.when(part == 0)
    def _():
        norm_t[...] = norm_ref[...].T
        gn_s[...] = jnp.zeros_like(gn_s)

    def tile(i, total):
        rows = pl.ds(pl.multiple_of(i * tm, tm), tm)
        grad = jnp.concatenate([g_ref[j, rows, :] for j in range(heads)], axis=1)
        gp_s[rows, :] = grad
        gn_s[rows, :] += mm_nt(grad, w_ref[...].reshape(width, part_width))
        return total + jnp.sum(grad.astype(f32), axis=0, keepdims=True)

    bias_ref[0] = lax.fori_loop(0, tiles, tile, jnp.zeros((1, part_width), f32))
    per = groups // 2
    for j in range(2):
        dw_ref[per * j : per * (j + 1), 0] = (
            mm(norm_t[per * j * rows_each : per * (j + 1) * rows_each, :], gp_s[...])
            .astype(bf16)
            .reshape(per, rows_each, part_width)
        )

    @pl.when(part == pl.num_programs(0) - 1)
    def _():
        def finish(i, sums):
            rows = pl.ds(pl.multiple_of(i * tm, tm), tm)
            center, inv = center_spread(x_ref[rows, :].astype(f32))
            unit = center * inv
            grad = gn_s[rows, :]
            gin_ref[rows, :] = (
                gmid_ref[rows, :] + norm_back(grad * (1.0 + mod_ref[1:2, :]), unit, inv)
            ).astype(gin_ref.dtype)
            return (
                sums[0] + jnp.sum(grad, axis=0, keepdims=True),
                sums[1] + jnp.sum(grad * unit, axis=0, keepdims=True),
            )

        zero = jnp.zeros((1, width), f32)
        shift, scale = lax.fori_loop(0, tiles, finish, (zero, zero))
        sums_ref[...] = jnp.zeros_like(sums_ref)
        sums_ref[0:1, :] = shift
        sums_ref[1:2, :] = scale


def qkv_back_call(grad, norm, weight, x, gmid, mod):
    slots, width = x.shape
    tm = min(256, slots)
    size = width // H
    groups, parts, rows_each, part_width = weight.shape
    heads = part_width // size
    w_spec = pl.BlockSpec((groups, 1, rows_each, part_width), lambda p: (0, place(p), 0, 0))
    return pl.pallas_call(
        functools.partial(qkv_back_kernel, tm),
        grid=(parts,),
        in_specs=[
            pl.BlockSpec((heads, slots, size), lambda p: (p, 0, 0)),
            once_spec((slots, width)),
            w_spec,
            once_spec((slots, width)),
            once_spec((slots, width)),
            whole_spec(mod.shape),
        ],
        out_specs=[
            once_spec((slots, width)),
            w_spec,
            pl.BlockSpec((1, 1, part_width), lambda p: (p, 0, 0)),
            whole_spec((8, width)),
        ],
        out_shape=[
            jax.ShapeDtypeStruct((slots, width), bf16),
            jax.ShapeDtypeStruct(weight.shape, bf16),
            jax.ShapeDtypeStruct((parts, 1, part_width), f32),
            jax.ShapeDtypeStruct((8, width), f32),
        ],
        scratch_shapes=[
            pltpu.VMEM((width, slots), bf16),
            pltpu.VMEM((slots, part_width), bf16),
            pltpu.VMEM((slots, width), f32),
        ],
        compiler_params=params(),
        name="qkv_backward",
    )(grad, norm, weight, x, gmid, mod)


MESH = pl.DeviceIdType.MESH


class Place:
    def __init__(self):
        self.dp = lax.axis_size("dp")
        head = lax.axis_size("head")
        near = self.dp // 8
        at = lax.axis_index("dp")
        self.size = {"z": 4, "x": 2, "c": near, "y": head}
        self.at = {
            "z": lax.div(at, 2 * near),
            "x": lax.rem(lax.div(at, near), 2),
            "c": lax.rem(at, near),
            "y": lax.axis_index("head"),
        }
        self.count = self.dp * head
        self.me = at * head + self.at["y"]

    def device(self, axis, index):
        spot = dict(self.at)
        spot[axis] = index
        return ((spot["z"] * 2 + spot["x"]) * self.size["c"] + spot["c"], spot["y"])

    def numbered(self, index):
        head = self.size["y"]
        return (lax.div(index, head), lax.rem(index, head))

    def after(self, axis, step):
        return lax.rem(self.at[axis] + step, self.size[axis])

    def before(self, axis, step):
        return lax.rem(self.at[axis] + self.size[axis] - step, self.size[axis])


class Sems:
    def __init__(self, send, recv):
        self.send, self.recv, self.used = send, recv, 0
        self.sent = []

    def copy(self, src, dst, device):
        at = self.used
        self.used += 1
        made = pltpu.make_async_remote_copy(
            src_ref=src, dst_ref=dst, send_sem=self.send.at[at], recv_sem=self.recv.at[at],
            device_id=device, device_id_type=MESH,
        )
        made.start()
        self.sent.append(made)
        return at

    def arrived(self, at, dst, device):
        pltpu.make_async_remote_copy(
            src_ref=dst, dst_ref=dst, send_sem=self.send.at[at], recv_sem=self.recv.at[at],
            device_id=device, device_id_type=MESH,
        ).wait_recv()

    def local(self, src, dst):
        at = self.used
        self.used += 1
        made = pltpu.make_async_copy(src, dst, self.send.at[at])
        made.start()
        return made

    def drain(self):
        for made in self.sent:
            made.wait_send()


AXES = "zxcy"


class Gather:
    def __init__(self, place, sems, piece, full, axes, rows=None):
        self.place, self.sems, self.piece, self.full, self.axes = place, sems, piece, full, axes
        self.rows = rows
        self.slots = {}

    def part(self, got, axis=None, index=None):
        spot = dict(self.place.at)
        if axis is not None:
            spot[axis] = index
        spots = tuple(slice(None) if name in got else spot[name] for name in AXES)
        if self.rows is not None:
            spots = spots + (pl.ds(*self.rows), slice(None))
        return self.full.at[spots]

    def first(self):
        return self.piece if self.rows is None else self.piece.at[pl.ds(*self.rows)]

    def own(self):
        self.kept = self.sems.local(self.first(), self.part(""))

    def start(self, stage):
        axis = self.axes[stage]
        got = self.axes[:stage]
        if stage == 1:
            self.kept.wait()
        src = self.first() if stage == 0 else self.part(got)
        for step in range(1, self.place.size[axis]):
            self.slots[stage, step] = self.sems.copy(
                src, self.part(got), self.place.device(axis, self.place.after(axis, step))
            )

    def wait(self, stage):
        axis = self.axes[stage]
        got = self.axes[:stage]
        for step in range(1, self.place.size[axis]):
            index = self.place.before(axis, step)
            self.sems.arrived(
                self.slots[stage, step], self.part(got, axis, index), self.place.device(axis, index)
            )


def greet(place):
    barrier = pltpu.get_barrier_semaphore()

    def one(step, carry):
        pl.semaphore_signal(
            barrier, inc=1, device_id=place.numbered(lax.rem(place.me + step, place.count)),
            device_id_type=MESH,
        )
        return carry

    lax.fori_loop(1, place.count, one, 0)
    pl.semaphore_wait(barrier, place.count - 1)


def sems_needed(sizes, units, pairs):
    return units * (1 + sum(size - 1 for size in sizes.values())) + pairs


def exchange(place, sems, mine, whole):
    sent = []
    for step in range(1, place.size["y"]):
        other = place.after("y", step)
        sent.append(
            (step, sems.copy(mine.at[other], whole.at[place.at["y"]], place.device("y", other)))
        )
    kept = sems.local(mine.at[place.at["y"]], whole.at[place.at["y"]])

    def finish():
        kept.wait()
        for step, at in sent:
            index = place.before("y", step)
            sems.arrived(at, whole.at[index], place.device("y", index))

    return finish


def start_kernel(
    silu_ref, ada_ref, x_ref, cot_ref, qkv_ref, out_ref, up_ref, down_ref,
    mod_ref, rows_ref, hot_ref, x_full, cot_full, qkv_full, out_full, up_full, down_full,
    silu_s, share_s, terms_s, send, recv, share_send, share_recv,
):
    place = Place()
    sems = Sems(send, recv)
    count, me = place.count, place.me
    width = silu_ref.shape[1] - hot_ref.shape[1]
    rows_each = ada_ref.shape[0]
    greet(place)

    half = 16 * (qkv_ref.shape[0] // 32)
    silu = Gather(place, sems, silu_ref, silu_s, "zxyc")
    units = [
        Gather(place, sems, qkv_ref, qkv_full, "zxyc", (0, half)),
        Gather(place, sems, qkv_ref, qkv_full, "zyxc", (half, qkv_ref.shape[0] - half)),
        Gather(place, sems, out_ref, out_full, "zyxc"),
        Gather(place, sems, up_ref, up_full, "zyxc"),
        Gather(place, sems, down_ref, down_full, "zxyc"),
    ]
    silu.own()
    silu.start(0)
    for unit in units[:2]:
        unit.own()
        unit.start(0)
    x_done = exchange(place, sems, x_ref, x_full)
    for unit in units[2:]:
        unit.own()
        unit.start(0)
    silu.wait(0)
    silu.start(1)
    silu.wait(1)
    silu.start(2)
    silu.wait(2)
    silu.start(3)
    silu.wait(3)

    rows = silu_s[...].reshape(count, silu_ref.shape[1])
    hot = (
        rows[:, width:] == lax.broadcasted_iota(jnp.int32, (count, hot_ref.shape[1]), 1).astype(f32)
    ).astype(bf16)
    hot_ref[...] = hot.astype(f32)
    first = lax.axis_index("dp") * rows_each
    pick = (
        lax.broadcasted_iota(jnp.int32, (width, rows_each), 0)
        == first + lax.broadcasted_iota(jnp.int32, (width, rows_each), 1)
    ).astype(bf16)
    local = mm(rows[:, :width].astype(bf16), pick).astype(bf16)
    grouped = mm(hot[:, :count], local)
    rows_ref[...] = grouped
    share = mm(grouped.astype(bf16), ada_ref[...])
    share_s[...] = share.reshape(share_s.shape)

    def push(step):
        to = lax.rem(me + step, count)
        return pltpu.make_async_remote_copy(
            src_ref=share_s.at[to], dst_ref=terms_s.at[me],
            send_sem=share_send.at[step], recv_sem=share_recv.at[step],
            device_id=place.numbered(to), device_id_type=MESH,
        )

    def came(step):
        source = lax.rem(me + count - step, count)
        return pltpu.make_async_remote_copy(
            src_ref=terms_s.at[source], dst_ref=terms_s.at[source],
            send_sem=share_send.at[step], recv_sem=share_recv.at[step],
            device_id=place.numbered(source), device_id_type=MESH,
        )

    def do_push(step, carry):
        push(step).start()
        return carry

    lax.fori_loop(1, count, do_push, 0)
    terms_s[me] = share_s[me]

    def do_wait(step, carry):
        came(step).wait_recv()
        return carry

    def do_sent(step, carry):
        push(step).wait_send()
        return carry

    for unit in units[:2]:
        unit.wait(0)
        unit.start(1)
    lax.fori_loop(1, count, do_wait, 0)
    heads = place.size["y"]
    for y in range(heads):
        mod_ref[y] = lax.fori_loop(
            0, count // heads, lambda i, total: total + terms_s[i * heads + y],
            jnp.zeros(terms_s.shape[1:], f32),
        )
    for unit in units[2:]:
        unit.wait(0)
        unit.start(1)
    cot_done = exchange(place, sems, cot_ref, cot_full)
    for stage in (1, 2):
        for unit in units:
            unit.wait(stage)
            unit.start(stage + 1)
    x_done()
    cot_done()
    for unit in units:
        unit.wait(3)
    sems.drain()
    lax.fori_loop(1, count, do_sent, 0)


def start_call(silu, order_mine, ada, x, cot, qkv, out, up, down):
    dp, head = lax.axis_size("dp"), lax.axis_size("head")
    count = dp * head
    lead = (4, 2, dp // 8, head)
    lanes = max(128, count)
    width = silu.shape[1]
    row = jnp.concatenate(
        [silu.astype(bf16).astype(f32), jnp.broadcast_to(order_mine.astype(f32), (1, lanes))], axis=1
    )
    sizes = {"z": 4, "x": 2, "c": dp // 8, "y": head}
    needed = sems_needed(sizes, 6, 2 * head)
    anywhere = pl.BlockSpec(memory_space=pl.ANY)
    vmem = pl.BlockSpec(memory_space=pltpu.VMEM)
    slot_shape = x.shape
    return pl.pallas_call(
        start_kernel,
        in_specs=[anywhere, vmem] + [anywhere] * 6,
        out_specs=[vmem] * 3 + [anywhere] * 6,
        out_shape=[
            jax.ShapeDtypeStruct((head, 1, ada.shape[1]), f32),
            jax.ShapeDtypeStruct((count, ada.shape[0]), f32),
            jax.ShapeDtypeStruct((count, lanes), f32),
            jax.ShapeDtypeStruct(slot_shape, bf16),
            jax.ShapeDtypeStruct(slot_shape, bf16),
        ]
        + [jax.ShapeDtypeStruct(lead + piece.shape, bf16) for piece in (qkv, out, up, down)],
        scratch_shapes=[
            pltpu.VMEM(lead + (1, width + lanes), f32),
            pltpu.VMEM((count, 1, ada.shape[1]), f32),
            pltpu.VMEM((count, 1, ada.shape[1]), f32),
            pltpu.SemaphoreType.DMA((needed,)),
            pltpu.SemaphoreType.DMA((needed,)),
            pltpu.SemaphoreType.DMA((count,)),
            pltpu.SemaphoreType.DMA((count,)),
        ],
        compiler_params=pltpu.CompilerParams(
            collective_id=0, has_side_effects=True, vmem_limit_bytes=VMEM_MOST
        ),
        name="gather_start",
    )(row, ada, x, cot, qkv, out, up, down)


class Scatter:
    def __init__(self, place, sems, grad, held, recvs, axes, rows=None):
        self.place, self.sems, self.grad, self.held, self.recvs, self.axes = (
            place, sems, grad, held, recvs, axes
        )
        self.rows = rows
        self.slots = {}

    @staticmethod
    def scratch(sizes, axes, rows, width):
        held = pltpu.VMEM(tuple(sizes[a] for a in "zxy") + (rows, width), bf16)
        recvs = []
        for at, axis in enumerate(axes):
            left = tuple(sizes[a] for a in "zxy" if a not in axes[: at + 1])
            recvs.append(pltpu.VMEM((sizes[axis] - 1,) + left + (rows, width), bf16))
        return [held] + recvs

    def wanted(self, of):
        spots = tuple(of if name == "c" else slice(None) for name in AXES)
        if self.rows is not None:
            spots = spots + (pl.ds(*self.rows), slice(None))
        return self.grad.at[spots]

    def share(self, stage, index):
        done = self.axes[1:stage]
        spots = []
        for name in "zxy":
            if name in done:
                spots.append(self.place.at[name])
            elif name == self.axes[stage]:
                spots.append(index)
            else:
                spots.append(slice(None))
        return self.held.at[tuple(spots)]

    def start(self, stage):
        axis = self.axes[stage]
        place = self.place
        if stage == 0:
            self.kept = self.sems.local(self.wanted(place.at["c"]), self.held)
        for step in range(1, place.size[axis]):
            index = place.after(axis, step)
            src = self.wanted(index) if stage == 0 else self.share(stage, index)
            self.slots[stage, step] = self.sems.copy(
                src, self.recvs[stage].at[step - 1], place.device(axis, index)
            )

    def arrive(self, stage):
        axis = self.axes[stage]
        place = self.place
        if stage == 0:
            self.kept.wait()
        for step in range(1, place.size[axis]):
            self.sems.arrived(
                self.slots[stage, step], self.recvs[stage].at[step - 1],
                place.device(axis, place.before(axis, step)),
            )

    def finish(self, stage):
        self.arrive(stage)
        place = self.place
        left = [a for a in "zxy" if a not in self.axes[: stage + 1]]
        recv = self.recvs[stage]

        def one(at, carry):
            spots = {}
            for a in reversed(left):
                spots[a] = lax.rem(at, place.size[a])
                at = lax.div(at, place.size[a])
            where = tuple(spots.get(a, place.at[a]) for a in "zxy")
            inner = tuple(spots[a] for a in left)
            total = self.held[where].astype(f32)
            for step in range(recv.shape[0]):
                total = total + recv[(step,) + inner].astype(f32)
            self.held[where] = total.astype(bf16)
            return carry

        lax.fori_loop(0, math.prod(place.size[a] for a in left), one, 0)

    def result(self, stage):
        self.arrive(stage)
        place = self.place
        recv = self.recvs[stage]
        total = self.held[tuple(place.at[a] for a in "zxy")].astype(f32)
        for step in range(recv.shape[0]):
            total = total + recv[step].astype(f32)
        return total


def halves(rows):
    first = 16 * (rows // 32)
    return ((0, first), (first, rows - first))


SUM_AXES = ("cyxz", "cxyz")


def sum_scratch(sizes, grads):
    scratch = []
    for rows, width, whole in grads:
        near = sizes["c"]
        scratch.append(
            pltpu.VMEM((rows, width) if whole else (near, rows // near, width), f32)
        )
        for span, axes in zip(halves(rows), SUM_AXES):
            scratch += Scatter.scratch(sizes, axes, span[1], width)
    return scratch


class Sums:
    def __init__(self, place, sems, grads, finals, scratch):
        self.place, self.sems, self.finals = place, sems, finals
        scratch = list(scratch)
        self.totals, self.pairs = [], []
        for grad in grads:
            self.totals.append(scratch.pop(0))
            pair = []
            for span, axes in zip(halves(grad.shape[4]), SUM_AXES):
                held, recvs, scratch = scratch[0], scratch[1:5], scratch[5:]
                pair.append((Scatter(place, sems, grad, held, recvs, axes, span), span))
            self.pairs.append(pair)
        self.ticks = len(self.pairs) + 3

    def start(self, tick):
        for back in range(3, -1, -1):
            if 0 <= tick - back < len(self.pairs):
                for unit, _ in self.pairs[tick - back]:
                    unit.start(back)

    def finish(self, tick):
        if 0 <= tick - 3 < len(self.pairs):
            for unit, span in self.pairs[tick - 3]:
                self.settle(tick - 3, unit, span)
        for back in range(2, -1, -1):
            if 0 <= tick - back < len(self.pairs):
                for unit, _ in self.pairs[tick - back]:
                    unit.finish(back)

    def settle(self, at, unit, span):
        value = unit.result(3)
        first, size = span
        total = self.totals[at]
        if len(total.shape) == 2:
            total[first : first + size, :] = value
            return
        each = total.shape[1]
        for to in range(total.shape[0]):
            low, high = max(first, to * each), min(first + size, (to + 1) * each)
            if low < high:
                total[to, low - to * each : high - to * each, :] = value[
                    low - first : high - first, :
                ]

    def deliver(self):
        place = self.place
        mine = place.at["c"]
        self.kept, self.flights = [], []
        for total, final in zip(self.totals, self.finals):
            if len(total.shape) == 2:
                self.kept.append(self.sems.local(total, final))
                continue
            self.kept.append(self.sems.local(total.at[mine], final.at[mine]))
            for step in range(1, place.size["c"]):
                to = place.after("c", step)
                slot = self.sems.copy(total.at[to], final.at[mine], place.device("c", to))
                self.flights.append((final, step, slot))

    def delivered(self):
        for made in self.kept:
            made.wait()
        for final, step, slot in self.flights:
            source = self.place.before("c", step)
            self.sems.arrived(slot, final.at[source], self.place.device("c", source))


def sums_kernel(act_ref, up_ref, down_ref, act_full, dup_ref, ddown_ref, send, recv, *scratch):
    place = Place()
    sems = Sems(send, recv)
    sums = Sums(place, sems, (up_ref, down_ref), (dup_ref, ddown_ref), scratch)
    greet(place)
    act_done = exchange(place, sems, act_ref, act_full)
    for tick in range(sums.ticks):
        sums.start(tick)
        sums.finish(tick)
    sums.deliver()
    sums.delivered()
    act_done()
    sems.drain()


def sizes_of():
    dp, head = lax.axis_size("dp"), lax.axis_size("head")
    return {"z": 4, "x": 2, "c": dp // 8, "y": head}


def final_shape(grad, near):
    return jax.ShapeDtypeStruct((near, grad.shape[4] // near, grad.shape[5]), f32)


def sums_call(act, up, down):
    sizes = sizes_of()
    anywhere = pl.BlockSpec(memory_space=pl.ANY)
    needed = sems_needed(sizes, 4, 2 * sizes["y"] + 4 * sizes["c"])
    return pl.pallas_call(
        sums_kernel,
        in_specs=[anywhere] * 3,
        out_specs=[anywhere] * 3,
        out_shape=[
            jax.ShapeDtypeStruct(act.shape, bf16),
            final_shape(up, sizes["c"]),
            jax.ShapeDtypeStruct(down.shape[4:], f32),
        ],
        scratch_shapes=[
            pltpu.SemaphoreType.DMA((needed,)),
            pltpu.SemaphoreType.DMA((needed,)),
        ]
        + sum_scratch(sizes, (up.shape[4:] + (False,), down.shape[4:] + (True,))),
        compiler_params=pltpu.CompilerParams(
            collective_id=2, has_side_effects=True, vmem_limit_bytes=VMEM_MOST
        ),
        name="sum_feed_forward",
    )(act, up, down)


def finish_kernel(
    row_ref, ada_ref, rows_ref, hot_ref, gin_ref, qkv_ref, out_ref,
    bias_ref, dada_ref, gsilu_ref, gin_full, dqkv_ref, dout_ref,
    send, recv, share_send, share_recv, row_s, share_s, *scratch,
):
    place = Place()
    count, me = place.count, place.me
    sems = Sems(send, recv)
    sums = Sums(place, sems, (qkv_ref, out_ref), (dqkv_ref, dout_ref), scratch)
    greet(place)
    rows = Gather(place, sems, row_ref, row_s, "zxyc")
    rows.own()
    rows.start(0)
    gin_done = exchange(place, sems, gin_ref, gin_full)
    for tick in range(sums.ticks):
        sums.start(tick)
        sums.finish(tick)
        if tick < 4:
            rows.wait(tick)
            if tick < 3:
                rows.start(tick + 1)
    sums.deliver()

    whole = row_s[...].reshape(count, row_ref.shape[1])
    bias_ref[...] = jnp.sum(whole, axis=0, keepdims=True)
    cols = ada_ref.shape[1]
    low = jnp.zeros((count, cols), f32)
    for y in range(place.size["y"]):
        low = jnp.where(place.at["y"] == y, whole[:, y * cols : (y + 1) * cols], low)
    low = low.astype(bf16)
    dada_ref[...] = lax.dot_general(
        rows_ref[...].astype(bf16), low, (((0,), (0,)), ((), ())), preferred_element_type=f32
    )
    grad = mm_nt(low, ada_ref[...])
    hot = hot_ref[...][:, :count]
    placed = lax.dot_general(
        hot, grad, (((0,), (0,)), ((), ())), precision=lax.Precision.HIGHEST,
        preferred_element_type=f32,
    )
    pad = share_s.shape[2] - placed.shape[1]
    placed = jnp.concatenate([placed, jnp.zeros((count, pad), f32)], axis=1)
    share_s[...] = placed.reshape(share_s.shape)

    def push(step):
        to = lax.rem(me + step, count)
        return pltpu.make_async_remote_copy(
            src_ref=share_s.at[to], dst_ref=gsilu_ref.at[me],
            send_sem=share_send.at[step], recv_sem=share_recv.at[step],
            device_id=place.numbered(to), device_id_type=MESH,
        )

    def came(step):
        source = lax.rem(me + count - step, count)
        return pltpu.make_async_remote_copy(
            src_ref=gsilu_ref.at[source], dst_ref=gsilu_ref.at[source],
            send_sem=share_send.at[step], recv_sem=share_recv.at[step],
            device_id=place.numbered(source), device_id_type=MESH,
        )

    def do_push(step, carry):
        push(step).start()
        return carry

    def do_wait(step, carry):
        came(step).wait_recv()
        push(step).wait_send()
        return carry

    lax.fori_loop(1, count, do_push, 0)
    gsilu_ref[me] = share_s[me]
    lax.fori_loop(1, count, do_wait, 0)
    sums.delivered()
    gin_done()
    sems.drain()


def finish_call(row, ada, silu_rows, hot, gin, qkv, out):
    sizes = sizes_of()
    near = sizes["c"]
    count = 8 * near * sizes["y"]
    anywhere = pl.BlockSpec(memory_space=pl.ANY)
    vmem = pl.BlockSpec(memory_space=pltpu.VMEM)
    needed = sems_needed(sizes, 5, 2 * sizes["y"] + 4 * near)
    return pl.pallas_call(
        finish_kernel,
        in_specs=[anywhere, vmem, vmem, vmem] + [anywhere] * 3,
        out_specs=[vmem] * 3 + [anywhere] * 3,
        out_shape=[
            jax.ShapeDtypeStruct(row.shape, f32),
            jax.ShapeDtypeStruct(ada.shape, f32),
            jax.ShapeDtypeStruct((count, 1, 128), f32),
            jax.ShapeDtypeStruct(gin.shape, bf16),
            final_shape(qkv, near),
            final_shape(out, near),
        ],
        scratch_shapes=[
            pltpu.SemaphoreType.DMA((needed,)),
            pltpu.SemaphoreType.DMA((needed,)),
            pltpu.SemaphoreType.DMA((count,)),
            pltpu.SemaphoreType.DMA((count,)),
            pltpu.VMEM((4, 2, near, sizes["y"], 1, row.shape[1]), f32),
            pltpu.VMEM((count, 1, 128), f32),
        ]
        + sum_scratch(sizes, (qkv.shape[4:] + (False,), out.shape[4:] + (False,))),
        compiler_params=pltpu.CompilerParams(
            collective_id=1, has_side_effects=True, vmem_limit_bytes=VMEM_MOST
        ),
        name="sum_finish",
    )(row, ada, silu_rows, hot, gin, qkv, out)


class Wire:
    def __init__(self, width):
        self.dp = lax.axis_size("dp")
        self.head = lax.axis_size("head")
        self.near = self.dp // (width // 144)
        self.width = width
        self.groups = [
            list(range(first, first + self.near)) for first in range(0, self.dp, self.near)
        ]

    def piece(self, weight):
        return lax.all_to_all(
            weight.astype(bf16), "dp", split_axis=1, concat_axis=0,
            axis_index_groups=self.groups, tiled=True,
        )

    def unpiece(self, piece):
        return lax.all_to_all(
            piece, "dp", split_axis=0, concat_axis=1, axis_index_groups=self.groups, tiled=True
        )

    def gather(self, piece):
        return lax.all_gather(piece, ("dp", "head"), axis=0)

    def scatter(self, stack):
        return lax.psum_scatter(stack, ("dp", "head"), scatter_dimension=0)

    def columns(self, stack):
        devices, rows, cols = stack.shape
        stack = stack.reshape(self.dp // self.near, self.near, self.head, rows, cols)
        if (self.near, self.head) != (2, 2):
            quarter = self.near * self.head * cols // 4
            stack = stack.transpose(0, 3, 2, 1, 4).reshape(-1, rows, 2, 2, quarter)
            stack = stack.transpose(0, 3, 2, 1, 4)
            return stack.reshape(-1, 4, rows, quarter)
        return stack.reshape(-1, 4, rows, cols)

    def uncolumns(self, stack):
        groups, _, rows, quarter = stack.shape
        cols = 4 * quarter // (self.near * self.head)
        if (self.near, self.head) != (2, 2):
            stack = stack.reshape(groups, 2, 2, rows, quarter).transpose(0, 3, 2, 1, 4)
            stack = stack.reshape(groups, rows, self.head, self.near, cols)
            stack = stack.transpose(0, 3, 2, 1, 4)
        return stack.reshape(self.dp * self.head, rows, cols)

    def rows(self, stack):
        devices, rows, cols = stack.shape
        if self.head != 2 or self.dp != 16:
            stack = stack.reshape(self.dp, self.head, rows, cols).transpose(0, 2, 1, 3)
            stack = stack.reshape(16, self.dp * rows // 16, 2, self.head * cols // 2)
            return stack.transpose(0, 2, 1, 3)
        return stack.reshape(self.dp, self.head, rows, cols)

    def unrows(self, stack):
        _, _, rows, cols = stack.shape
        if self.head != 2 or self.dp != 16:
            stack = stack.transpose(0, 2, 1, 3).reshape(
                self.dp, 16 * rows // self.dp, self.head, 2 * cols // self.head
            )
            stack = stack.transpose(0, 2, 1, 3)
        return stack.reshape(self.dp * self.head, stack.shape[-2], stack.shape[-1])


def body(
    inputs, cond, order, grid_kind, weight_ada, bias_ada, weight_qkv, bias_query, bias_value,
    weight_out, bias_out, weight_up, bias_up, weight_down, bias_down, cotangent,
):
    images, slot_local, width = inputs.shape
    head_count = lax.axis_size("head")
    dp_count = lax.axis_size("dp")
    head_at = lax.axis_index("head")
    dp_at = lax.axis_index("dp")
    assert images == head_count
    wire = Wire(width)

    def from_image(array):
        return lax.all_to_all(
            array[None], "head", split_axis=1, concat_axis=0, tiled=True
        ).astype(f32)

    rows_ada, cols_ada = weight_ada.shape
    ada_low = weight_ada.astype(bf16)
    silu_own, silu_pull = jax.vjp(lambda v: v * jax.nn.sigmoid(v), cond)
    order_mine = lax.dynamic_slice_in_dim(order, head_at, 1, 0)
    kind = lax.dynamic_slice_in_dim(grid_kind, head_at, 1, 0)
    mod, silu_grouped, hot, x, cot, qkv_full, out_full, up_full, down_full = start_call(
        silu_own, order_mine, ada_low, inputs.astype(bf16), cotangent.astype(bf16),
        wire.piece(weight_qkv), wire.piece(weight_out), wire.piece(weight_up),
        weight_down.astype(bf16),
    )
    x = x.reshape(-1, width)
    cot = cot.reshape(-1, width)
    device_stack = lambda full: full.reshape((-1,) + full.shape[4:])
    qkv_full = wire.columns(device_stack(qkv_full))
    out_full = wire.columns(device_stack(out_full))
    up_full = wire.columns(device_stack(up_full))
    down_full = wire.rows(device_stack(down_full))
    mod_flat = mod.reshape(6, width) + bias_ada.reshape(6, width)
    mod = jnp.concatenate([mod_flat, jnp.zeros((2, width), f32)], axis=0)

    bias_qkv = jnp.concatenate([bias_query, jnp.zeros_like(bias_query), bias_value])
    qkv, norm = qkv_call(x, mod, qkv_full, bias_qkv.reshape(4, 1, -1))
    mix, lse = attn_call(kind, qkv)
    attended, branch, second = out_call(mix, x, mod, out_full, bias_out)
    mlp, gsec, d_up, d_down, d_bias_up = mlp_call(
        second, cot, mod, up_full, down_full, bias_up.reshape(4, 1, -1)
    )
    act, gmid, gatt, d_out, sums = mid_back_call(
        x, branch, mlp, gsec, cot, attended, mod, out_full, bias_down
    )
    lead = (4, 2, dp_count // 8, head_count)
    stack = lambda grad: grad.reshape(lead + grad.shape[1:])
    by_image = lambda array: array.reshape(head_count, slot_local, width)
    act, d_up, d_down = sums_call(
        by_image(act), stack(wire.uncolumns(d_up)), stack(wire.unrows(d_down))
    )
    grad = attn_back_call(kind, qkv, gatt, lse)
    gin, d_qkv, d_bias_qkv, sums_in = qkv_back_call(
        grad.reshape(qkv.shape), norm, qkv_full, x, gmid, mod
    )

    bias_qkv_sum = d_bias_qkv.reshape(3, width)
    row = jnp.concatenate(
        [sums_in[0], sums_in[1], sums[0], sums[1], sums[2], sums[3],
         bias_qkv_sum[0], bias_qkv_sum[2], sums[4], sums[5], d_bias_up.reshape(-1)]
    ).reshape(1, -1)
    biases, d_ada, g_silu, gin, d_qkv, d_out = finish_call(
        row, ada_low, silu_grouped, hot, by_image(gin),
        stack(wire.uncolumns(d_qkv)), stack(wire.uncolumns(d_out)),
    )
    biases = biases[0]
    g_silu = g_silu.reshape(dp_count, head_count, 128)[:, :, :rows_ada].sum(axis=1)
    d_cond = silu_pull(g_silu.reshape(1, width))[0]
    side = lambda grad: grad.transpose(1, 0, 2).reshape(grad.shape[1], -1)
    mods = 6 * width
    return (
        act.astype(f32),
        gin.astype(f32),
        d_cond,
        d_ada,
        side(d_qkv),
        side(d_out),
        side(d_up),
        d_down,
        biases[:mods],
        biases[mods : mods + width],
        biases[mods + width : mods + 2 * width],
        biases[mods + 2 * width : mods + 3 * width],
        biases[mods + 4 * width :],
        biases[mods + 3 * width : mods + 4 * width],
    )


def solution(mesh):
    in_specs = (
        P("dp", "head", None), P(("dp", "head"), None), P("dp"), P("dp"), P("dp", "head"), P(),
        P("dp", "head"), P(), P(), P("dp", "head"), P(), P("dp", "head"), P(), P("dp", "head"),
        P(), P("dp", "head", None),
    )
    out_specs = (
        P("dp", "head", None), P("dp", "head", None), P(("dp", "head"), None), P("dp", "head"),
        P("dp", "head"), P("dp", "head"), P("dp", "head"), P("dp", "head"),
        P(), P(), P(), P(), P(), P(),
    )
    return jax.shard_map(body, mesh=mesh, in_specs=in_specs, out_specs=out_specs, check_vma=False)
```

time: 1720 us -> 934 us (0.54)
  Pallas kernels: 0 us -> 870 us
  waiting for transfers between devices: 502 us -> 0.01 us
  matrix products: 435 us -> 0 us
  blocking collectives: 336 us -> 9.24 us
  local copies, waits for them, and re-layouts: 254 us -> 16.8 us
  other arithmetic: 147 us -> 23.3 us
    pallas_call x0 -> x10, Pallas kernels: none -> 870 us  [the longest x1 269 us: start_call(): pl.pallas_call(start_kernel, in_specs=[anywhere, vmem] + [anywhere] * 6,...]
    dot_general x28 -> x0, matrix products: 435 us -> none  [the longest x4 64.1 us: masked_scores(): jnp.einsum('bshd,bthd->bhst', queries, keys_in, preferred_element_type=jn...]
    unnamed x23 -> x0, waiting for transfers between devices: 234 us -> none
    all_gather x6 -> x0, blocking collectives: 191 us -> none  [the longest x1 86.7 us: fetch_weights(): lax.all_gather(weight_down.astype(jnp.bfloat16), 'head', axis=1, tiled=True)]
    reduce_scatter x4 -> x0, waiting for transfers between devices: 146 us -> none  [the longest x1 130 us: body(): lax.psum_scatter(grad_weight_ada.astype(jnp.bfloat16), 'dp', scatter_dime...]
    all_to_all x1 -> x2, blocking collectives: 97 us -> 9.24 us  [piece(): lax.all_to_all(weight.astype(bf16), 'dp', split_axis=1, concat_axis=0, ax...]
    all_to_all x7 -> x5, local copies, waits for them, and re-layouts: 87.9 us -> 1.19 us  [piece(): lax.all_to_all(weight.astype(bf16), 'dp', split_axis=1, concat_axis=0, ax...]
    reshape x7 -> x13, local copies, waits for them, and re-layouts: 92.9 us -> 6.32 us  [the longest x3 2.92 us: body(): side = lambda grad: grad.transpose(1, 0, 2).reshape(grad.shape[1], -1)]
  transfers between devices with their start and end apart: 19 -> 1, of which waited for: 12 -> 0; matrix products, arithmetic and copies ran while one was open for 43% -> 1% of each run, Pallas kernels for 0% -> 0%
where the time goes in v1:
time: 934 us; the launch traced here: 925 us
  Pallas kernels  870 us (93%)
  other arithmetic  23.3 us (2%)
  local copies, waits for them, and re-layouts  16.8 us (2%)
    pallas_call x1, Pallas kernels, start_call(): pl.pallas_call(start_kernel, in_specs=[anywhere, vmem] + [anywhere] * 6,...  269 us
    pallas_call x1, Pallas kernels, sums_call(): pl.pallas_call(sums_kernel, in_specs=[anywhere] * 3, out_specs=[anywhere]...  168 us
    pallas_call x1, Pallas kernels, finish_call(): pl.pallas_call(finish_kernel, in_specs=[anywhere, vmem, vmem, vmem] + [an...  132 us
    pallas_call x1, Pallas kernels, mlp_call(): pl.pallas_call(functools.partial(mlp_kernel, tm), grid=(parts,), in_specs...  98.6 us
    pallas_call x1, Pallas kernels, attn_back_call(): pl.pallas_call(functools.partial(attn_back_kernel, ts), grid=(H,), in_spe...  57.7 us
    pallas_call x1, Pallas kernels, attn_call(): pl.pallas_call(functools.partial(attn_kernel, ts), grid=(H,), in_specs=[p...  50.5 us
    pallas_call x1, Pallas kernels, qkv_back_call(): pl.pallas_call(functools.partial(qkv_back_kernel, tm), grid=(parts,), in_...  37.5 us
    pallas_call x1, Pallas kernels, qkv_call(): pl.pallas_call(functools.partial(qkv_kernel, tm), grid=(parts, slots // t...  25.3 us
  transfers between devices with their start and end apart: 1, of which 0 were waited for; matrix products, arithmetic and copies ran while one was open for 1% of the time, Pallas kernels for 0%

profile of v1, /device:TPU:0, one launch (start us, length us, event | category | flops | bytes accessed | tf_op | source)
XLA Modules:
  0.0 925.1 jit_solution(10514982737298403147)
XLA Ops:
  0.6 1.1 convert_element_type.45
  2.7 3.4 all-to-all-start
  6.2 1.2 dynamic_slice.6
  8.8 2.2 convert_element_type.42.ada_ref
  11.0 4.0 convert_element_type.43.x_ref
  15.0 1.6 convert_element_type.44.cot_ref
  18.4 4.7 all_to_all.57
  23.1 4.5 all_to_all.58
  27.6 268.6 %gather_start.1 = (f32[2,1,3456]{2,1,0:T(1,128)}, f32[32,72]{1,0:T(8,128)}, f32[32,128]{1,0:T(8,128)}, bf16[2,512,1152]{2,1,0:T(8,128)(2,1)}, bf16[2,512,1152]{2...) custom-call(f32[1,1280]{1,0:T(1,128)} %concatenate.12.silu_ref, ...), custom_call_target="tpu_custom_call" | custom-call | tf_op jit(solution)/shard_map/gather_start/pallas_call | solution.py:807
  300.9 25.3 %qkv_forward.1 = (bf16[48,1024,72]{2,1,0:T(8,128)(2,1)}, bf16[1024,1152]{1,0:T(8,128)(2,1)}) custom-call(bf16[1024,1152]{1,0:T(8,128)(2,1)} %bitcast.34, f32[8,1152]{1,0:T(8,128)} %concatenate.13.mod_ref, bf16[8,4,144,864]{3,2,1,0:T(8,128)(2,1)} %bitcast.38, f32[4,1,864]{2,1,0:T(1,128)} %reshape.106.b_ref), custom_call_target="tpu_custom_call" | custom-call | tf_op jit(solution)/shard_map/qkv_forward/pallas_call | solution.py:84
  326.2 50.5 %attention_forward.1 = (bf16[16,1024,72]{2,1,0:T(8,128)(2,1)}, f32[16,1,1024]{2,1,0:T(1,128)}) custom-call(s32[1]{0:T(128)} %dynamic_slice.7.kind_ref, bf16[48,1024,72]{2,1,0:T(8,128)(2,1)} %get-tuple-element.56.q_ref.k_ref.v_ref, bf16[48,1024,72]{2,1,0:T(8,128)(2,1)} %get-tuple-element.56.q_ref.k_ref.v_ref, ...), custom_call_target="tpu_custom_call" | custom-call | tf_op jit(solution)/shard_map/attention_forward/pallas_call | solution.py:134
  376.7 10.2 %out_projection.1 = (bf16[1024,1152]{1,0:T(8,128)(2,1)}, bf16[1024,1152]{1,0:T(8,128)(2,1)}, bf16[1024,1152]{1,0:T(8,128)(2,1)}) custom-call(bf16[16,1024,72]{2,1,0:T(8,128)(2,1)} %get-tuple-element.57.o_ref, bf16[1024,1152]{1,0:T(8,128)(2,1)} %bitcast.35, f32[8,1152]{1,0:T(8,128)} %concatenate.13.mod_ref, bf16[8,4,144,288]{3,2,1,0:T(8,128)(2,1)} %bitcast.40, ...), custom_call_target="tpu_custom_call" | custom-call | tf_op jit(solution)/shard_map/out_projection/pallas_call | solution.py:237
  386.9 98.6 %feed_forward_both_ways.1 = (f32[1024,1152]{1,0:T(8,128)}, f32[1024,1152]{1,0:T(8,128)}, bf16[8,4,144,1152]{3,2,1,0:T(8,128)(2,1)}, bf16[16,2,288,576]{3,2,1,0:T(8,128)(2,1)}, f32[4,1,1152]{2,1,0:T(1,128)}) custom-call(bf16[1024,1152]{1,0:T(8,128)(2,1)} %get-tuple-element.60.second_ref, bf16[1024,1152]{1,0:T(8,128)(2,1)} %bitcast.46, ...), custom_call_target="tpu_custom_call" | custom-call | tf_op jit(solution)/shard_map/feed_forward_both_ways/pallas_call | solution.py:324
  485.5 21.4 %middle_backward.1 = (bf16[1024,1152]{1,0:T(8,128)(2,1)}, f32[1024,1152]{1,0:T(8,128)}, bf16[16,1024,72]{2,1,0:T(8,128)(2,1)}, bf16[8,4,144,288]{3,2,1,0:T(8,128)(2,1)}, f32[8,1152]{1,0:T(8,128)}) custom-call(bf16[1024,1152]{1,0:T(8,128)(2,1)} %bitcast.36, bf16[1024,1152]{1,0:T(8,128)(2,1)} %get-tuple-element.59.branch_ref, ...), custom_call_target="tpu_custom_call" | custom-call | tf_op jit(solution)/shard_map/middle_backward/pallas_call | solution.py:418
  506.9 57.7 %attention_backward.1 = bf16[3,16,1024,72]{3,2,1,0:T(8,128)(2,1)} custom-call(s32[1]{0:T(128)} %dynamic_slice.7.kind_ref, bf16[48,1024,72]{2,1,0:T(8,128)(2,1)} %get-tuple-element.56.q_ref.k_ref.v_ref, bf16[48,1024,72]{2,1,0:T(8,128)(2,1)} %get-tuple-element.56.q_ref.k_ref.v_ref, bf16[48,1024,72]{2,1,0:T(8,128)(2,1)} %get-tuple-element.56.q_ref.k_ref.v_ref, ...), custom_call_target="tpu_custom_call" | custom-call | tf_op jit(solution)/shard_map/attention_backward/pallas_call | solution.py:192
  564.6 37.5 %qkv_backward.1 = (bf16[1024,1152]{1,0:T(8,128)(2,1)}, bf16[8,4,144,864]{3,2,1,0:T(8,128)(2,1)}, f32[4,1,864]{2,1,0:T(1,128)}, f32[8,1152]{1,0:T(8,128)}) custom-call(bf16[48,1024,72]{2,1,0:T(8,128)(2,1)} %bitcast.33, bf16[1024,1152]{1,0:T(8,128)(2,1)} %get-tuple-element.73.norm_ref, bf16[8,4,144,864]{3,2,1,0:T(8,128)(2,1)} %bitcast.39, ...), custom_call_target="tpu_custom_call" | custom-call | tf_op jit(solution)/shard_map/qkv_backward/pallas_call | solution.py:499
  604.9 132.0 %sum_finish.1 = (f32[1,16128]{1,0:T(1,128)}, f32[72,3456]{1,0:T(8,128)}, f32[32,1,128]{2,1,0:T(1,128)}, bf16[2,512,1152]{2,1,0:T(8,128)(2,1)}, f32[2,72,864]{2,1,0:T(8,128)}, /*index=5*/f32[2,72,288]{2,1,0:T(8,128)}) custom-call(f32[1,16128]{1,0:T(1,128)} %reshape.115.row_ref, bf16[72,3456]{1,0:T(8,128)(2,1)} %convert_element_type.42.ada_ref, ...), custom_call_target="tpu_custom_call" | custom-call | tf_op jit(solution)/shard_map/sum_finish/pallas_call | solution.py:1142
  736.8 1.5 slice_reduce_fusion
  738.3 1.4 slice_reduce_fusion.1
  740.5 4.2 convert_element_type.50
  745.0 1.2 reshape.119
  747.2 168.4 %sum_feed_forward.1 = (bf16[2,512,1152]{2,1,0:T(8,128)(2,1)}, f32[2,72,1152]{2,1,0:T(8,128)}, f32[288,576]{1,0:T(8,128)}) custom-call(bf16[2,512,1152]{2,1,0:T(8,128)(2,1)} %bitcast.50, bf16[4,2,2,2,144,1152]{5,4,3,2,1,0:T(8,128)(2,1)} %bitcast.44, bf16[4,2,2,2,288,576]{5,4,3,2,1,0:T(8,128)(2,1)} %bitcast.42), custom_call_target="tpu_custom_call" | custom-call | tf_op jit(solution)/shard_map/sum_feed_forward/pallas_call | solution.py:1038
  915.6 4.3 convert_element_type.49
  920.8 2.0 slice_reduce_fusion.5
  (91 shorter events, 15.4 us)
Async XLA Ops:
  2.7 15.7 %all-to-all-start = ((bf16[72,2,864]{2,0,1:T(8,128)(2,1)}), bf16[72,2,864]{2,0,1:T(8,128)(2,1)S(1)}, u32[]{:S(2)}, u32[]{:S(2)}) async-start(bf16[72,2,864]{2,0,1:T(8,128)(2,1)} %copy.33), calls=%async_computation | async-start | bytes 516096 | tf_op jit(solution)/shard_map/all_to_all | solution.py:1181
  8.8 6.2 copy-start
  15.0 1.7 copy-start.5
  15.0 1.7 copy-start.3
  15.0 2.5 copy-start.9
  17.5 279.6 %copy-start.10 = (f32[6912]{0:T(1024)S(1)}, f32[6912]{0:T(1024)}, u32[]{:S(2)}) copy-start(f32[6912]{0:T(1024)} %param.21) | copy-start | bytes 82948
  17.5 280.3 %copy-start.15 = (f32[1152]{0:T(1024)S(1)}, f32[1152]{0:T(1024)}, u32[]{:S(2)}) copy-start(f32[1152]{0:T(1024)} %param.24) | copy-start | bytes 13828
  17.5 280.3 %copy-start.16 = (f32[1152]{0:T(1024)S(1)}, f32[1152]{0:T(1024)}, u32[]{:S(2)}) copy-start(f32[1152]{0:T(1024)} %param.23) | copy-start | bytes 13828
  17.5 281.0 %copy-start.19 = (s32[2]{0:T(128)S(1)}, s32[2]{0:T(128)}, u32[]{:S(2)}) copy-start(s32[2]{0:T(128)} %param.19) | copy-start | bytes 28
  17.5 281.6 %copy-start.17 = (f32[1152]{0:T(1024)S(1)}, f32[1152]{0:T(1024)}, u32[]{:S(2)}) copy-start(f32[1152]{0:T(1024)} %param.26) | copy-start | bytes 13828
  17.5 282.1 %copy-start.12 = (f32[4608]{0:T(1024)S(1)}, f32[4608]{0:T(1024)}, u32[]{:S(2)}) copy-start(f32[4608]{0:T(1024)} %param.28) | copy-start | bytes 55300
  17.6 282.8 %copy-start.18 = (f32[1152]{0:T(1024)S(1)}, f32[1152]{0:T(1024)}, u32[]{:S(2)}) copy-start(f32[1152]{0:T(1024)} %param.30) | copy-start | bytes 13828
  18.4 9.2 copy-start.1
  564.6 38.4 %copy-start.11 = (f32[8,1152]{1,0:T(8,128)S(1)}, f32[8,1152]{1,0:T(8,128)}, u32[]{:S(2)}) copy-start(f32[8,1152]{1,0:T(8,128)} %get-tuple-element.76) | copy-start | bytes 110596
  564.6 39.4 %copy-start.14 = (f32[4,1,1152]{2,1,0:T(1,128)S(1)}, f32[4,1,1152]{2,1,0:T(1,128)}, u32[]{:S(2)}) copy-start(f32[4,1,1152]{2,1,0:T(1,128)} %get-tuple-element.78) | copy-start | bytes 55300
  736.8 7.9 copy-start.7
  740.5 5.7 copy-start.8
  915.6 4.4 copy-start.6
  915.6 5.2 copy-start.13
  915.6 7.2 copy-start.2
  915.6 8.1 copy-start.4

commit v2 on v0

v2 whole, which is shorter than its diff:
```python
import functools
import math

import jax
import jax.numpy as jnp
from jax import lax
from jax.experimental import pallas as pl
from jax.experimental.pallas import tpu as pltpu
from jax.sharding import PartitionSpec as P

H = 16
norm_eps = 1e-06
log2_e = 1.4426950408889634
gelu_in = 0.7978845608028654
gelu_cube = 0.044715
f32 = jnp.float32
bf16 = jnp.bfloat16
VMEM_MOST = 60 * 1024 * 1024


def mm(left, right):
    return jnp.dot(left, right, preferred_element_type=f32)


def mm_nt(left, right):
    return lax.dot_general(left, right, (((1,), (1,)), ((), ())), preferred_element_type=f32)


def center_spread(values):
    center = values - jnp.mean(values, axis=-1, keepdims=True)
    spread = jnp.mean(center * center, axis=-1, keepdims=True)
    return center, lax.rsqrt(spread + norm_eps)


def norm_back(grad, unit, inv):
    return inv * (
        grad
        - jnp.mean(grad, axis=-1, keepdims=True)
        - unit * jnp.mean(grad * unit, axis=-1, keepdims=True)
    )


def whole_spec(shape):
    zeros = (0,) * len(shape)
    return pl.BlockSpec(shape, lambda *_: zeros)


def once_spec(shape):
    zeros = (0,) * len(shape)
    return pl.BlockSpec(shape, lambda *_: zeros, pipeline_mode=pl.Buffered(1))


def params(most=VMEM_MOST):
    return pltpu.CompilerParams(vmem_limit_bytes=most)


def place(quarter):
    return (quarter % 2) * 2 + quarter // 2


def masked(scores, full, kept):
    return jnp.concatenate(
        [scores[:kept], jnp.where(full, scores[kept:], -1e30)], axis=0
    )


def columns_of(w_ref):
    groups, parts, rows_each, width = w_ref.shape
    return jnp.concatenate(
        [w_ref[:, place(n)].reshape(groups * rows_each, width) for n in range(parts)], axis=1
    )


def out_kernel(
    o_ref, x_ref, cot_ref, mod_ref, w_ref, b_ref, att_ref, branch_ref, second_ref, gm_ref, w_s
):
    @pl.when(pl.program_id(0) == 0)
    def _():
        w_s[...] = columns_of(w_ref)

    attended = jnp.concatenate([o_ref[j] for j in range(o_ref.shape[0])], axis=1)
    att_ref[...] = attended
    branch = mm(attended, w_s[...]) + b_ref[...]
    branch_ref[...] = branch.astype(bf16)
    middle = x_ref[...].astype(f32) + mod_ref[2:3, :] * branch
    center, inv = center_spread(middle)
    second_ref[...] = (center * inv * (1.0 + mod_ref[4:5, :]) + mod_ref[3:4, :]).astype(bf16)
    gm_ref[...] = (cot_ref[...].astype(f32) * mod_ref[5:6, :]).astype(bf16)


def out_call(mix, x, cot, mod, weight, bias):
    slots, width = x.shape
    tm = min(256, slots)
    size = width // H
    tile = pl.BlockSpec((tm, width), lambda i: (i, 0))
    return pl.pallas_call(
        out_kernel,
        grid=(slots // tm,),
        in_specs=[
            pl.BlockSpec((H, tm, size), lambda i: (0, i, 0)),
            tile,
            tile,
            whole_spec(mod.shape),
            whole_spec(weight.shape),
            whole_spec((1, width)),
        ],
        out_specs=[tile] * 4,
        out_shape=[jax.ShapeDtypeStruct((slots, width), bf16)] * 4,
        scratch_shapes=[pltpu.VMEM((width, width), bf16)],
        compiler_params=params(),
        name="out_projection",
    )(mix, x, cot, mod, weight, bias.reshape(1, width))


def mid_back_kernel(
    x_ref, branch_ref, mlp_ref, gsec_ref, cot_ref, att_ref, mod_ref, w_ref, b_ref,
    act_ref, gmid_ref, gatt_ref, dw_ref, sums_ref, w_s, dw_s,
):
    step = pl.program_id(0)

    @pl.when(step == 0)
    def _():
        w_s[...] = columns_of(w_ref)
        sums_ref[...] = jnp.zeros_like(sums_ref)
        dw_s[...] = jnp.zeros_like(dw_s)

    gate_a = mod_ref[2:3, :]
    gate_m = mod_ref[5:6, :]
    branch = branch_ref[...].astype(f32)
    middle = x_ref[...].astype(f32) + gate_a * branch
    mlp = mlp_ref[...] + b_ref[...]
    cot = cot_ref[...].astype(f32)
    act_ref[...] = (middle + gate_m * mlp).astype(act_ref.dtype)
    center, inv = center_spread(middle)
    unit = center * inv
    grad = gsec_ref[...]
    grad_mid = cot + norm_back(grad * (1.0 + mod_ref[4:5, :]), unit, inv)
    gmid_ref[...] = grad_mid
    grad_branch = gate_a * grad_mid

    def add(row, value):
        sums_ref[row : row + 1, :] += jnp.sum(value, axis=0, keepdims=True)

    add(0, grad_mid * branch)
    add(1, grad)
    add(2, grad * unit)
    add(3, cot * mlp)
    add(4, grad_branch)
    add(5, gate_m * cot)
    grad_low = grad_branch.astype(bf16)
    grad_att = mm_nt(grad_low, w_s[...]).astype(bf16)
    size = gatt_ref.shape[2]
    for j in range(gatt_ref.shape[0]):
        gatt_ref[j] = grad_att[:, j * size : (j + 1) * size]
    dw_s[...] += mm(att_ref[...].T, grad_low)

    @pl.when(step == pl.num_programs(0) - 1)
    def _():
        groups, parts, rows_each, width = dw_ref.shape
        low = dw_s[...].astype(bf16)
        for n in range(parts):
            dw_ref[:, place(n)] = low[:, n * width : (n + 1) * width].reshape(
                groups, rows_each, width
            )


def mid_back_call(x, branch, mlp, gsec, cot, attended, mod, weight, bias_down):
    slots, width = x.shape
    tm = min(256, slots)
    size = width // H
    tile = pl.BlockSpec((tm, width), lambda i: (i, 0))
    return pl.pallas_call(
        mid_back_kernel,
        grid=(slots // tm,),
        in_specs=[tile] * 6 + [whole_spec(mod.shape), whole_spec(weight.shape), whole_spec((1, width))],
        out_specs=[
            tile,
            tile,
            pl.BlockSpec((H, tm, size), lambda i: (0, i, 0)),
            whole_spec(weight.shape),
            whole_spec((8, width)),
        ],
        out_shape=[
            jax.ShapeDtypeStruct((slots, width), bf16),
            jax.ShapeDtypeStruct((slots, width), f32),
            jax.ShapeDtypeStruct((H, slots, size), bf16),
            jax.ShapeDtypeStruct(weight.shape, bf16),
            jax.ShapeDtypeStruct((8, width), f32),
        ],
        scratch_shapes=[pltpu.VMEM((width, width), bf16), pltpu.VMEM((width, width), f32)],
        compiler_params=params(),
        name="middle_backward",
    )(x, branch, mlp, gsec, cot, attended, mod, weight, bias_down.reshape(1, width))


MESH = pl.DeviceIdType.MESH


class Place:
    def __init__(self):
        self.dp = lax.axis_size("dp")
        head = lax.axis_size("head")
        near = self.dp // 8
        at = lax.axis_index("dp")
        self.size = {"z": 4, "x": 2, "c": near, "y": head}
        self.at = {
            "z": lax.div(at, 2 * near),
            "x": lax.rem(lax.div(at, near), 2),
            "c": lax.rem(at, near),
            "y": lax.axis_index("head"),
        }
        self.count = self.dp * head
        self.me = at * head + self.at["y"]

    def device(self, axis, index):
        spot = dict(self.at)
        spot[axis] = index
        return ((spot["z"] * 2 + spot["x"]) * self.size["c"] + spot["c"], spot["y"])

    def numbered(self, index):
        head = self.size["y"]
        return (lax.div(index, head), lax.rem(index, head))

    def after(self, axis, step):
        return lax.rem(self.at[axis] + step, self.size[axis])

    def before(self, axis, step):
        return lax.rem(self.at[axis] + self.size[axis] - step, self.size[axis])


class Local:
    def __init__(self, sem, ends):
        self.sem, self.ends = sem, ends

    def made(self):
        return pltpu.make_async_copy(*self.ends(), self.sem())

    def wait(self):
        self.made().wait()


class Sems:
    def __init__(self, send, recv):
        self.send, self.recv, self.used = send, recv, 0
        self.sent = []

    def describe(self, at, src, dst, device):
        return pltpu.make_async_remote_copy(
            src_ref=src, dst_ref=dst, send_sem=self.send.at[at], recv_sem=self.recv.at[at],
            device_id=device, device_id_type=MESH,
        )

    def copy(self, ends):
        at = self.used
        self.used += 1
        self.describe(at, *ends()).start()
        self.sent.append((at, ends))
        return at

    def arrived(self, at, dst, device):
        self.describe(at, dst, dst, device).wait_recv()

    def local(self, ends):
        at = self.used
        self.used += 1
        made = Local(lambda: self.send.at[at], ends)
        made.made().start()
        return made

    def drain(self):
        for at, ends in self.sent:
            self.describe(at, *ends()).wait_send()


AXES = "zxcy"


def spans_of(rows, count):
    cuts = [16 * (rows // 16 * at // count) for at in range(count)] + [rows]
    return [(low, high - low) for low, high in zip(cuts, cuts[1:])]


def halves(rows):
    return spans_of(rows, 2)


class Gather:
    def __init__(self, place, sems, piece, full, axes, rows=None):
        self.place, self.sems, self.piece, self.full, self.axes = place, sems, piece, full, axes
        self.rows = rows
        self.slots = {}

    def part(self, got, axis=None, index=None):
        spot = dict(self.place.at)
        if axis is not None:
            spot[axis] = index
        spots = tuple(slice(None) if name in got else spot[name] for name in AXES)
        if self.rows is not None:
            spots = spots + (pl.ds(*self.rows), slice(None))
        return self.full.at[spots]

    def first(self):
        return self.piece if self.rows is None else self.piece.at[pl.ds(*self.rows)]

    def own(self):
        self.kept = self.sems.local(lambda: (self.first(), self.part("")))

    def start(self, stage):
        axis = self.axes[stage]
        got = self.axes[:stage]
        if stage == 1:
            self.kept.wait()

        def ends(step):
            return (
                self.first() if stage == 0 else self.part(got),
                self.part(got),
                self.place.device(axis, self.place.after(axis, step)),
            )

        for step in range(1, self.place.size[axis]):
            self.slots[stage, step] = self.sems.copy(functools.partial(ends, step))

    def wait(self, stage):
        axis = self.axes[stage]
        got = self.axes[:stage]
        for step in range(1, self.place.size[axis]):
            index = self.place.before(axis, step)
            self.sems.arrived(
                self.slots[stage, step], self.part(got, axis, index), self.place.device(axis, index)
            )


EVEN = ("zxyc", "zyxc")
WIDE = ("zyxc", "yzxc")


class Gathers:
    def __init__(self, place, sems, spans, orders):
        self.pairs = []
        for at in range(0, len(spans), 2):
            pair = orders[at // 2 % len(orders)]
            self.pairs.append(
                [
                    Gather(place, sems, piece, full, axes, rows)
                    for (piece, full, rows), axes in zip(spans[at : at + 2], pair)
                ]
            )
        self.ticks = len(self.pairs) + 3

    def advance(self, tick):
        if tick < len(self.pairs):
            for unit in self.pairs[tick]:
                unit.own()
                unit.start(0)
        for stage in (1, 0, 2, 3):
            if 0 <= tick - 1 - stage < len(self.pairs):
                for unit in self.pairs[tick - 1 - stage]:
                    unit.wait(stage)
                    if stage < 3:
                        unit.start(stage + 1)


def greet_all(place):
    barrier = pltpu.get_barrier_semaphore()

    def one(step, carry):
        pl.semaphore_signal(
            barrier, inc=1, device_id=place.numbered(lax.rem(place.me + step, place.count)),
            device_id_type=MESH,
        )
        return carry

    lax.fori_loop(1, place.count, one, 0)
    pl.semaphore_wait(barrier, place.count - 1)


def greet(place):
    barrier = pltpu.get_barrier_semaphore()
    for axis in AXES:
        for step in range(1, place.size[axis]):
            pl.semaphore_signal(
                barrier, inc=1, device_id=place.device(axis, place.after(axis, step)),
                device_id_type=MESH,
            )


def met(place):
    pl.semaphore_wait(pltpu.get_barrier_semaphore(), sum(n - 1 for n in place.size.values()))


def sems_needed(sizes, units, pairs):
    return units * (1 + sum(size - 1 for size in sizes.values())) + pairs


class Exchange:
    def __init__(self, place, sems, mine, whole):
        self.place, self.sems, self.mine, self.whole = place, sems, mine, whole

    def start(self):
        place = self.place
        at = place.at["y"]
        self.kept = self.sems.local(lambda: (self.mine.at[at], self.whole.at[at]))

        def ends(step):
            other = place.after("y", step)
            return self.mine.at[other], self.whole.at[at], place.device("y", other)

        self.sent = [
            (step, self.sems.copy(functools.partial(ends, step)))
            for step in range(1, place.size["y"])
        ]
        return self

    def finish(self):
        self.kept.wait()
        for step, slot in self.sent:
            index = self.place.before("y", step)
            self.sems.arrived(slot, self.whole.at[index], self.place.device("y", index))


def exchange(place, sems, mine, whole):
    return Exchange(place, sems, mine, whole).start().finish


START_ORDERS = (WIDE,)
FRONT_ORDERS = (EVEN,)
MLP_ORDERS = (EVEN,)
MLP_SUM_ORDERS = (EVEN,)
BACK_ORDERS = (EVEN,)
FINISH_ORDERS = (WIDE,)


def start_kernel(
    silu_ref, ada_ref, x_ref, qkv_ref, mod_ref, rows_ref, hot_ref, x_full, qkv_full, silu_s, share_s, terms_s, send, recv, share_send, share_recv,
):
    place = Place()
    sems = Sems(send, recv)
    count, me = place.count, place.me
    width = silu_ref.shape[1] - hot_ref.shape[1]
    rows_each = ada_ref.shape[0]
    greet_all(place)

    silu = Gather(place, sems, silu_ref, silu_s, "czxy")
    gathers = Gathers(place, sems, [(qkv_ref, qkv_full, span) for span in spans_of(qkv_ref.shape[0], 4)], START_ORDERS)
    silu.own()
    silu.start(0)
    gathers.advance(0)
    silu.wait(0)
    silu.start(1)
    silu.wait(1)
    silu.start(2)
    silu.wait(2)
    silu.start(3)
    gathers.advance(1)
    silu.wait(3)

    rows = silu_s[...].reshape(count, silu_ref.shape[1])
    hot = (
        rows[:, width:] == lax.broadcasted_iota(jnp.int32, (count, hot_ref.shape[1]), 1).astype(f32)
    ).astype(bf16)
    hot_ref[...] = hot.astype(f32)
    first = lax.axis_index("dp") * rows_each
    pick = (
        lax.broadcasted_iota(jnp.int32, (width, rows_each), 0)
        == first + lax.broadcasted_iota(jnp.int32, (width, rows_each), 1)
    ).astype(bf16)
    local = mm(rows[:, :width].astype(bf16), pick).astype(bf16)
    grouped = mm(hot[:, :count], local)
    rows_ref[...] = grouped
    share = mm(grouped.astype(bf16), ada_ref[...])
    share_s[...] = share.reshape(share_s.shape)

    def push(step):
        to = lax.rem(me + step, count)
        return pltpu.make_async_remote_copy(
            src_ref=share_s.at[to], dst_ref=terms_s.at[me],
            send_sem=share_send.at[step], recv_sem=share_recv.at[step],
            device_id=place.numbered(to), device_id_type=MESH,
        )

    def came(step):
        source = lax.rem(me + count - step, count)
        return pltpu.make_async_remote_copy(
            src_ref=terms_s.at[source], dst_ref=terms_s.at[source],
            send_sem=share_send.at[step], recv_sem=share_recv.at[step],
            device_id=place.numbered(source), device_id_type=MESH,
        )

    def do_push(step, carry):
        push(step).start()
        return carry

    lax.fori_loop(1, count, do_push, 0)
    terms_s[me] = share_s[me]

    def do_wait(step, carry):
        came(step).wait_recv()
        return carry

    def do_sent(step, carry):
        push(step).wait_send()
        return carry

    x_done = exchange(place, sems, x_ref, x_full)
    gathers.advance(2)
    lax.fori_loop(1, count, do_wait, 0)
    heads = place.size["y"]
    for y in range(heads):
        mod_ref[y] = lax.fori_loop(
            0, count // heads, lambda i, total: total + terms_s[i * heads + y],
            jnp.zeros(terms_s.shape[1:], f32),
        )
    for tick in range(3, gathers.ticks + 1):
        gathers.advance(tick)
    x_done()
    sems.drain()
    lax.fori_loop(1, count, do_sent, 0)


def start_call(silu, order_mine, ada, x, qkv):
    dp, head = lax.axis_size("dp"), lax.axis_size("head")
    count = dp * head
    lead = (4, 2, dp // 8, head)
    lanes = max(128, count)
    width = silu.shape[1]
    row = jnp.concatenate(
        [silu.astype(bf16).astype(f32), jnp.broadcast_to(order_mine.astype(f32), (1, lanes))], axis=1
    )
    sizes = {"z": 4, "x": 2, "c": dp // 8, "y": head}
    needed = sems_needed(sizes, 5, 2 * head)
    anywhere = pl.BlockSpec(memory_space=pl.ANY)
    vmem = pl.BlockSpec(memory_space=pltpu.VMEM)
    slot_shape = x.shape
    return pl.pallas_call(
        start_kernel,
        in_specs=[anywhere, vmem] + [anywhere] * 2,
        out_specs=[vmem] * 3 + [anywhere] * 2,
        out_shape=[
            jax.ShapeDtypeStruct((head, 1, ada.shape[1]), f32),
            jax.ShapeDtypeStruct((count, ada.shape[0]), f32),
            jax.ShapeDtypeStruct((count, lanes), f32),
            jax.ShapeDtypeStruct(slot_shape, bf16),
            jax.ShapeDtypeStruct(lead + qkv.shape, bf16),
        ],
        scratch_shapes=[
            pltpu.VMEM(lead + (1, width + lanes), f32),
            pltpu.VMEM((count, 1, ada.shape[1]), f32),
            pltpu.VMEM((count, 1, ada.shape[1]), f32),
            pltpu.SemaphoreType.DMA((needed,)),
            pltpu.SemaphoreType.DMA((needed,)),
            pltpu.SemaphoreType.DMA((count,)),
            pltpu.SemaphoreType.DMA((count,)),
        ],
        compiler_params=pltpu.CompilerParams(
            collective_id=0, has_side_effects=True, vmem_limit_bytes=VMEM_MOST
        ),
        name="gather_start",
    )(row, ada, x, qkv)


def front_kernel(
    tiles, ts, kind_ref, x_ref, mod_ref, w_ref, b_ref, out_p, up_p, down_p, cot_p,
    qkv_ref, norm_ref, o_ref, lse_ref, out_f, up_f, down_f, cot_f,
    qkv_s, norm_s, copied, send, recv,
):
    step = pl.program_id(0)
    groups, _, rows_each, width = w_ref.shape
    _, slots, size = qkv_s.shape
    heads = width // size
    parts = 3 * H // heads
    tm = slots // tiles
    first_head = parts * tiles
    last = first_head + H - 1

    place = Place()
    sems = Sems(send, recv)
    wanted = []
    for piece, full, count in ((up_p, up_f, 4), (down_p, down_f, 4), (out_p, out_f, 2)):
        wanted += [(piece, full, span) for span in spans_of(piece.shape[0], count)]
    gathers = Gathers(place, sems, wanted, FRONT_ORDERS)
    keep = pltpu.make_async_copy(qkv_s, qkv_ref, copied.at[0])
    keep_norm = pltpu.make_async_copy(norm_s, norm_ref, copied.at[1])
    cot_done = None
    for tick in range(gathers.ticks):
        at = min(FRONT_STEPS[tick], last)
        if tick == 0:
            @pl.when(step == 0)
            def _():
                greet(place)

            @pl.when(step == at)
            def _():
                met(place)
                gathers.advance(0)
        elif at < last:
            if tick == 1:
                cot_done = Exchange(place, sems, cot_p, cot_f)

            @pl.when(step == at)
            def _(tick=tick):
                gathers.advance(tick)
                if tick == 1:
                    cot_done.start()

    @pl.when(step < first_head)
    def _():
        rows = pl.ds(pl.multiple_of(lax.rem(step, tiles) * tm, tm), tm)
        part = lax.div(step, tiles)

        @pl.when(part == 0)
        def _():
            center, inv = center_spread(x_ref[...].astype(f32))
            norm_s[rows, :] = (
                center * inv * (1.0 + mod_ref[1:2, :]) + mod_ref[0:1, :]
            ).astype(bf16)

        weight = w_ref[...].reshape(groups * rows_each, width)
        out = (mm(norm_s[rows, :], weight) + b_ref[0]).astype(bf16)
        for j in range(heads):
            qkv_s[part * heads + j, rows, :] = out[:, j * size : (j + 1) * size]

    @pl.when(step == first_head)
    def _():
        keep.start()
        keep_norm.start()

    @pl.when(step >= first_head)
    def _():
        head = step - first_head
        kept = slots - slots // 16
        factor = log2_e * size ** (-0.5)
        full = kind_ref[0] == 0
        keys = qkv_s[H + head]
        values_t = qkv_s[2 * H + head].T
        for start in range(0, slots, ts):
            here = slice(start, start + ts)
            scores = masked(mm_nt(keys, qkv_s[head, here, :]), full, kept)
            peak = jnp.max(scores, axis=0, keepdims=True) * factor
            exponent = jnp.exp2(scores * factor - peak)
            total = jnp.sum(exponent, axis=0, keepdims=True)
            mix = mm(values_t, exponent.astype(bf16)) * (1.0 / total)
            o_ref[0, here, :] = mix.T.astype(bf16)
            lse_ref[0, :, here] = peak + jnp.log2(total)

    @pl.when(step == last)
    def _():
        for tick in range(gathers.ticks):
            if FRONT_STEPS[tick] >= last:
                gathers.advance(tick)
        gathers.advance(gathers.ticks)
        cot_done.finish()
        keep.wait()
        keep_norm.wait()
        sems.drain()


FRONT_STEPS = (1, 3, 6, 10, 14, 18, 21, 99)


def front_call(kind, x, mod, weight, bias, out, up, down, cot):
    slots, width = x.shape
    tiles = 2
    groups, parts, rows_each, part_width = weight.shape
    size = width // H
    sizes = sizes_of()
    lead = tuple(sizes[a] for a in AXES)
    needed = sems_needed(sizes, 10, 2 * sizes["y"])
    first_head = parts * tiles
    anywhere = pl.BlockSpec(memory_space=pl.ANY)

    def part(s):
        return jnp.minimum(lax.div(s, tiles), parts - 1)

    def head(s):
        return jnp.maximum(s - first_head, 0)

    return pl.pallas_call(
        functools.partial(front_kernel, tiles, min(256, slots)),
        grid=(first_head + H,),
        in_specs=[
            pl.BlockSpec(memory_space=pltpu.SMEM),
            pl.BlockSpec((slots // tiles, width), lambda s: (jnp.where(s < tiles, s, tiles - 1), 0)),
            whole_spec(mod.shape),
            pl.BlockSpec(
                (groups, 1, rows_each, part_width),
                lambda s: (0, lax.rem(part(s), 2) * 2 + lax.div(part(s), 2), 0, 0),
            ),
            pl.BlockSpec((1, 1, part_width), lambda s: (part(s), 0, 0)),
        ]
        + [anywhere] * 4,
        out_specs=[
            anywhere,
            anywhere,
            pl.BlockSpec((1, slots, size), lambda s: (head(s), 0, 0)),
            pl.BlockSpec((1, 1, slots), lambda s: (head(s), 0, 0)),
        ]
        + [anywhere] * 4,
        out_shape=[
            jax.ShapeDtypeStruct((3 * H, slots, size), bf16),
            jax.ShapeDtypeStruct((slots, width), bf16),
            jax.ShapeDtypeStruct((H, slots, size), bf16),
            jax.ShapeDtypeStruct((H, 1, slots), f32),
        ]
        + [jax.ShapeDtypeStruct(lead + piece.shape, bf16) for piece in (out, up, down)]
        + [jax.ShapeDtypeStruct(cot.shape, bf16)],
        scratch_shapes=[
            pltpu.VMEM((3 * H, slots, size), bf16),
            pltpu.VMEM((slots, width), bf16),
            pltpu.SemaphoreType.DMA((2,)),
            pltpu.SemaphoreType.DMA((needed,)),
            pltpu.SemaphoreType.DMA((needed,)),
        ],
        compiler_params=pltpu.CompilerParams(
            collective_id=3, has_side_effects=True, vmem_limit_bytes=VMEM_MOST
        ),
        name="front",
    )(kind, x, mod, weight, bias, out, up, down, cot)


class Scatter:
    def __init__(self, place, sems, grad, held, recvs, axes, rows=None):
        self.place, self.sems, self.grad, self.held, self.recvs, self.axes = (
            place, sems, grad, held, recvs, axes
        )
        self.rows = rows
        self.slots = {}

    @staticmethod
    def scratch(sizes, axes, rows, width):
        held = pltpu.VMEM(tuple(sizes[a] for a in "zxy") + (rows, width), bf16)
        recvs = []
        for at, axis in enumerate(axes):
            left = tuple(sizes[a] for a in "zxy" if a not in axes[: at + 1])
            recvs.append(pltpu.VMEM((sizes[axis] - 1,) + left + (rows, width), bf16))
        return [held] + recvs

    def wanted(self, of):
        spots = tuple(of if name == "c" else slice(None) for name in AXES)
        if self.rows is not None:
            spots = spots + (pl.ds(*self.rows), slice(None))
        return self.grad.at[spots]

    def share(self, stage, index):
        done = self.axes[1:stage]
        spots = []
        for name in "zxy":
            if name in done:
                spots.append(self.place.at[name])
            elif name == self.axes[stage]:
                spots.append(index)
            else:
                spots.append(slice(None))
        return self.held.at[tuple(spots)]

    def start(self, stage):
        axis = self.axes[stage]
        place = self.place
        if stage == 0:
            self.kept = self.sems.local(lambda: (self.wanted(place.at["c"]), self.held))

        def ends(step):
            index = place.after(axis, step)
            src = self.wanted(index) if stage == 0 else self.share(stage, index)
            return src, self.recvs[stage].at[step - 1], place.device(axis, index)

        for step in range(1, place.size[axis]):
            self.slots[stage, step] = self.sems.copy(functools.partial(ends, step))

    def arrive(self, stage):
        axis = self.axes[stage]
        place = self.place
        if stage == 0:
            self.kept.wait()
        for step in range(1, place.size[axis]):
            self.sems.arrived(
                self.slots[stage, step], self.recvs[stage].at[step - 1],
                place.device(axis, place.before(axis, step)),
            )

    def finish(self, stage):
        self.arrive(stage)
        place = self.place
        left = [a for a in "zxy" if a not in self.axes[: stage + 1]]
        recv = self.recvs[stage]

        def one(at, carry):
            spots = {}
            for a in reversed(left):
                spots[a] = lax.rem(at, place.size[a])
                at = lax.div(at, place.size[a])
            where = tuple(spots.get(a, place.at[a]) for a in "zxy")
            inner = tuple(spots[a] for a in left)
            total = self.held[where].astype(f32)
            for step in range(recv.shape[0]):
                total = total + recv[(step,) + inner].astype(f32)
            self.held[where] = total.astype(bf16)
            return carry

        lax.fori_loop(0, math.prod(place.size[a] for a in left), one, 0)

    def result(self, stage):
        self.arrive(stage)
        place = self.place
        recv = self.recvs[stage]
        total = self.held[tuple(place.at[a] for a in "zxy")].astype(f32)
        for step in range(recv.shape[0]):
            total = total + recv[step].astype(f32)
        return total


def sum_axes(orders, at):
    return orders[at // 2 % len(orders)][at % 2][::-1]


def sum_scratch(sizes, grads, orders):
    scratch, number = [], 0
    for rows, width, whole, count in grads:
        near = sizes["c"]
        scratch.append(
            pltpu.VMEM((rows, width) if whole else (near, rows // near, width), f32)
        )
        for span in spans_of(rows, count):
            scratch += Scatter.scratch(sizes, sum_axes(orders, number), span[1], width)
            number += 1
    return scratch


class Sums:
    def __init__(self, place, sems, grads, finals, scratch, orders):
        self.place, self.sems, self.finals = place, sems, finals
        scratch = list(scratch)
        self.totals, self.pairs = [], []
        at = -1
        for which, (grad, count) in enumerate(grads):
            self.totals.append(scratch.pop(0))
            for span in spans_of(grad.shape[4], count):
                at += 1
                axes = sum_axes(orders, at)
                held, recvs, scratch = scratch[0], scratch[1:5], scratch[5:]
                unit = Scatter(place, sems, grad, held, recvs, axes, span)
                if at % 2 == 0:
                    self.pairs.append([])
                self.pairs[-1].append((unit, span, which))
        self.ticks = len(self.pairs) + 3

    def advance(self, tick):
        if tick < len(self.pairs):
            for unit, *_ in self.pairs[tick]:
                unit.start(0)
        for stage in (0, 2, 1, 3):
            if 0 <= tick - 1 - stage < len(self.pairs):
                for unit, span, which in self.pairs[tick - 1 - stage]:
                    if stage == 3:
                        self.settle(which, unit, span)
                    else:
                        unit.finish(stage)
                        unit.start(stage + 1)

    def settle(self, at, unit, span):
        value = unit.result(3)
        first, size = span
        total = self.totals[at]
        if len(total.shape) == 2:
            total[first : first + size, :] = value
            return
        each = total.shape[1]
        for to in range(total.shape[0]):
            low, high = max(first, to * each), min(first + size, (to + 1) * each)
            if low < high:
                total[to, low - to * each : high - to * each, :] = value[
                    low - first : high - first, :
                ]

    def deliver(self):
        place = self.place
        mine = place.at["c"]
        self.kept, self.flights = [], []
        def ends(total, final, step):
            to = place.after("c", step)
            return total.at[to], final.at[mine], place.device("c", to)

        for total, final in zip(self.totals, self.finals):
            if len(total.shape) == 2:
                self.kept.append(self.sems.local(lambda t=total, f=final: (t, f)))
                continue
            self.kept.append(self.sems.local(lambda t=total, f=final: (t.at[mine], f.at[mine])))
            for step in range(1, place.size["c"]):
                slot = self.sems.copy(functools.partial(ends, total, final, step))
                self.flights.append((final, step, slot))

    def delivered(self):
        for made in self.kept:
            made.wait()
        for final, step, slot in self.flights:
            source = self.place.before("c", step)
            self.sems.arrived(slot, final.at[source], self.place.device("c", source))


def sizes_of():
    dp, head = lax.axis_size("dp"), lax.axis_size("head")
    return {"z": 4, "x": 2, "c": dp // 8, "y": head}


def final_shape(grad, near):
    return jax.ShapeDtypeStruct((near, grad.shape[4] // near, grad.shape[5]), f32)


def finish_kernel(
    row_ref, ada_ref, rows_ref, hot_ref, gin_ref, qkv_ref,
    bias_ref, dada_ref, gsilu_ref, gin_full, dqkv_ref,
    send, recv, share_send, share_recv, row_s, share_s, *scratch,
):
    place = Place()
    count, me = place.count, place.me
    sems = Sems(send, recv)
    sums = Sums(
        place, sems, [(qkv_ref, FINISH_SPANS)], (dqkv_ref,), scratch, FINISH_ORDERS
    )
    greet_all(place)
    rows = Gather(place, sems, row_ref, row_s, "zxyc")
    rows.own()
    rows.start(0)
    gin_done = exchange(place, sems, gin_ref, gin_full)
    sums.advance(0)
    for tick in range(1, sums.ticks + 1):
        sums.advance(tick)
        if tick < 5:
            rows.wait(tick - 1)
            if tick < 4:
                rows.start(tick)
    sums.deliver()

    whole = row_s[...].reshape(count, row_ref.shape[1])
    bias_ref[...] = jnp.sum(whole, axis=0, keepdims=True)
    cols = ada_ref.shape[1]
    low = jnp.zeros((count, cols), f32)
    for y in range(place.size["y"]):
        low = jnp.where(place.at["y"] == y, whole[:, y * cols : (y + 1) * cols], low)
    low = low.astype(bf16)
    dada_ref[...] = lax.dot_general(
        rows_ref[...].astype(bf16), low, (((0,), (0,)), ((), ())), preferred_element_type=f32
    )
    grad = mm_nt(low, ada_ref[...])
    hot = hot_ref[...][:, :count]
    placed = lax.dot_general(
        hot, grad, (((0,), (0,)), ((), ())), precision=lax.Precision.HIGHEST,
        preferred_element_type=f32,
    )
    pad = share_s.shape[2] - placed.shape[1]
    placed = jnp.concatenate([placed, jnp.zeros((count, pad), f32)], axis=1)
    share_s[...] = placed.reshape(share_s.shape)

    def push(step):
        to = lax.rem(me + step, count)
        return pltpu.make_async_remote_copy(
            src_ref=share_s.at[to], dst_ref=gsilu_ref.at[me],
            send_sem=share_send.at[step], recv_sem=share_recv.at[step],
            device_id=place.numbered(to), device_id_type=MESH,
        )

    def came(step):
        source = lax.rem(me + count - step, count)
        return pltpu.make_async_remote_copy(
            src_ref=gsilu_ref.at[source], dst_ref=gsilu_ref.at[source],
            send_sem=share_send.at[step], recv_sem=share_recv.at[step],
            device_id=place.numbered(source), device_id_type=MESH,
        )

    def do_push(step, carry):
        push(step).start()
        return carry

    def do_wait(step, carry):
        came(step).wait_recv()
        push(step).wait_send()
        return carry

    lax.fori_loop(1, count, do_push, 0)
    gsilu_ref[me] = share_s[me]
    lax.fori_loop(1, count, do_wait, 0)
    sums.delivered()
    gin_done()
    sems.drain()


FINISH_SPANS = 4


def finish_call(row, ada, silu_rows, hot, gin, qkv):
    sizes = sizes_of()
    near = sizes["c"]
    count = 8 * near * sizes["y"]
    anywhere = pl.BlockSpec(memory_space=pl.ANY)
    vmem = pl.BlockSpec(memory_space=pltpu.VMEM)
    needed = sems_needed(sizes, 2 + FINISH_SPANS, 2 * sizes["y"] + 4 * near)
    return pl.pallas_call(
        finish_kernel,
        in_specs=[anywhere, vmem, vmem, vmem] + [anywhere] * 2,
        out_specs=[vmem] * 3 + [anywhere] * 2,
        out_shape=[
            jax.ShapeDtypeStruct(row.shape, f32),
            jax.ShapeDtypeStruct(ada.shape, f32),
            jax.ShapeDtypeStruct((count, 1, 128), f32),
            jax.ShapeDtypeStruct(gin.shape, bf16),
            final_shape(qkv, near),
        ],
        scratch_shapes=[
            pltpu.SemaphoreType.DMA((needed,)),
            pltpu.SemaphoreType.DMA((needed,)),
            pltpu.SemaphoreType.DMA((count,)),
            pltpu.SemaphoreType.DMA((count,)),
            pltpu.VMEM((4, 2, near, sizes["y"], 1, row.shape[1]), f32),
            pltpu.VMEM((count, 1, 128), f32),
        ]
        + sum_scratch(
            sizes,
            [qkv.shape[4:] + (False, FINISH_SPANS)],
            FINISH_ORDERS,
        ),
        compiler_params=pltpu.CompilerParams(
            collective_id=1, has_side_effects=True, vmem_limit_bytes=VMEM_MOST
        ),
        name="sum_finish",
    )(row, ada, silu_rows, hot, gin, qkv)


BACK_SPANS = (4, 4, 2)
BACK_STEPS = (1, 2, 4, 7, 10, 13, 99, 99)


def attn_back_kernel(
    ts, kind_ref, q_ref, k_ref, v_ref, g_ref, lse_ref, act_p, up_p, down_p, out_p,
    out_ref, act_f, dup_ref, ddown_ref, dout_ref, dk_s, dv_s, send, recv, *scratch,
):
    step = pl.program_id(0)
    last = pl.num_programs(0) - 1
    place = Place()
    sems = Sems(send, recv)
    sums = Sums(
        place, sems, list(zip((up_p, down_p, out_p), BACK_SPANS)), (dup_ref, ddown_ref, dout_ref),
        scratch, BACK_ORDERS,
    )
    act_move = Exchange(place, sems, act_p, act_f)

    @pl.when(step == 0)
    def _():
        greet(place)

    for tick in range(sums.ticks):
        if BACK_STEPS[tick] < H - 1:
            @pl.when(step == BACK_STEPS[tick])
            def _(tick=tick):
                if tick == 0:
                    met(place)
                sums.advance(tick)
                if tick == 2:
                    act_move.start()

    slots, size = q_ref.shape[1:]
    kept = slots - slots // 16
    scale = size ** (-0.5)
    factor = log2_e * scale
    full = kind_ref[0] == 0
    keys = k_ref[0]
    keys_t = keys.T
    values = v_ref[0]
    for start in range(0, slots, ts):
        here = slice(start, start + ts)
        queries = q_ref[0, here, :]
        grad = g_ref[0, here, :]
        scores = masked(mm_nt(keys, queries), full, kept)
        probs = jnp.exp2(scores * factor - lse_ref[0, :, here])
        weighted = probs * mm_nt(values, grad)
        inner = jnp.sum(weighted, axis=0, keepdims=True)
        grad_scores = (weighted - probs * inner).astype(bf16)
        add_v = mm(probs.astype(bf16), grad)
        add_k = mm(grad_scores, queries)
        if start == 0:
            dv_s[...] = add_v
            dk_s[...] = add_k
        else:
            dv_s[...] += add_v
            dk_s[...] += add_k
        out_ref[0, 0, here, :] = (mm(keys_t, grad_scores) * scale).T.astype(bf16)
    out_ref[1, 0] = (dk_s[...] * scale).astype(bf16)
    out_ref[2, 0] = dv_s[...].astype(bf16)

    @pl.when(step == last)
    def _():
        for tick in range(sums.ticks):
            if BACK_STEPS[tick] >= H - 1:
                sums.advance(tick)
        sums.advance(sums.ticks)
        sums.deliver()
        sums.delivered()
        act_move.finish()
        sems.drain()


def attn_back_call(kind, qkv, grad, lse, act, up, down, out):
    _, slots, size = qkv.shape
    ts = min(256, slots)
    block = (1, slots, size)
    sizes = sizes_of()
    anywhere = pl.BlockSpec(memory_space=pl.ANY)
    needed = sems_needed(sizes, sum(BACK_SPANS), 2 * sizes["y"] + 4 * sizes["c"])
    return pl.pallas_call(
        functools.partial(attn_back_kernel, ts),
        grid=(H,),
        in_specs=[
            pl.BlockSpec(memory_space=pltpu.SMEM),
            pl.BlockSpec(block, lambda h: (h, 0, 0)),
            pl.BlockSpec(block, lambda h: (h + H, 0, 0)),
            pl.BlockSpec(block, lambda h: (h + 2 * H, 0, 0)),
            pl.BlockSpec(block, lambda h: (h, 0, 0)),
            pl.BlockSpec((1, 1, slots), lambda h: (h, 0, 0)),
        ]
        + [anywhere] * 4,
        out_specs=[pl.BlockSpec((3, 1, slots, size), lambda h: (0, h, 0, 0))] + [anywhere] * 4,
        out_shape=[
            jax.ShapeDtypeStruct((3, H, slots, size), bf16),
            jax.ShapeDtypeStruct(act.shape, bf16),
            final_shape(up, sizes["c"]),
            jax.ShapeDtypeStruct(down.shape[4:], f32),
            final_shape(out, sizes["c"]),
        ],
        scratch_shapes=[
            pltpu.VMEM((slots, size), f32),
            pltpu.VMEM((slots, size), f32),
            pltpu.SemaphoreType.DMA((needed,)),
            pltpu.SemaphoreType.DMA((needed,)),
        ]
        + sum_scratch(
            sizes,
            [
                grad.shape[4:] + (at == 1, count)
                for at, (grad, count) in enumerate(zip((up, down, out), BACK_SPANS))
            ],
            BACK_ORDERS,
        ),
        compiler_params=pltpu.CompilerParams(
            collective_id=2, has_side_effects=True, vmem_limit_bytes=VMEM_MOST
        ),
        name="attention_backward",
    )(kind, qkv, qkv, qkv, grad, lse, act, up, down, out)


MLP_SPANS = 4
MLP_GATHER = (1, 2, 3, 5, 7, 9, 11)
MLP_SUM = (12, 13, 15, 17, 19, 21, 22)


def mlp_kernel(
    tiles, second_ref, gm_ref, up0_f, down0_f, up1_p, down1_p, b_ref,
    mlp_ref, gsec_ref, bias_ref, up1_f, down1_f, dup0_ref, ddown0_ref, dup1_ref, ddown1_ref,
    sup_ref, sdown_ref,
    sec_t, act_t, gh_s, up_s, down_s, raw_up, raw_down, loaded, stored,
    send, recv, *scratch,
):
    step = pl.program_id(0)
    subs = tiles + 2
    last = 4 * subs - 1
    tile_at = lax.div(step, subs)
    sub = lax.rem(step, subs)
    slots, width = second_ref.shape
    hidden = up_s.shape[1]
    tm = slots // tiles

    place = Place()
    sems = Sems(send, recv)
    near, head_half = place.size["c"], place.size["y"] // 2

    def loads(tile):
        half = tile % 2
        up, down = ((up0_f, down0_f), (up1_f, down1_f))[tile // 2]
        return (
            pltpu.make_async_copy(
                up.at[:, :, :, pl.ds(half * head_half, head_half)], raw_up, loaded.at[0]
            ),
            pltpu.make_async_copy(down.at[pl.ds(2 * half, 2)], raw_down, loaded.at[1]),
        )

    def stores(tile):
        half = tile % 2
        up, down = ((dup0_ref, ddown0_ref), (dup1_ref, ddown1_ref))[tile // 2]
        return (
            pltpu.make_async_copy(
                raw_up, up.at[:, :, :, pl.ds(half * head_half, head_half)], stored.at[0]
            ),
            pltpu.make_async_copy(raw_down, down.at[pl.ds(2 * half, 2)], stored.at[1]),
        )

    wanted = []
    for piece, full in ((up1_p, up1_f), (down1_p, down1_f)):
        wanted += [(piece, full, span) for span in spans_of(piece.shape[0], MLP_SPANS)]
    gathers = Gathers(place, sems, wanted, MLP_ORDERS)
    sums = Sums(
        place, sems, [(dup0_ref, MLP_SPANS), (ddown0_ref, MLP_SPANS)], (sup_ref, sdown_ref), scratch,
        MLP_SUM_ORDERS,
    )

    @pl.when(step == 0)
    def _():
        greet(place)

    for tick in range(gathers.ticks):
        @pl.when(step == MLP_GATHER[tick])
        def _(tick=tick):
            if tick == 0:
                met(place)
            gathers.advance(tick)

    @pl.when(step == 2 * subs)
    def _():
        gathers.advance(gathers.ticks)

    @pl.when(step == 0)
    def _():
        sec_t[...] = second_ref[...].T
        mlp_ref[...] = jnp.zeros_like(mlp_ref)
        gsec_ref[...] = jnp.zeros_like(gsec_ref)
        for made in loads(0):
            made.start()

    for tile in range(4):
        @pl.when(step == tile * subs)
        def _(tile=tile):
            if tile > 0:
                stores(tile - 1)[1].wait()
                loads(tile)[1].start()
            if tile == 2:
                loads(tile)[0].start()
            for made in loads(tile):
                made.wait()

    @pl.when(sub == 0)
    def _():
        share = raw_up.shape[5]
        for y in range(raw_up.shape[3]):
            for c in range(near):
                off = (y * near + c) * share
                up_s[:, off : off + share] = raw_up[:, :, c, y].reshape(width, share)
        chunk, share = raw_down.shape[4:]
        for at in range(4 * near):
            for y in range(raw_down.shape[3]):
                down_s[at * chunk : (at + 1) * chunk, y * share : (y + 1) * share] = raw_down[
                    at // (2 * near), (at // near) % 2, at % near, y
                ]
        bias_ref[...] = jnp.zeros_like(bias_ref)

    for tick in range(sums.ticks):
        if MLP_SUM[tick] < last:
            @pl.when(step == MLP_SUM[tick])
            def _(tick=tick):
                sums.advance(tick)

    @pl.when(sub < tiles)
    def _():
        rows = pl.ds(pl.multiple_of(sub * tm, tm), tm)
        pre = mm(second_ref[rows, :], up_s[...]) + b_ref[0]
        square = pre * pre
        tanh = jnp.tanh(gelu_in * (pre + gelu_cube * pre * square))
        act = (0.5 * pre * (1.0 + tanh)).astype(bf16)
        slope = 0.5 * (1.0 + tanh) + 0.5 * pre * (1.0 - tanh * tanh) * (
            gelu_in * (1.0 + 3.0 * gelu_cube * square)
        )
        grad = mm_nt(gm_ref[rows, :], down_s[...]) * slope
        bias_ref[0] += jnp.sum(grad, axis=0, keepdims=True)
        grad_low = grad.astype(bf16)
        gh_s[rows, :] = grad_low
        act_t[:, rows] = act.T
        mlp_ref[rows, :] += mm(act, down_s[...])
        gsec_ref[rows, :] += mm_nt(grad_low, up_s[...])

    @pl.when(sub == tiles)
    def _():
        share = raw_up.shape[5]
        half = width // 2
        for j in range(2):
            grad = mm(sec_t[j * half : (j + 1) * half, :], gh_s[...]).astype(bf16)
            for y in range(raw_up.shape[3]):
                for c in range(near):
                    off = (y * near + c) * share
                    raw_up[2 * j : 2 * j + 2, :, c, y] = grad[:, off : off + share].reshape(
                        2, 2, half // 4, share
                    )

    @pl.when(sub == tiles + 1)
    def _():
        chunk, share = raw_down.shape[4:]
        half = hidden // 2
        for j in range(2):
            grad = mm(act_t[j * half : (j + 1) * half, :], gm_ref[...]).astype(bf16)
            for at in range(2 * near):
                for y in range(raw_down.shape[3]):
                    raw_down[j, at // near, at % near, y] = grad[
                        at * chunk : (at + 1) * chunk, y * share : (y + 1) * share
                    ]

    for tile in range(4):
        @pl.when(step == tile * subs + tiles)
        def _(tile=tile):
            stores(tile)[0].start()

        @pl.when(step == tile * subs + tiles + 1)
        def _(tile=tile):
            stores(tile)[0].wait()
            if tile in (0, 2):
                loads(tile + 1)[0].start()
            stores(tile)[1].start()

    @pl.when(step == last)
    def _():
        stores(3)[1].wait()
        for tick in range(sums.ticks):
            if MLP_SUM[tick] >= last:
                sums.advance(tick)
        sums.advance(sums.ticks)
        sums.deliver()
        sums.delivered()
        sems.drain()


def mlp_call(second, gm, up0, down0, up1, down1, bias):
    slots, width = second.shape
    tiles = 4
    subs = tiles + 2
    sizes = sizes_of()
    near, head = sizes["c"], sizes["y"]
    lead = tuple(sizes[a] for a in AXES)
    rows_up, share_up = up1.shape
    rows_down, share_down = down1.shape
    hidden = share_up * near * head // 2
    anywhere = pl.BlockSpec(memory_space=pl.ANY)
    needed = sems_needed(sizes, 4 * MLP_SPANS, 4 * near)
    bias_spec = pl.BlockSpec((1, 1, hidden), lambda s: (lax.div(s, subs), 0, 0))
    full_up = jax.ShapeDtypeStruct(lead + up1.shape, bf16)
    full_down = jax.ShapeDtypeStruct(lead + down1.shape, bf16)
    return pl.pallas_call(
        functools.partial(mlp_kernel, tiles),
        grid=(4 * subs,),
        in_specs=[once_spec((slots, width)), once_spec((slots, width))]
        + [anywhere] * 4
        + [bias_spec],
        out_specs=[once_spec((slots, width)), once_spec((slots, width)), bias_spec] + [anywhere] * 8,
        out_shape=[
            jax.ShapeDtypeStruct((slots, width), f32),
            jax.ShapeDtypeStruct((slots, width), f32),
            jax.ShapeDtypeStruct(bias.shape, f32),
            full_up, full_down, full_up, full_down, full_up, full_down,
            final_shape(full_up, near),
            jax.ShapeDtypeStruct(down1.shape, f32),
        ],
        scratch_shapes=[
            pltpu.VMEM((width, slots), bf16),
            pltpu.VMEM((hidden, slots), bf16),
            pltpu.VMEM((slots, hidden), bf16),
            pltpu.VMEM((width, hidden), bf16),
            pltpu.VMEM((hidden, width), bf16),
            pltpu.VMEM((4, 2, near, head // 2) + up1.shape, bf16),
            pltpu.VMEM((2, 2, near, head) + down1.shape, bf16),
            pltpu.SemaphoreType.DMA((2,)),
            pltpu.SemaphoreType.DMA((2,)),
            pltpu.SemaphoreType.DMA((needed,)),
            pltpu.SemaphoreType.DMA((needed,)),
        ]
        + sum_scratch(
            sizes, (up1.shape + (False, MLP_SPANS), down1.shape + (True, MLP_SPANS)), MLP_SUM_ORDERS
        ),
        compiler_params=pltpu.CompilerParams(
            collective_id=4, has_side_effects=True, vmem_limit_bytes=MLP_VMEM
        ),
        name="feed_forward_both_ways",
    )(second, gm, up0, down0, up1, down1, bias)


MLP_VMEM = 63 * 1024 * 1024


def qkv_back_kernel(
    tm, g_ref, norm_ref, w_ref, x_ref, gmid_ref, mod_ref,
    gin_ref, dw_ref, bias_ref, sums_ref, norm_t, gp_s, gn_s,
):
    part = pl.program_id(0)
    slots, width = x_ref.shape
    tiles = slots // tm
    groups, _, rows_each, part_width = w_ref.shape
    heads = g_ref.shape[0]

    @pl.when(part == 0)
    def _():
        norm_t[...] = norm_ref[...].T
        gn_s[...] = jnp.zeros_like(gn_s)

    def tile(i, total):
        rows = pl.ds(pl.multiple_of(i * tm, tm), tm)
        grad = jnp.concatenate([g_ref[j, rows, :] for j in range(heads)], axis=1)
        gp_s[rows, :] = grad
        gn_s[rows, :] += mm_nt(grad, w_ref[...].reshape(width, part_width))
        return total + jnp.sum(grad.astype(f32), axis=0, keepdims=True)

    bias_ref[0] = lax.fori_loop(0, tiles, tile, jnp.zeros((1, part_width), f32))
    per = groups // 2
    for j in range(2):
        dw_ref[per * j : per * (j + 1), 0] = (
            mm(norm_t[per * j * rows_each : per * (j + 1) * rows_each, :], gp_s[...])
            .astype(bf16)
            .reshape(per, rows_each, part_width)
        )

    @pl.when(part == pl.num_programs(0) - 1)
    def _():
        def finish(i, sums):
            rows = pl.ds(pl.multiple_of(i * tm, tm), tm)
            center, inv = center_spread(x_ref[rows, :].astype(f32))
            unit = center * inv
            grad = gn_s[rows, :]
            gin_ref[rows, :] = (
                gmid_ref[rows, :] + norm_back(grad * (1.0 + mod_ref[1:2, :]), unit, inv)
            ).astype(gin_ref.dtype)
            return (
                sums[0] + jnp.sum(grad, axis=0, keepdims=True),
                sums[1] + jnp.sum(grad * unit, axis=0, keepdims=True),
            )

        zero = jnp.zeros((1, width), f32)
        shift, scale = lax.fori_loop(0, tiles, finish, (zero, zero))
        sums_ref[...] = jnp.zeros_like(sums_ref)
        sums_ref[0:1, :] = shift
        sums_ref[1:2, :] = scale


def qkv_back_call(grad, norm, weight, x, gmid, mod):
    slots, width = x.shape
    tm = min(256, slots)
    size = width // H
    groups, parts, rows_each, part_width = weight.shape
    heads = part_width // size
    w_spec = pl.BlockSpec((groups, 1, rows_each, part_width), lambda p: (0, place(p), 0, 0))
    return pl.pallas_call(
        functools.partial(qkv_back_kernel, tm),
        grid=(parts,),
        in_specs=[
            pl.BlockSpec((heads, slots, size), lambda p: (p, 0, 0)),
            once_spec((slots, width)),
            w_spec,
            once_spec((slots, width)),
            once_spec((slots, width)),
            whole_spec(mod.shape),
        ],
        out_specs=[
            once_spec((slots, width)),
            w_spec,
            pl.BlockSpec((1, 1, part_width), lambda p: (p, 0, 0)),
            whole_spec((8, width)),
        ],
        out_shape=[
            jax.ShapeDtypeStruct((slots, width), bf16),
            jax.ShapeDtypeStruct(weight.shape, bf16),
            jax.ShapeDtypeStruct((parts, 1, part_width), f32),
            jax.ShapeDtypeStruct((8, width), f32),
        ],
        scratch_shapes=[
            pltpu.VMEM((width, slots), bf16),
            pltpu.VMEM((slots, part_width), bf16),
            pltpu.VMEM((slots, width), f32),
        ],
        compiler_params=params(),
        name="qkv_backward",
    )(grad, norm, weight, x, gmid, mod)


class Wire:
    def __init__(self, width):
        self.dp = lax.axis_size("dp")
        self.head = lax.axis_size("head")
        self.near = self.dp // (width // 144)
        self.width = width
        self.groups = [
            list(range(first, first + self.near)) for first in range(0, self.dp, self.near)
        ]

    def piece(self, weight):
        return lax.all_to_all(
            weight.astype(bf16), "dp", split_axis=1, concat_axis=0,
            axis_index_groups=self.groups, tiled=True,
        )

    def columns(self, stack):
        devices, rows, cols = stack.shape
        stack = stack.reshape(self.dp // self.near, self.near, self.head, rows, cols)
        if (self.near, self.head) != (2, 2):
            quarter = self.near * self.head * cols // 4
            stack = stack.transpose(0, 3, 2, 1, 4).reshape(-1, rows, 2, 2, quarter)
            stack = stack.transpose(0, 3, 2, 1, 4)
            return stack.reshape(-1, 4, rows, quarter)
        return stack.reshape(-1, 4, rows, cols)

    def uncolumns(self, stack):
        groups, _, rows, quarter = stack.shape
        cols = 4 * quarter // (self.near * self.head)
        if (self.near, self.head) != (2, 2):
            stack = stack.reshape(groups, 2, 2, rows, quarter).transpose(0, 3, 2, 1, 4)
            stack = stack.reshape(groups, rows, self.head, self.near, cols)
            stack = stack.transpose(0, 3, 2, 1, 4)
        return stack.reshape(self.dp * self.head, rows, cols)


def body(
    inputs, cond, order, grid_kind, weight_ada, bias_ada, weight_qkv, bias_query, bias_value,
    weight_out, bias_out, weight_up, bias_up, weight_down, bias_down, cotangent,
):
    images, slot_local, width = inputs.shape
    head_count = lax.axis_size("head")
    dp_count = lax.axis_size("dp")
    head_at = lax.axis_index("head")
    dp_at = lax.axis_index("dp")
    assert images == head_count
    wire = Wire(width)

    def from_image(array):
        return lax.all_to_all(
            array[None], "head", split_axis=1, concat_axis=0, tiled=True
        ).astype(f32)

    rows_ada, cols_ada = weight_ada.shape
    ada_low = weight_ada.astype(bf16)
    silu_own, silu_pull = jax.vjp(lambda v: v * jax.nn.sigmoid(v), cond)
    order_mine = lax.dynamic_slice_in_dim(order, head_at, 1, 0)
    kind = lax.dynamic_slice_in_dim(grid_kind, head_at, 1, 0)
    mod, silu_grouped, hot, x, qkv_full = start_call(
        silu_own, order_mine, ada_low, inputs.astype(bf16), wire.piece(weight_qkv)
    )
    x = x.reshape(-1, width)
    device_stack = lambda full: full.reshape((-1,) + full.shape[4:])
    qkv_full = wire.columns(device_stack(qkv_full))
    mod_flat = mod.reshape(6, width) + bias_ada.reshape(6, width)
    mod = jnp.concatenate([mod_flat, jnp.zeros((2, width), f32)], axis=0)

    bias_qkv = jnp.concatenate([bias_query, jnp.zeros_like(bias_query), bias_value])
    chunk = weight_down.shape[0] // 2
    up_phases = weight_up.astype(bf16).reshape(rows_ada, -1, 2, chunk)
    up0, up1 = (wire.piece(up_phases[:, :, at].reshape(rows_ada, -1)) for at in range(2))
    down0, down1 = (weight_down[at * chunk : (at + 1) * chunk].astype(bf16) for at in range(2))
    bias_phases = bias_up.reshape(-1, 2, chunk).swapaxes(0, 1).reshape(4, 1, -1)
    qkv, norm, mix, lse, out_full, up_full, down_full, cot = front_call(
        kind, x, mod, qkv_full, bias_qkv.reshape(4, 1, -1),
        wire.piece(weight_out), up0, down0, cotangent.astype(bf16),
    )
    cot = cot.reshape(-1, width)
    out_full = wire.columns(device_stack(out_full))
    attended, branch, second, gm = out_call(mix, x, cot, mod, out_full, bias_out)
    mlp, gsec, d_bias_up, _, _, _, _, d_up1, d_down1, d_up0, d_down0 = mlp_call(
        second, gm, up_full, down_full, up1, down1, bias_phases
    )
    d_bias_up = d_bias_up.reshape(2, -1, chunk).swapaxes(0, 1)
    act, gmid, gatt, d_out, sums = mid_back_call(
        x, branch, mlp, gsec, cot, attended, mod, out_full, bias_down
    )
    lead = (4, 2, dp_count // 8, head_count)
    stack = lambda grad: grad.reshape(lead + grad.shape[1:])
    by_image = lambda array: array.reshape(head_count, slot_local, width)
    grad, act, d_up1, d_down1, d_out = attn_back_call(
        kind, qkv, gatt, lse, by_image(act), d_up1, d_down1, stack(wire.uncolumns(d_out))
    )
    gin, d_qkv, d_bias_qkv, sums_in = qkv_back_call(
        grad.reshape(qkv.shape), norm, qkv_full, x, gmid, mod
    )

    bias_qkv_sum = d_bias_qkv.reshape(3, width)
    row = jnp.concatenate(
        [sums_in[0], sums_in[1], sums[0], sums[1], sums[2], sums[3],
         bias_qkv_sum[0], bias_qkv_sum[2], sums[4], sums[5], d_bias_up.reshape(-1)]
    ).reshape(1, -1)
    biases, d_ada, g_silu, gin, d_qkv = finish_call(
        row, ada_low, silu_grouped, hot, by_image(gin), stack(wire.uncolumns(d_qkv))
    )
    biases = biases[0]
    g_silu = g_silu.reshape(dp_count, head_count, 128)[:, :, :rows_ada].sum(axis=1)
    d_cond = silu_pull(g_silu.reshape(1, width))[0]
    side = lambda grad: grad.transpose(1, 0, 2).reshape(grad.shape[1], -1)
    d_up = jnp.stack(
        [side(part).reshape(rows_ada, -1, chunk) for part in (d_up0, d_up1)], axis=2
    ).reshape(rows_ada, -1)
    d_down = jnp.concatenate([d_down0, d_down1], axis=0)
    mods = 6 * width
    return (
        act.astype(f32),
        gin.astype(f32),
        d_cond,
        d_ada,
        side(d_qkv),
        side(d_out),
        d_up,
        d_down,
        biases[:mods],
        biases[mods : mods + width],
        biases[mods + width : mods + 2 * width],
        biases[mods + 2 * width : mods + 3 * width],
        biases[mods + 4 * width :],
        biases[mods + 3 * width : mods + 4 * width],
    )


def solution(mesh):
    in_specs = (
        P("dp", "head", None), P(("dp", "head"), None), P("dp"), P("dp"), P("dp", "head"), P(),
        P("dp", "head"), P(), P(), P("dp", "head"), P(), P("dp", "head"), P(), P("dp", "head"),
        P(), P("dp", "head", None),
    )
    out_specs = (
        P("dp", "head", None), P("dp", "head", None), P(("dp", "head"), None), P("dp", "head"),
        P("dp", "head"), P("dp", "head"), P("dp", "head"), P("dp", "head"),
        P(), P(), P(), P(), P(), P(),
    )
    return jax.shard_map(body, mesh=mesh, in_specs=in_specs, out_specs=out_specs, check_vma=False)
```

time: 1720 us -> 737 us (0.43)
  Pallas kernels: 0 us -> 661 us
  waiting for transfers between devices: 502 us -> 0.01 us
  matrix products: 435 us -> 0 us
  blocking collectives: 336 us -> 4.51 us
  local copies, waits for them, and re-layouts: 254 us -> 27.1 us
  other arithmetic: 147 us -> 24.5 us
    pallas_call x0 -> x8, Pallas kernels: none -> 661 us  [the longest x1 172 us: mlp_call(): pl.pallas_call(functools.partial(mlp_kernel, tiles), grid=(4 * subs,), in...]
    dot_general x28 -> x0, matrix products: 435 us -> none  [the longest x4 64.1 us: masked_scores(): jnp.einsum('bshd,bthd->bhst', queries, keys_in, preferred_element_type=jn...]
    unnamed x23 -> x0, waiting for transfers between devices: 234 us -> none
    all_gather x6 -> x0, blocking collectives: 191 us -> none  [the longest x1 86.7 us: fetch_weights(): lax.all_gather(weight_down.astype(jnp.bfloat16), 'head', axis=1, tiled=True)]
    reduce_scatter x4 -> x0, waiting for transfers between devices: 146 us -> none  [the longest x1 130 us: body(): lax.psum_scatter(grad_weight_ada.astype(jnp.bfloat16), 'dp', scatter_dime...]
    all_to_all x1, blocking collectives: 97 us -> 4.51 us  [piece(): lax.all_to_all(weight.astype(bf16), 'dp', split_axis=1, concat_axis=0, ax...]
    all_to_all x7 -> x8, local copies, waits for them, and re-layouts: 87.9 us -> 3.54 us  [piece(): lax.all_to_all(weight.astype(bf16), 'dp', split_axis=1, concat_axis=0, ax...]
    reshape x7 -> x17, local copies, waits for them, and re-layouts: 92.9 us -> 9.15 us  [the longest x1 2.33 us: body(): d_up = jnp.stack([side(part).reshape(rows_ada, -1, chunk) for part in (d_...]
  transfers between devices with their start and end apart: 19 -> 3, of which waited for: 12 -> 0; matrix products, arithmetic and copies ran while one was open for 43% -> 3% of each run, Pallas kernels for 0% -> 30%
where the time goes in v2:
time: 737 us; the launch traced here: 730 us
  Pallas kernels  661 us (90%)
  local copies, waits for them, and re-layouts  27.1 us (4%)
  other arithmetic  24.5 us (3%)
  starting transfers between devices  10.8 us (1%)
    pallas_call x1, Pallas kernels, mlp_call(): pl.pallas_call(functools.partial(mlp_kernel, tiles), grid=(4 * subs,), in...  172 us
    pallas_call x1, Pallas kernels, front_call(): pl.pallas_call(functools.partial(front_kernel, tiles, min(256, slots)), g...  116 us
    pallas_call x1, Pallas kernels, attn_back_call(): pl.pallas_call(functools.partial(attn_back_kernel, ts), grid=(H,), in_spe...  116 us
    pallas_call x1, Pallas kernels, finish_call(): pl.pallas_call(finish_kernel, in_specs=[anywhere, vmem, vmem, vmem] + [an...  94.4 us
    pallas_call x1, Pallas kernels, start_call(): pl.pallas_call(start_kernel, in_specs=[anywhere, vmem] + [anywhere] * 2,...  92.1 us
    pallas_call x1, Pallas kernels, qkv_back_call(): pl.pallas_call(functools.partial(qkv_back_kernel, tm), grid=(parts,), in_...  37.7 us
    pallas_call x1, Pallas kernels, mid_back_call(): pl.pallas_call(mid_back_kernel, grid=(slots // tm,), in_specs=[tile] * 6...  21.2 us
  transfers between devices with their start and end apart: 3, of which 0 were waited for; matrix products, arithmetic and copies ran while one was open for 3% of the time, Pallas kernels for 30%

profile of v2, /device:TPU:0, one launch (start us, length us, event | category | flops | bytes accessed | tf_op | source)
XLA Modules:
  0.0 730.2 jit_solution(10650340039815364122)
XLA Ops:
  2.7 3.4 all-to-all-start
  6.2 1.2 dynamic_slice.7
  8.8 2.1 convert_element_type.41.ada_ref
  10.9 4.0 convert_element_type.42.x_ref
  15.9 2.4 slice_reduce_fusion
  20.2 3.4 all-to-all-start.2
  23.6 92.1 %gather_start.1 = (f32[2,1,3456]{2,1,0:T(1,128)}, f32[32,72]{1,0:T(8,128)}, f32[32,128]{1,0:T(8,128)}, bf16[2,512,1152]{2,1,0:T(8,128)(2,1)}, bf16[4,2,2,2,144,864]{5,4,3,2,1,0:T(8,128)(2,1)}) custom-call(f32[1,1280]{1,0:T(1,128)} %concatenate.15.silu_ref, bf16[72,3456]{1,0:T(8,128)(2,1)} %convert_element_type.41.ada_ref, ...), custom_call_target="tpu_custom_call" | custom-call | tf_op jit(solution)/shard_map/gather_start/pallas_call | solution.py:535
  118.1 4.0 convert_element_type.46.cot_p
  126.9 4.5 all_to_all.76
  131.4 4.0 all-to-all-start.3
  135.3 116.3 %front.1 = (bf16[48,1024,72]{2,1,0:T(8,128)(2,1)}, bf16[1024,1152]{1,0:T(8,128)(2,1)}, bf16[16,1024,72]{2,1,0:T(8,128)(2,1)}, f32[16,1,1024]{2,1,0:T(1,128)}, bf...) custom-call(s32[1]{0:T(128)} %dynamic_slice.6.kind_ref, ...), custom_call_target="tpu_custom_call" | custom-call | tf_op jit(solution)/shard_map/front/pallas_call | solution.py:678
  251.6 11.1 %out_projection.1 = (bf16[1024,1152]{1,0:T(8,128)(2,1)}, bf16[1024,1152]{1,0:T(8,128)(2,1)}, bf16[1024,1152]{1,0:T(8,128)(2,1)}, bf16[1024,1152]{1,0:T(8,128)(2,1)}) custom-call(bf16[16,1024,72]{2,1,0:T(8,128)(2,1)} %get-tuple-element.61.o_ref, bf16[1024,1152]{1,0:T(8,128)(2,1)} %bitcast.32, bf16[1024,1152]{1,0:T(8,128)(2,1)} %bitcast.40, ...), custom_call_target="tpu_custom_call" | custom-call | tf_op jit(solution)/shard_map/out_projection/pallas_call | solution.py:96
  263.4 172.5 %feed_forward_both_ways.1 = (f32[1024,1152]{1,0:T(8,128)}, f32[1024,1152]{1,0:T(8,128)}, f32[4,1,1152]{2,1,0:T(1,128)}, bf16[4,2,2,2,144,576]{5,4,3,2,1,0:T(8,12...) custom-call(bf16[1024,1152]{1,0:T(8,128)(2,1)} %get-tuple-element.65, ...), custom_call_target="tpu_custom_call" | custom-call | tf_op jit(solution)/shard_map/feed_forward_both_ways/pallas_call | solution.py:1340
  435.9 21.2 %middle_backward.1 = (bf16[1024,1152]{1,0:T(8,128)(2,1)}, f32[1024,1152]{1,0:T(8,128)}, bf16[16,1024,72]{2,1,0:T(8,128)(2,1)}, bf16[8,4,144,288]{3,2,1,0:T(8,128)(2,1)}, f32[8,1152]{1,0:T(8,128)}) custom-call(bf16[1024,1152]{1,0:T(8,128)(2,1)} %bitcast.33, bf16[1024,1152]{1,0:T(8,128)(2,1)} %get-tuple-element.64.branch_ref, ...), custom_call_target="tpu_custom_call" | custom-call | tf_op jit(solution)/shard_map/middle_backward/pallas_call | solution.py:172
  457.1 116.0 %attention_backward.1 = (bf16[3,16,1024,72]{3,2,1,0:T(8,128)(2,1)}, bf16[2,512,1152]{2,1,0:T(8,128)(2,1)}, f32[2,72,576]{2,1,0:T(8,128)}, f32[144,576]{1,0:T(8,128)}, f32[2,72,288]{2,1,0:T(8,128)}) custom-call(s32[1]{0:T(128)} %dynamic_slice.6.kind_ref, bf16[48,1024,72]{2,1,0:T(8,128)(2,1)} %get-tuple-element.60.q_ref.k_ref.v_ref, ...), custom_call_target="tpu_custom_call" | custom-call | tf_op jit(solution)/shard_map/attention_backward/pallas_call | solution.py:1108
  573.1 37.7 %qkv_backward.1 = (bf16[1024,1152]{1,0:T(8,128)(2,1)}, bf16[8,4,144,864]{3,2,1,0:T(8,128)(2,1)}, f32[4,1,864]{2,1,0:T(1,128)}, f32[8,1152]{1,0:T(8,128)}) custom-call(bf16[48,1024,72]{2,1,0:T(8,128)(2,1)} %bitcast.39, bf16[1024,1152]{1,0:T(8,128)(2,1)} %get-tuple-element.80.norm_ref, bf16[8,4,144,864]{3,2,1,0:T(8,128)(2,1)} %bitcast.36, ...), custom_call_target="tpu_custom_call" | custom-call | tf_op jit(solution)/shard_map/qkv_backward/pallas_call | solution.py:1441
  613.8 94.4 %sum_finish.1 = (f32[1,16128]{1,0:T(1,128)}, f32[72,3456]{1,0:T(8,128)}, f32[32,1,128]{2,1,0:T(1,128)}, bf16[2,512,1152]{2,1,0:T(8,128)(2,1)}, f32[2,72,864]{2,1,0:T(8,128)}) custom-call(f32[1,16128]{1,0:T(1,128)} %reshape.132.row_ref, bf16[72,3456]{1,0:T(8,128)(2,1)} %convert_element_type.41.ada_ref, f32[32,72]{1,0:T(8,128)} %get-tuple-element.86.rows_ref, ...), custom_call_target="tpu_custom_call" | custom-call | tf_op jit(solution)/shard_map/sum_finish/pallas_call | solution.py:997
  708.2 1.4 slice_reduce_fusion.2
  709.6 1.4 slice_reduce_fusion.3
  713.3 2.3 reshape.138
  715.8 4.3 convert_element_type.48
  721.6 2.5 convert_element_type.47
  725.0 2.0 pad_maximum_fusion.1
  727.1 2.0 slice_reduce_fusion.7
  (114 shorter events, 21.9 us)
Async XLA Ops:
  2.7 17.5 %all-to-all-start = ((bf16[72,2,864]{2,0,1:T(8,128)(2,1)}), bf16[72,2,864]{2,0,1:T(8,128)(2,1)S(1)}, u32[]{:S(2)}, u32[]{:S(2)}) async-start(bf16[72,2,864]{2,0,1:T(8,128)(2,1)} %copy.57), calls=%async_computation | async-start | bytes 516096 | tf_op jit(solution)/shard_map/all_to_all | solution.py:1485
  8.8 6.1 copy-start.6
  14.9 101.7 %copy-start.12 = (f32[6912]{0:T(1024)S(1)}, f32[6912]{0:T(1024)}, u32[]{:S(2)}) copy-start(f32[6912]{0:T(1024)} %param.21) | copy-start | bytes 82948
  14.9 101.7 %copy-start.22 = (s32[2]{0:T(128)S(1)}, s32[2]{0:T(128)}, u32[]{:S(2)}) copy-start(s32[2]{0:T(128)} %param.19) | copy-start | bytes 28
  14.9 102.3 %copy-start.4 = (f32[288,576]{1,0:T(8,128)S(1)}, f32[288,576]{1,0:T(8,128)}, u32[]{:S(2)}) copy-start(f32[288,576]{1,0:T(8,128)} %param.29) | copy-start | bytes 1990660
  20.2 3.4 copy-start.1
  20.2 106.7 %all-to-all-start.2 = ((bf16[72,2,576]{2,0,1:T(8,128)(2,1)}), bf16[72,2,576]{2,0,1:T(8,128)(2,1)S(1)}, u32[]{:S(2)}, u32[]{:S(2)}) async-start(bf16[72,2,576]{2,0,1:T(8,128)(2,1)} %copy.60), calls=%async_computation.2 | async-start | bytes 368640 | tf_op jit(solution)/shard_map/all_to_all | solution.py:1485
  117.2 4.9 copy-start.11
  117.3 5.6 copy-start.18
  117.3 5.6 copy-start.19
  118.1 5.5 copy-start.20
  118.1 7.3 %copy-start.14 = (f32[4608]{0:T(1024)S(1)}, f32[4608]{0:T(1024)}, u32[]{:S(2)}) copy-start(f32[4608]{0:T(1024)} %param.28) | copy-start | bytes 55300
  118.1 8.2 %copy-start.21 = (f32[1152]{0:T(1024)S(1)}, f32[1152]{0:T(1024)}, u32[]{:S(2)}) copy-start(f32[1152]{0:T(1024)} %param.30) | copy-start | bytes 13828
  126.8 8.5 %copy-start.5 = (bf16[72,2,576]{2,0,1:T(8,128)(2,1)}, bf16[72,2,576]{2,0,1:T(8,128)(2,1)S(1)}, u32[]{:S(2)}) copy-start(bf16[72,2,576]{2,0,1:T(8,128)(2,1)S(1)} %all-to-all-done.2) | copy-start | bytes 497668
  131.4 131.4 %all-to-all-start.3 = ((bf16[72,2,576]{2,0,1:T(8,128)(2,1)}), bf16[72,2,576]{2,0,1:T(8,128)(2,1)S(1)}, u32[]{:S(2)}, u32[]{:S(2)}) async-start(bf16[72,2,576]{2,0,1:T(8,128)(2,1)} %copy.62), calls=%async_computation.3 | async-start | bytes 368640 | tf_op jit(solution)/shard_map/all_to_all | solution.py:1485
  573.1 38.6 %copy-start.13 = (f32[8,1152]{1,0:T(8,128)S(1)}, f32[8,1152]{1,0:T(8,128)}, u32[]{:S(2)}) copy-start(f32[8,1152]{1,0:T(8,128)} %get-tuple-element.83) | copy-start | bytes 110596
  573.1 39.5 %copy-start.16 = (f32[4,1,1152]{2,1,0:T(1,128)S(1)}, f32[4,1,1152]{2,1,0:T(1,128)}, u32[]{:S(2)}) copy-start(f32[4,1,1152]{2,1,0:T(1,128)} %get-tuple-element.85) | copy-start | bytes 55300
  613.8 97.2 %copy-start.9 = (f32[2,72,576]{2,1,0:T(8,128)S(1)}, f32[2,72,576]{2,1,0:T(8,128)}, u32[]{:S(2)}) copy-start(f32[2,72,576]{2,1,0:T(8,128)} %get-tuple-element.96) | copy-start | bytes 995332
  613.8 97.9 %copy-start.8 = (f32[2,72,576]{2,1,0:T(8,128)S(1)}, f32[2,72,576]{2,1,0:T(8,128)}, u32[]{:S(2)}) copy-start(f32[2,72,576]{2,1,0:T(8,128)} %get-tuple-element.95) | copy-start | bytes 995332
  711.6 4.0 copy-start.17
  713.3 6.8 copy-start.7
  715.8 5.8 copy-start
  721.6 5.5 copy-start.15
  721.6 7.4 %copy-start.2 = (f32[72,3456]{1,0:T(8,128)S(1)}, f32[72,3456]{1,0:T(8,128)}, u32[]{:S(2)}) copy-start(f32[72,3456]{1,0:T(8,128)} %get-tuple-element.138) | copy-start | bytes 2985988
  (2 other events, 3.2 us)

commit v3 on v2

--- a/solution.py
+++ b/solution.py
@@ -335,6 +335,13 @@
 WIDE = ("zyxc", "yzxc")
 
 
+AHEAD = 2
+
+
+def fresh(pairs, tick):
+    return pairs[:AHEAD] if tick == 0 else pairs[tick + AHEAD - 1 : tick + AHEAD]
+
+
 class Gathers:
     def __init__(self, place, sems, spans, orders):
         self.pairs = []
@@ -349,8 +356,8 @@
         self.ticks = len(self.pairs) + 3
 
     def advance(self, tick):
-        if tick < len(self.pairs):
-            for unit in self.pairs[tick]:
+        for pair in fresh(self.pairs, tick):
+            for unit in pair:
                 unit.own()
                 unit.start(0)
         for stage in (1, 0, 2, 3):
@@ -394,33 +401,33 @@
 
 
 class Exchange:
-    def __init__(self, place, sems, mine, whole):
+    def __init__(self, place, sems, mine, whole, chunks):
         self.place, self.sems, self.mine, self.whole = place, sems, mine, whole
-
-    def start(self):
+        self.spans = spans_of(mine.shape[1], chunks)
+        self.sent = []
+
+    def start(self, which):
         place = self.place
         at = place.at["y"]
-        self.kept = self.sems.local(lambda: (self.mine.at[at], self.whole.at[at]))
+        rows = pl.ds(*self.spans[which])
+        if which == 0:
+            self.kept = self.sems.local(lambda: (self.mine.at[at], self.whole.at[at]))
 
         def ends(step):
             other = place.after("y", step)
-            return self.mine.at[other], self.whole.at[at], place.device("y", other)
-
-        self.sent = [
-            (step, self.sems.copy(functools.partial(ends, step)))
-            for step in range(1, place.size["y"])
-        ]
-        return self
+            return self.mine.at[other, rows], self.whole.at[at, rows], place.device("y", other)
+
+        for step in range(1, place.size["y"]):
+            self.sent.append((step, rows, self.sems.copy(functools.partial(ends, step))))
 
     def finish(self):
         self.kept.wait()
-        for step, slot in self.sent:
+        for step, rows, slot in self.sent:
             index = self.place.before("y", step)
-            self.sems.arrived(slot, self.whole.at[index], self.place.device("y", index))
-
-
-def exchange(place, sems, mine, whole):
-    return Exchange(place, sems, mine, whole).start().finish
+            self.sems.arrived(slot, self.whole.at[index, rows], self.place.device("y", index))
+
+
+EXCHANGE_CHUNKS = 4
 
 
 START_ORDERS = (WIDE,)
@@ -502,8 +509,10 @@
         push(step).wait_send()
         return carry
 
-    x_done = exchange(place, sems, x_ref, x_full)
+    x_move = Exchange(place, sems, x_ref, x_full, EXCHANGE_CHUNKS)
     gathers.advance(2)
+    for which in range(2):
+        x_move.start(which)
     lax.fori_loop(1, count, do_wait, 0)
     heads = place.size["y"]
     for y in range(heads):
@@ -513,7 +522,9 @@
         )
     for tick in range(3, gathers.ticks + 1):
         gathers.advance(tick)
-    x_done()
+        if tick < EXCHANGE_CHUNKS + 1:
+            x_move.start(tick - 1)
+    x_move.finish()
     sems.drain()
     lax.fori_loop(1, count, do_sent, 0)
 
@@ -528,7 +539,7 @@
         [silu.astype(bf16).astype(f32), jnp.broadcast_to(order_mine.astype(f32), (1, lanes))], axis=1
     )
     sizes = {"z": 4, "x": 2, "c": dp // 8, "y": head}
-    needed = sems_needed(sizes, 5, 2 * head)
+    needed = sems_needed(sizes, 5, 1 + EXCHANGE_CHUNKS * head)
     anywhere = pl.BlockSpec(memory_space=pl.ANY)
     vmem = pl.BlockSpec(memory_space=pltpu.VMEM)
     slot_shape = x.shape
@@ -581,7 +592,7 @@
     gathers = Gathers(place, sems, wanted, FRONT_ORDERS)
     keep = pltpu.make_async_copy(qkv_s, qkv_ref, copied.at[0])
     keep_norm = pltpu.make_async_copy(norm_s, norm_ref, copied.at[1])
-    cot_done = None
+    cot_move = Exchange(place, sems, cot_p, cot_f, EXCHANGE_CHUNKS)
     for tick in range(gathers.ticks):
         at = min(FRONT_STEPS[tick], last)
         if tick == 0:
@@ -594,14 +605,11 @@
                 met(place)
                 gathers.advance(0)
         elif at < last:
-            if tick == 1:
-                cot_done = Exchange(place, sems, cot_p, cot_f)
-
             @pl.when(step == at)
             def _(tick=tick):
                 gathers.advance(tick)
-                if tick == 1:
-                    cot_done.start()
+                if tick in FRONT_EXCHANGE:
+                    cot_move.start(FRONT_EXCHANGE.index(tick))
 
     @pl.when(step < first_head)
     def _():
@@ -649,12 +657,13 @@
             if FRONT_STEPS[tick] >= last:
                 gathers.advance(tick)
         gathers.advance(gathers.ticks)
-        cot_done.finish()
+        cot_move.finish()
         keep.wait()
         keep_norm.wait()
         sems.drain()
 
 
+FRONT_EXCHANGE = (1, 2, 4, 5)
 FRONT_STEPS = (1, 3, 6, 10, 14, 18, 21, 99)
 
 
@@ -665,7 +674,7 @@
     size = width // H
     sizes = sizes_of()
     lead = tuple(sizes[a] for a in AXES)
-    needed = sems_needed(sizes, 10, 2 * sizes["y"])
+    needed = sems_needed(sizes, 10, 1 + EXCHANGE_CHUNKS * sizes["y"])
     first_head = parts * tiles
     anywhere = pl.BlockSpec(memory_space=pl.ANY)
 
@@ -845,8 +854,8 @@
         self.ticks = len(self.pairs) + 3
 
     def advance(self, tick):
-        if tick < len(self.pairs):
-            for unit, *_ in self.pairs[tick]:
+        for pair in fresh(self.pairs, tick):
+            for unit, *_ in pair:
                 unit.start(0)
         for stage in (0, 2, 1, 3):
             if 0 <= tick - 1 - stage < len(self.pairs):
@@ -921,15 +930,16 @@
     rows = Gather(place, sems, row_ref, row_s, "zxyc")
     rows.own()
     rows.start(0)
-    gin_done = exchange(place, sems, gin_ref, gin_full)
+    gin_move = Exchange(place, sems, gin_ref, gin_full, EXCHANGE_CHUNKS)
     sums.advance(0)
-    for tick in range(1, sums.ticks + 1):
+    gin_move.start(0)
+    for tick in range(1, 5):
         sums.advance(tick)
-        if tick < 5:
-            rows.wait(tick - 1)
-            if tick < 4:
-                rows.start(tick)
-    sums.deliver()
+        if tick < EXCHANGE_CHUNKS:
+            gin_move.start(tick)
+        rows.wait(tick - 1)
+        if tick < 4:
+            rows.start(tick)
 
     whole = row_s[...].reshape(count, row_ref.shape[1])
     bias_ref[...] = jnp.sum(whole, axis=0, keepdims=True)
@@ -978,9 +988,12 @@
 
     lax.fori_loop(1, count, do_push, 0)
     gsilu_ref[me] = share_s[me]
+    for tick in range(5, sums.ticks + 1):
+        sums.advance(tick)
+    sums.deliver()
     lax.fori_loop(1, count, do_wait, 0)
     sums.delivered()
-    gin_done()
+    gin_move.finish()
     sems.drain()
 
 
@@ -993,7 +1006,7 @@
     count = 8 * near * sizes["y"]
     anywhere = pl.BlockSpec(memory_space=pl.ANY)
     vmem = pl.BlockSpec(memory_space=pltpu.VMEM)
-    needed = sems_needed(sizes, 2 + FINISH_SPANS, 2 * sizes["y"] + 4 * near)
+    needed = sems_needed(sizes, 2 + FINISH_SPANS, 1 + EXCHANGE_CHUNKS * sizes["y"] + 4 * near)
     return pl.pallas_call(
         finish_kernel,
         in_specs=[anywhere, vmem, vmem, vmem] + [anywhere] * 2,
@@ -1025,23 +1038,22 @@
     )(row, ada, silu_rows, hot, gin, qkv)
 
 
-BACK_SPANS = (4, 4, 2)
-BACK_STEPS = (1, 2, 4, 7, 10, 13, 99, 99)
+BACK_SPANS = (4, 4)
+BACK_STEPS = (1, 2, 4, 7, 10, 13, 99)
 
 
 def attn_back_kernel(
-    ts, kind_ref, q_ref, k_ref, v_ref, g_ref, lse_ref, act_p, up_p, down_p, out_p,
-    out_ref, act_f, dup_ref, ddown_ref, dout_ref, dk_s, dv_s, send, recv, *scratch,
+    ts, kind_ref, q_ref, k_ref, v_ref, g_ref, lse_ref, up_p, down_p,
+    out_ref, dup_ref, ddown_ref, dk_s, dv_s, send, recv, *scratch,
 ):
     step = pl.program_id(0)
     last = pl.num_programs(0) - 1
     place = Place()
     sems = Sems(send, recv)
     sums = Sums(
-        place, sems, list(zip((up_p, down_p, out_p), BACK_SPANS)), (dup_ref, ddown_ref, dout_ref),
-        scratch, BACK_ORDERS,
-    )
-    act_move = Exchange(place, sems, act_p, act_f)
+        place, sems, list(zip((up_p, down_p), BACK_SPANS)), (dup_ref, ddown_ref), scratch,
+        BACK_ORDERS,
+    )
 
     @pl.when(step == 0)
     def _():
@@ -1054,8 +1066,6 @@
                 if tick == 0:
                     met(place)
                 sums.advance(tick)
-                if tick == 2:
-                    act_move.start()
 
     slots, size = q_ref.shape[1:]
     kept = slots - slots // 16
@@ -1094,11 +1104,10 @@
         sums.advance(sums.ticks)
         sums.deliver()
         sums.delivered()
-        act_move.finish()
         sems.drain()
 
 
-def attn_back_call(kind, qkv, grad, lse, act, up, down, out):
+def attn_back_call(kind, qkv, grad, lse, up, down):
     _, slots, size = qkv.shape
     ts = min(256, slots)
     block = (1, slots, size)
@@ -1116,14 +1125,12 @@
             pl.BlockSpec(block, lambda h: (h, 0, 0)),
             pl.BlockSpec((1, 1, slots), lambda h: (h, 0, 0)),
         ]
-        + [anywhere] * 4,
-        out_specs=[pl.BlockSpec((3, 1, slots, size), lambda h: (0, h, 0, 0))] + [anywhere] * 4,
+        + [anywhere] * 2,
+        out_specs=[pl.BlockSpec((3, 1, slots, size), lambda h: (0, h, 0, 0))] + [anywhere] * 2,
         out_shape=[
             jax.ShapeDtypeStruct((3, H, slots, size), bf16),
-            jax.ShapeDtypeStruct(act.shape, bf16),
             final_shape(up, sizes["c"]),
             jax.ShapeDtypeStruct(down.shape[4:], f32),
-            final_shape(out, sizes["c"]),
         ],
         scratch_shapes=[
             pltpu.VMEM((slots, size), f32),
@@ -1135,7 +1142,7 @@
             sizes,
             [
                 grad.shape[4:] + (at == 1, count)
-                for at, (grad, count) in enumerate(zip((up, down, out), BACK_SPANS))
+                for at, (grad, count) in enumerate(zip((up, down), BACK_SPANS))
             ],
             BACK_ORDERS,
         ),
@@ -1143,7 +1150,7 @@
             collective_id=2, has_side_effects=True, vmem_limit_bytes=VMEM_MOST
         ),
         name="attention_backward",
-    )(kind, qkv, qkv, qkv, grad, lse, act, up, down, out)
+    )(kind, qkv, qkv, qkv, grad, lse, up, down)
 
 
 MLP_SPANS = 4
@@ -1378,15 +1385,33 @@
 MLP_VMEM = 63 * 1024 * 1024
 
 
+QKV_SPANS = 2
+QKV_ORDERS = (EVEN,)
+
+
 def qkv_back_kernel(
-    tm, g_ref, norm_ref, w_ref, x_ref, gmid_ref, mod_ref,
-    gin_ref, dw_ref, bias_ref, sums_ref, norm_t, gp_s, gn_s,
+    tm, g_ref, norm_ref, w_ref, x_ref, gmid_ref, mod_ref, act_p, out_p,
+    gin_ref, dw_ref, bias_ref, sums_ref, act_f, dout_ref, norm_t, gp_s, gn_s, send, recv, *scratch,
 ):
     part = pl.program_id(0)
     slots, width = x_ref.shape
     tiles = slots // tm
     groups, _, rows_each, part_width = w_ref.shape
     heads = g_ref.shape[0]
+    last = pl.num_programs(0) - 1
+
+    place = Place()
+    sems = Sems(send, recv)
+    sums = Sums(place, sems, [(out_p, QKV_SPANS)], (dout_ref,), scratch, QKV_ORDERS)
+    act_move = Exchange(place, sems, act_p, act_f, EXCHANGE_CHUNKS)
+    for tick in range(4):
+        @pl.when(part == tick)
+        def _(tick=tick):
+            if tick == 0:
+                greet(place)
+                met(place)
+            sums.advance(tick)
+            act_move.start(tick)
 
     @pl.when(part == 0)
     def _():
@@ -1430,13 +1455,24 @@
         sums_ref[0:1, :] = shift
         sums_ref[1:2, :] = scale
 
-
-def qkv_back_call(grad, norm, weight, x, gmid, mod):
+    @pl.when(part == last)
+    def _():
+        sums.advance(4)
+        sums.deliver()
+        sums.delivered()
+        act_move.finish()
+        sems.drain()
+
+
+def qkv_back_call(grad, norm, weight, x, gmid, mod, act, out):
     slots, width = x.shape
     tm = min(256, slots)
     size = width // H
     groups, parts, rows_each, part_width = weight.shape
     heads = part_width // size
+    sizes = sizes_of()
+    anywhere = pl.BlockSpec(memory_space=pl.ANY)
+    needed = sems_needed(sizes, QKV_SPANS, 1 + EXCHANGE_CHUNKS * sizes["y"] + 4 * sizes["c"])
     w_spec = pl.BlockSpec((groups, 1, rows_each, part_width), lambda p: (0, place(p), 0, 0))
     return pl.pallas_call(
         functools.partial(qkv_back_kernel, tm),
@@ -1448,27 +1484,38 @@
             once_spec((slots, width)),
             once_spec((slots, width)),
             whole_spec(mod.shape),
+            anywhere,
+            anywhere,
         ],
         out_specs=[
             once_spec((slots, width)),
             w_spec,
             pl.BlockSpec((1, 1, part_width), lambda p: (p, 0, 0)),
             whole_spec((8, width)),
+            anywhere,
+            anywhere,
         ],
         out_shape=[
             jax.ShapeDtypeStruct((slots, width), bf16),
             jax.ShapeDtypeStruct(weight.shape, bf16),
             jax.ShapeDtypeStruct((parts, 1, part_width), f32),
             jax.ShapeDtypeStruct((8, width), f32),
+            jax.ShapeDtypeStruct(act.shape, bf16),
+            final_shape(out, sizes["c"]),
         ],
         scratch_shapes=[
             pltpu.VMEM((width, slots), bf16),
             pltpu.VMEM((slots, part_width), bf16),
             pltpu.VMEM((slots, width), f32),
-        ],
-        compiler_params=params(),
+            pltpu.SemaphoreType.DMA((needed,)),
+            pltpu.SemaphoreType.DMA((needed,)),
+        ]
+        + sum_scratch(sizes, [out.shape[4:] + (False, QKV_SPANS)], QKV_ORDERS),
+        compiler_params=pltpu.CompilerParams(
+            collective_id=5, has_side_effects=True, vmem_limit_bytes=VMEM_MOST
+        ),
         name="qkv_backward",
-    )(grad, norm, weight, x, gmid, mod)
+    )(grad, norm, weight, x, gmid, mod, act, out)
 
 
 class Wire:
@@ -1481,11 +1528,19 @@
             list(range(first, first + self.near)) for first in range(0, self.dp, self.near)
         ]
 
-    def piece(self, weight):
-        return lax.all_to_all(
-            weight.astype(bf16), "dp", split_axis=1, concat_axis=0,
-            axis_index_groups=self.groups, tiled=True,
+    def pieces(self, weights):
+        rows = weights[0].shape[0]
+        stack = jnp.concatenate(
+            [weight.astype(bf16).reshape(rows, self.near, -1) for weight in weights], axis=2
         )
+        stack = lax.all_to_all(
+            stack, "dp", split_axis=1, concat_axis=0, axis_index_groups=self.groups, tiled=True
+        )
+        stack = stack.reshape(rows * self.near, -1)
+        ends = [0]
+        for weight in weights:
+            ends.append(ends[-1] + weight.shape[1] // self.near)
+        return [stack[:, low:high] for low, high in zip(ends, ends[1:])]
 
     def columns(self, stack):
         devices, rows, cols = stack.shape
@@ -1527,10 +1582,15 @@
     rows_ada, cols_ada = weight_ada.shape
     ada_low = weight_ada.astype(bf16)
     silu_own, silu_pull = jax.vjp(lambda v: v * jax.nn.sigmoid(v), cond)
+    chunk = weight_down.shape[0] // 2
+    up_phases = weight_up.reshape(rows_ada, -1, 2, chunk)
+    up0_p, up1_p, qkv_p, out_p = wire.pieces(
+        [up_phases[:, :, at].reshape(rows_ada, -1) for at in range(2)] + [weight_qkv, weight_out]
+    )
     order_mine = lax.dynamic_slice_in_dim(order, head_at, 1, 0)
     kind = lax.dynamic_slice_in_dim(grid_kind, head_at, 1, 0)
     mod, silu_grouped, hot, x, qkv_full = start_call(
-        silu_own, order_mine, ada_low, inputs.astype(bf16), wire.piece(weight_qkv)
+        silu_own, order_mine, ada_low, inputs.astype(bf16), qkv_p
     )
     x = x.reshape(-1, width)
     device_stack = lambda full: full.reshape((-1,) + full.shape[4:])
@@ -1539,20 +1599,17 @@
     mod = jnp.concatenate([mod_flat, jnp.zeros((2, width), f32)], axis=0)
 
     bias_qkv = jnp.concatenate([bias_query, jnp.zeros_like(bias_query), bias_value])
-    chunk = weight_down.shape[0] // 2
-    up_phases = weight_up.astype(bf16).reshape(rows_ada, -1, 2, chunk)
-    up0, up1 = (wire.piece(up_phases[:, :, at].reshape(rows_ada, -1)) for at in range(2))
     down0, down1 = (weight_down[at * chunk : (at + 1) * chunk].astype(bf16) for at in range(2))
     bias_phases = bias_up.reshape(-1, 2, chunk).swapaxes(0, 1).reshape(4, 1, -1)
     qkv, norm, mix, lse, out_full, up_full, down_full, cot = front_call(
         kind, x, mod, qkv_full, bias_qkv.reshape(4, 1, -1),
-        wire.piece(weight_out), up0, down0, cotangent.astype(bf16),
+        out_p, up0_p, down0, cotangent.astype(bf16),
     )
     cot = cot.reshape(-1, width)
     out_full = wire.columns(device_stack(out_full))
     attended, branch, second, gm = out_call(mix, x, cot, mod, out_full, bias_out)
     mlp, gsec, d_bias_up, _, _, _, _, d_up1, d_down1, d_up0, d_down0 = mlp_call(
-        second, gm, up_full, down_full, up1, down1, bias_phases
+        second, gm, up_full, down_full, up1_p, down1, bias_phases
     )
     d_bias_up = d_bias_up.reshape(2, -1, chunk).swapaxes(0, 1)
     act, gmid, gatt, d_out, sums = mid_back_call(
@@ -1561,11 +1618,10 @@
     lead = (4, 2, dp_count // 8, head_count)
     stack = lambda grad: grad.reshape(lead + grad.shape[1:])
     by_image = lambda array: array.reshape(head_count, slot_local, width)
-    grad, act, d_up1, d_down1, d_out = attn_back_call(
-        kind, qkv, gatt, lse, by_image(act), d_up1, d_down1, stack(wire.uncolumns(d_out))
-    )
-    gin, d_qkv, d_bias_qkv, sums_in = qkv_back_call(
-        grad.reshape(qkv.shape), norm, qkv_full, x, gmid, mod
+    grad, d_up1, d_down1 = attn_back_call(kind, qkv, gatt, lse, d_up1, d_down1)
+    gin, d_qkv, d_bias_qkv, sums_in, act, d_out = qkv_back_call(
+        grad.reshape(qkv.shape), norm, qkv_full, x, gmid, mod, by_image(act),
+        stack(wire.uncolumns(d_out)),
     )
 
     bias_qkv_sum = d_bias_qkv.reshape(3, width)

time: 737 us -> 691 us (0.938)
  Pallas kernels: 661 us -> 628 us
    pallas_call x1, Pallas kernels: 116 us -> 83.4 us  [attn_back_call(): pl.pallas_call(functools.partial(attn_back_kernel, ts), grid=(H,), in_spe...]
    pallas_call x1, Pallas kernels: 37.7 us -> 54.4 us  [qkv_back_call(): pl.pallas_call(functools.partial(qkv_back_kernel, tm), grid=(parts,), in_...]
    pallas_call x1, Pallas kernels: 116 us -> 105 us  [front_call(): pl.pallas_call(functools.partial(front_kernel, tiles, min(256, slots)), g...]
  transfers between devices with their start and end apart: 3 -> 1, of which waited for: 0 -> 1; matrix products, arithmetic and copies ran while one was open for 3% -> 0% of each run, Pallas kernels for 30% -> 0%
where the time goes in v3:
time: 691 us; the launch traced here: 686 us
  Pallas kernels  628 us (91%)
  local copies, waits for them, and re-layouts  27.1 us (4%)
  other arithmetic  22.7 us (3%)
    pallas_call x1, Pallas kernels, mlp_call(): pl.pallas_call(functools.partial(mlp_kernel, tiles), grid=(4 * subs,), in...  177 us
    pallas_call x1, Pallas kernels, front_call(): pl.pallas_call(functools.partial(front_kernel, tiles, min(256, slots)), g...  105 us
    pallas_call x1, Pallas kernels, start_call(): pl.pallas_call(start_kernel, in_specs=[anywhere, vmem] + [anywhere] * 2,...  88.9 us
    pallas_call x1, Pallas kernels, finish_call(): pl.pallas_call(finish_kernel, in_specs=[anywhere, vmem, vmem, vmem] + [an...  88.1 us
    pallas_call x1, Pallas kernels, attn_back_call(): pl.pallas_call(functools.partial(attn_back_kernel, ts), grid=(H,), in_spe...  83.4 us
    pallas_call x1, Pallas kernels, qkv_back_call(): pl.pallas_call(functools.partial(qkv_back_kernel, tm), grid=(parts,), in_...  54.4 us
    pallas_call x1, Pallas kernels, mid_back_call(): pl.pallas_call(mid_back_kernel, grid=(slots // tm,), in_specs=[tile] * 6...  21.2 us
  transfers between devices with their start and end apart: 1, of which 1 were waited for; matrix products, arithmetic and copies ran while one was open for 0% of the time, Pallas kernels for 0%

profile of v3, /device:TPU:0, one launch (start us, length us, event | category | flops | bytes accessed | tf_op | source)
XLA Modules:
  0.0 686.0 jit_solution(7216499248065113537)
XLA Ops:
  0.7 1.2 convert.10
  1.9 1.0 reshape.144
  2.9 2.4 slice_reduce_fusion
  6.9 1.1 concatenate.19
  8.1 4.0 all-to-all-start
  12.1 1.8 all-to-all-done
  18.3 4.1 convert_element_type.49.x_ref
  23.0 88.9 %gather_start.1 = (f32[2,1,3456]{2,1,0:T(1,128)}, f32[32,72]{1,0:T(8,128)}, f32[32,128]{1,0:T(8,128)}, bf16[2,512,1152]{2,1,0:T(8,128)(2,1)}, bf16[4,2,2,2,144,864]{5,4,3,2,1,0:T(8,128)(2,1)}) custom-call(f32[1,1280]{1,0:T(1,128)} %concatenate.18.silu_ref, bf16[72,3456]{1,0:T(8,128)(2,1)} %convert_element_type.48.ada_ref, ...), custom_call_target="tpu_custom_call" | custom-call | tf_op jit(solution)/shard_map/gather_start/pallas_call | solution.py:546
  114.3 4.0 convert_element_type.54.cot_p
  121.6 104.6 %front.1 = (bf16[48,1024,72]{2,1,0:T(8,128)(2,1)}, bf16[1024,1152]{1,0:T(8,128)(2,1)}, bf16[16,1024,72]{2,1,0:T(8,128)(2,1)}, f32[16,1,1024]{2,1,0:T(1,128)}, bf...) custom-call(s32[1]{0:T(128)} %dynamic_slice.6.kind_ref, ...), custom_call_target="tpu_custom_call" | custom-call | tf_op jit(solution)/shard_map/front/pallas_call | solution.py:687
  226.2 11.1 %out_projection.1 = (bf16[1024,1152]{1,0:T(8,128)(2,1)}, bf16[1024,1152]{1,0:T(8,128)(2,1)}, bf16[1024,1152]{1,0:T(8,128)(2,1)}, bf16[1024,1152]{1,0:T(8,128)(2,1)}) custom-call(bf16[16,1024,72]{2,1,0:T(8,128)(2,1)} %get-tuple-element.61.o_ref, bf16[1024,1152]{1,0:T(8,128)(2,1)} %bitcast.25, bf16[1024,1152]{1,0:T(8,128)(2,1)} %bitcast.33, ...), custom_call_target="tpu_custom_call" | custom-call | tf_op jit(solution)/shard_map/out_projection/pallas_call | solution.py:96
  237.3 176.6 %feed_forward_both_ways.1 = (f32[1024,1152]{1,0:T(8,128)}, f32[1024,1152]{1,0:T(8,128)}, f32[4,1,1152]{2,1,0:T(1,128)}, bf16[4,2,2,2,144,576]{5,4,3,2,1,0:T(8,12...) custom-call(bf16[1024,1152]{1,0:T(8,128)(2,1)} %get-tuple-element.65, ...), custom_call_target="tpu_custom_call" | custom-call | tf_op jit(solution)/shard_map/feed_forward_both_ways/pallas_call | solution.py:1347
  413.9 21.2 %middle_backward.1 = (bf16[1024,1152]{1,0:T(8,128)(2,1)}, f32[1024,1152]{1,0:T(8,128)}, bf16[16,1024,72]{2,1,0:T(8,128)(2,1)}, bf16[8,4,144,288]{3,2,1,0:T(8,128)(2,1)}, f32[8,1152]{1,0:T(8,128)}) custom-call(bf16[1024,1152]{1,0:T(8,128)(2,1)} %bitcast.26, bf16[1024,1152]{1,0:T(8,128)(2,1)} %get-tuple-element.64.branch_ref, ...), custom_call_target="tpu_custom_call" | custom-call | tf_op jit(solution)/shard_map/middle_backward/pallas_call | solution.py:172
  435.1 83.4 %attention_backward.1 = (bf16[3,16,1024,72]{3,2,1,0:T(8,128)(2,1)}, f32[2,72,576]{2,1,0:T(8,128)}, f32[144,576]{1,0:T(8,128)}) custom-call(s32[1]{0:T(128)} %dynamic_slice.6.kind_ref, bf16[48,1024,72]{2,1,0:T(8,128)(2,1)} %get-tuple-element.60.q_ref.k_ref.v_ref, bf16[48,1024,72]{2,1,0:T(8,128)(2,1)} %get-tuple-element.60.q_ref.k_ref.v_ref, ...), custom_call_target="tpu_custom_call" | custom-call | tf_op jit(solution)/shard_map/attention_backward/pallas_call | solution.py:1117
  518.5 54.4 %qkv_backward.1 = (bf16[1024,1152]{1,0:T(8,128)(2,1)}, bf16[8,4,144,864]{3,2,1,0:T(8,128)(2,1)}, f32[4,1,864]{2,1,0:T(1,128)}, f32[8,1152]{1,0:T(8,128)}, bf16[2...) custom-call(bf16[48,1024,72]{2,1,0:T(8,128)(2,1)} %bitcast.32, bf16[1024,1152]{1,0:T(8,128)(2,1)} %get-tuple-element.77.norm_ref, ...), custom_call_target="tpu_custom_call" | custom-call | tf_op jit(solution)/shard_map/qkv_backward/pallas_call | solution.py:1477
  575.9 88.1 %sum_finish.1 = (f32[1,16128]{1,0:T(1,128)}, f32[72,3456]{1,0:T(8,128)}, f32[32,1,128]{2,1,0:T(1,128)}, bf16[2,512,1152]{2,1,0:T(8,128)(2,1)}, f32[2,72,864]{2,1,0:T(8,128)}) custom-call(f32[1,16128]{1,0:T(1,128)} %reshape.137.row_ref, bf16[72,3456]{1,0:T(8,128)(2,1)} %convert_element_type.48.ada_ref, f32[32,72]{1,0:T(8,128)} %get-tuple-element.86.rows_ref, ...), custom_call_target="tpu_custom_call" | custom-call | tf_op jit(solution)/shard_map/sum_finish/pallas_call | solution.py:1010
  664.1 1.4 slice_reduce_fusion.2
  665.5 1.4 slice_reduce_fusion.3
  669.2 2.3 reshape.143
  671.7 4.3 convert_element_type.56
  676.2 1.2 reshape.141
  677.4 2.5 convert_element_type.55
  680.9 2.0 pad_maximum_fusion.1
  682.9 2.0 slice_reduce_fusion.7
  (111 shorter events, 18.9 us)
Async XLA Ops:
  0.6 5.7 copy-start.4
  0.7 6.1 copy-start.9
  5.3 10.9 %copy-start.20 = (s32[2]{0:T(128)S(1)}, s32[2]{0:T(128)}, u32[]{:S(2)}) copy-start(s32[2]{0:T(128)} %param.18) | copy-start | bytes 28
  5.3 12.1 %copy-start.13 = (f32[1,1152]{1,0:T(1,128)S(1)}, f32[1,1152]{1,0:T(1,128)}, u32[]{:S(2)}) copy-start(f32[1,1152]{1,0:T(1,128)} %param.17) | copy-start | bytes 13828
  5.3 12.1 %copy-start.1 = (f32[72,3456]{1,0:T(8,128)S(1)}, f32[72,3456]{1,0:T(8,128)}, u32[]{:S(2)}) copy-start(f32[72,3456]{1,0:T(8,128)} %param.20) | copy-start | bytes 2985988
  8.1 5.9 all-to-all-start
  18.3 94.5 %copy-start.10 = (f32[6912]{0:T(1024)S(1)}, f32[6912]{0:T(1024)}, u32[]{:S(2)}) copy-start(f32[6912]{0:T(1024)} %param.21) | copy-start | bytes 82948
  18.3 94.5 %copy-start.21 = (s32[2]{0:T(128)S(1)}, s32[2]{0:T(128)}, u32[]{:S(2)}) copy-start(s32[2]{0:T(128)} %param.19) | copy-start | bytes 28
  18.3 95.1 %copy-start.3 = (f32[288,576]{1,0:T(8,128)S(1)}, f32[288,576]{1,0:T(8,128)}, u32[]{:S(2)}) copy-start(f32[288,576]{1,0:T(8,128)} %param.29) | copy-start | bytes 1990660
  113.4 5.4 copy-start.16
  113.5 5.4 copy-start.17
  113.5 6.1 copy-start.18
  113.5 6.7 copy-start.12
  113.5 7.5 %copy-start.19 = (f32[1152]{0:T(1024)S(1)}, f32[1152]{0:T(1024)}, u32[]{:S(2)}) copy-start(f32[1152]{0:T(1024)} %param.30) | copy-start | bytes 13828
  518.5 55.3 %copy-start.11 = (f32[8,1152]{1,0:T(8,128)S(1)}, f32[8,1152]{1,0:T(8,128)}, u32[]{:S(2)}) copy-start(f32[8,1152]{1,0:T(8,128)} %get-tuple-element.83) | copy-start | bytes 110596
  518.5 56.3 %copy-start.14 = (f32[4,1,1152]{2,1,0:T(1,128)S(1)}, f32[4,1,1152]{2,1,0:T(1,128)}, u32[]{:S(2)}) copy-start(f32[4,1,1152]{2,1,0:T(1,128)} %get-tuple-element.85) | copy-start | bytes 55300
  575.9 90.9 %copy-start.7 = (f32[2,72,576]{2,1,0:T(8,128)S(1)}, f32[2,72,576]{2,1,0:T(8,128)}, u32[]{:S(2)}) copy-start(f32[2,72,576]{2,1,0:T(8,128)} %get-tuple-element.96) | copy-start | bytes 995332
  575.9 91.6 %copy-start.6 = (f32[2,72,576]{2,1,0:T(8,128)S(1)}, f32[2,72,576]{2,1,0:T(8,128)}, u32[]{:S(2)}) copy-start(f32[2,72,576]{2,1,0:T(8,128)} %get-tuple-element.95) | copy-start | bytes 995332
  667.5 4.0 copy-start.15
  669.2 6.8 copy-start.5
  671.6 5.8 copy-start
  677.4 2.5 copy-start.8
  677.4 7.4 %copy-start.2 = (f32[72,3456]{1,0:T(8,128)S(1)}, f32[72,3456]{1,0:T(8,128)}, u32[]{:S(2)}) copy-start(f32[72,3456]{1,0:T(8,128)} %get-tuple-element.140) | copy-start | bytes 2985988

commit v4 on v3

--- a/solution.py
+++ b/solution.py
@@ -459,7 +459,9 @@
     silu.start(2)
     silu.wait(2)
     silu.start(3)
+    x_move = Exchange(place, sems, x_ref, x_full, EXCHANGE_CHUNKS)
     gathers.advance(1)
+    x_move.start(0)
     silu.wait(3)
 
     rows = silu_s[...].reshape(count, silu_ref.shape[1])
@@ -509,10 +511,8 @@
         push(step).wait_send()
         return carry
 
-    x_move = Exchange(place, sems, x_ref, x_full, EXCHANGE_CHUNKS)
     gathers.advance(2)
-    for which in range(2):
-        x_move.start(which)
+    x_move.start(1)
     lax.fori_loop(1, count, do_wait, 0)
     heads = place.size["y"]
     for y in range(heads):
@@ -1039,7 +1039,7 @@
 
 
 BACK_SPANS = (4, 4)
-BACK_STEPS = (1, 2, 4, 7, 10, 13, 99)
+BACK_STEPS = (1, 2, 4, 6, 9, 11, 13)
 
 
 def attn_back_kernel(
@@ -1154,8 +1154,8 @@
 
 
 MLP_SPANS = 4
-MLP_GATHER = (1, 2, 3, 5, 7, 9, 11)
-MLP_SUM = (12, 13, 15, 17, 19, 21, 22)
+MLP_GATHER = (1, 2, 3, 4, 6, 8, 10)
+MLP_SUM = (12, 13, 14, 16, 18, 20, 22)
 
 
 def mlp_kernel(

time: 691 us -> 688 us (level)
  no operation moved by 1% of the time
where the time goes in v4:
time: 688 us; the launch traced here: 683 us
  Pallas kernels  625 us (91%)
  local copies, waits for them, and re-layouts  27.1 us (4%)
  other arithmetic  22.7 us (3%)
    pallas_call x1, Pallas kernels, mlp_call(): pl.pallas_call(functools.partial(mlp_kernel, tiles), grid=(4 * subs,), in...  173 us
    pallas_call x1, Pallas kernels, front_call(): pl.pallas_call(functools.partial(front_kernel, tiles, min(256, slots)), g...  105 us
    pallas_call x1, Pallas kernels, start_call(): pl.pallas_call(start_kernel, in_specs=[anywhere, vmem] + [anywhere] * 2,...  88.4 us
    pallas_call x1, Pallas kernels, finish_call(): pl.pallas_call(finish_kernel, in_specs=[anywhere, vmem, vmem, vmem] + [an...  87.7 us
    pallas_call x1, Pallas kernels, attn_back_call(): pl.pallas_call(functools.partial(attn_back_kernel, ts), grid=(H,), in_spe...  85.3 us
    pallas_call x1, Pallas kernels, qkv_back_call(): pl.pallas_call(functools.partial(qkv_back_kernel, tm), grid=(parts,), in_...  53.6 us
    pallas_call x1, Pallas kernels, mid_back_call(): pl.pallas_call(mid_back_kernel, grid=(slots // tm,), in_specs=[tile] * 6...  21.2 us
  transfers between devices with their start and end apart: 1, of which 1 were waited for; matrix products, arithmetic and copies ran while one was open for 0% of the time, Pallas kernels for 0%

profile of v4, /device:TPU:0, one launch (start us, length us, event | category | flops | bytes accessed | tf_op | source)
XLA Modules:
  0.0 683.1 jit_solution(2278625995013813799)
XLA Ops:
  0.7 1.2 convert.10
  1.9 1.0 reshape.144
  2.9 2.4 slice_reduce_fusion
  6.9 1.1 concatenate.19
  8.1 4.0 all-to-all-start
  12.1 1.8 all-to-all-done
  18.3 4.1 convert_element_type.49.x_ref
  23.0 88.4 %gather_start.1 = (f32[2,1,3456]{2,1,0:T(1,128)}, f32[32,72]{1,0:T(8,128)}, f32[32,128]{1,0:T(8,128)}, bf16[2,512,1152]{2,1,0:T(8,128)(2,1)}, bf16[4,2,2,2,144,864]{5,4,3,2,1,0:T(8,128)(2,1)}) custom-call(f32[1,1280]{1,0:T(1,128)} %concatenate.18.silu_ref, bf16[72,3456]{1,0:T(8,128)(2,1)} %convert_element_type.48.ada_ref, ...), custom_call_target="tpu_custom_call" | custom-call | tf_op jit(solution)/shard_map/gather_start/pallas_call | solution.py:546
  113.7 4.0 convert_element_type.54.cot_p
  121.1 105.1 %front.1 = (bf16[48,1024,72]{2,1,0:T(8,128)(2,1)}, bf16[1024,1152]{1,0:T(8,128)(2,1)}, bf16[16,1024,72]{2,1,0:T(8,128)(2,1)}, f32[16,1,1024]{2,1,0:T(1,128)}, bf...) custom-call(s32[1]{0:T(128)} %dynamic_slice.6.kind_ref, ...), custom_call_target="tpu_custom_call" | custom-call | tf_op jit(solution)/shard_map/front/pallas_call | solution.py:687
  226.2 11.1 %out_projection.1 = (bf16[1024,1152]{1,0:T(8,128)(2,1)}, bf16[1024,1152]{1,0:T(8,128)(2,1)}, bf16[1024,1152]{1,0:T(8,128)(2,1)}, bf16[1024,1152]{1,0:T(8,128)(2,1)}) custom-call(bf16[16,1024,72]{2,1,0:T(8,128)(2,1)} %get-tuple-element.61.o_ref, bf16[1024,1152]{1,0:T(8,128)(2,1)} %bitcast.25, bf16[1024,1152]{1,0:T(8,128)(2,1)} %bitcast.33, ...), custom_call_target="tpu_custom_call" | custom-call | tf_op jit(solution)/shard_map/out_projection/pallas_call | solution.py:96
  237.3 173.0 %feed_forward_both_ways.1 = (f32[1024,1152]{1,0:T(8,128)}, f32[1024,1152]{1,0:T(8,128)}, f32[4,1,1152]{2,1,0:T(1,128)}, bf16[4,2,2,2,144,576]{5,4,3,2,1,0:T(8,12...) custom-call(bf16[1024,1152]{1,0:T(8,128)(2,1)} %get-tuple-element.65, ...), custom_call_target="tpu_custom_call" | custom-call | tf_op jit(solution)/shard_map/feed_forward_both_ways/pallas_call | solution.py:1347
  410.3 21.2 %middle_backward.1 = (bf16[1024,1152]{1,0:T(8,128)(2,1)}, f32[1024,1152]{1,0:T(8,128)}, bf16[16,1024,72]{2,1,0:T(8,128)(2,1)}, bf16[8,4,144,288]{3,2,1,0:T(8,128)(2,1)}, f32[8,1152]{1,0:T(8,128)}) custom-call(bf16[1024,1152]{1,0:T(8,128)(2,1)} %bitcast.26, bf16[1024,1152]{1,0:T(8,128)(2,1)} %get-tuple-element.64.branch_ref, ...), custom_call_target="tpu_custom_call" | custom-call | tf_op jit(solution)/shard_map/middle_backward/pallas_call | solution.py:172
  431.5 85.3 %attention_backward.1 = (bf16[3,16,1024,72]{3,2,1,0:T(8,128)(2,1)}, f32[2,72,576]{2,1,0:T(8,128)}, f32[144,576]{1,0:T(8,128)}) custom-call(s32[1]{0:T(128)} %dynamic_slice.6.kind_ref, bf16[48,1024,72]{2,1,0:T(8,128)(2,1)} %get-tuple-element.60.q_ref.k_ref.v_ref, bf16[48,1024,72]{2,1,0:T(8,128)(2,1)} %get-tuple-element.60.q_ref.k_ref.v_ref, ...), custom_call_target="tpu_custom_call" | custom-call | tf_op jit(solution)/shard_map/attention_backward/pallas_call | solution.py:1117
  516.9 53.6 %qkv_backward.1 = (bf16[1024,1152]{1,0:T(8,128)(2,1)}, bf16[8,4,144,864]{3,2,1,0:T(8,128)(2,1)}, f32[4,1,864]{2,1,0:T(1,128)}, f32[8,1152]{1,0:T(8,128)}, bf16[2...) custom-call(bf16[48,1024,72]{2,1,0:T(8,128)(2,1)} %bitcast.32, bf16[1024,1152]{1,0:T(8,128)(2,1)} %get-tuple-element.77.norm_ref, ...), custom_call_target="tpu_custom_call" | custom-call | tf_op jit(solution)/shard_map/qkv_backward/pallas_call | solution.py:1477
  573.5 87.7 %sum_finish.1 = (f32[1,16128]{1,0:T(1,128)}, f32[72,3456]{1,0:T(8,128)}, f32[32,1,128]{2,1,0:T(1,128)}, bf16[2,512,1152]{2,1,0:T(8,128)(2,1)}, f32[2,72,864]{2,1,0:T(8,128)}) custom-call(f32[1,16128]{1,0:T(1,128)} %reshape.137.row_ref, bf16[72,3456]{1,0:T(8,128)(2,1)} %convert_element_type.48.ada_ref, f32[32,72]{1,0:T(8,128)} %get-tuple-element.86.rows_ref, ...), custom_call_target="tpu_custom_call" | custom-call | tf_op jit(solution)/shard_map/sum_finish/pallas_call | solution.py:1010
  661.2 1.4 slice_reduce_fusion.2
  662.6 1.4 slice_reduce_fusion.3
  666.3 2.3 reshape.143
  668.8 4.3 convert_element_type.56
  673.4 1.2 reshape.141
  674.6 2.5 convert_element_type.55
  678.0 2.0 pad_maximum_fusion.1
  680.0 2.0 slice_reduce_fusion.7
  (111 shorter events, 18.9 us)
Async XLA Ops:
  0.6 5.7 copy-start.4
  0.7 6.1 copy-start.9
  5.3 10.9 %copy-start.20 = (s32[2]{0:T(128)S(1)}, s32[2]{0:T(128)}, u32[]{:S(2)}) copy-start(s32[2]{0:T(128)} %param.18) | copy-start | bytes 28
  5.3 12.1 %copy-start.13 = (f32[1,1152]{1,0:T(1,128)S(1)}, f32[1,1152]{1,0:T(1,128)}, u32[]{:S(2)}) copy-start(f32[1,1152]{1,0:T(1,128)} %param.17) | copy-start | bytes 13828
  5.3 12.1 %copy-start.1 = (f32[72,3456]{1,0:T(8,128)S(1)}, f32[72,3456]{1,0:T(8,128)}, u32[]{:S(2)}) copy-start(f32[72,3456]{1,0:T(8,128)} %param.20) | copy-start | bytes 2985988
  8.1 5.9 all-to-all-start
  18.3 93.9 %copy-start.10 = (f32[6912]{0:T(1024)S(1)}, f32[6912]{0:T(1024)}, u32[]{:S(2)}) copy-start(f32[6912]{0:T(1024)} %param.21) | copy-start | bytes 82948
  18.3 93.9 %copy-start.21 = (s32[2]{0:T(128)S(1)}, s32[2]{0:T(128)}, u32[]{:S(2)}) copy-start(s32[2]{0:T(128)} %param.19) | copy-start | bytes 28
  18.3 94.5 %copy-start.3 = (f32[288,576]{1,0:T(8,128)S(1)}, f32[288,576]{1,0:T(8,128)}, u32[]{:S(2)}) copy-start(f32[288,576]{1,0:T(8,128)} %param.29) | copy-start | bytes 1990660
  112.9 5.4 copy-start.16
  112.9 5.4 copy-start.17
  112.9 6.1 copy-start.18
  112.9 6.7 copy-start.12
  113.0 7.5 %copy-start.19 = (f32[1152]{0:T(1024)S(1)}, f32[1152]{0:T(1024)}, u32[]{:S(2)}) copy-start(f32[1152]{0:T(1024)} %param.30) | copy-start | bytes 13828
  516.9 54.5 %copy-start.11 = (f32[8,1152]{1,0:T(8,128)S(1)}, f32[8,1152]{1,0:T(8,128)}, u32[]{:S(2)}) copy-start(f32[8,1152]{1,0:T(8,128)} %get-tuple-element.83) | copy-start | bytes 110596
  516.9 55.5 %copy-start.14 = (f32[4,1,1152]{2,1,0:T(1,128)S(1)}, f32[4,1,1152]{2,1,0:T(1,128)}, u32[]{:S(2)}) copy-start(f32[4,1,1152]{2,1,0:T(1,128)} %get-tuple-element.85) | copy-start | bytes 55300
  573.5 90.5 %copy-start.7 = (f32[2,72,576]{2,1,0:T(8,128)S(1)}, f32[2,72,576]{2,1,0:T(8,128)}, u32[]{:S(2)}) copy-start(f32[2,72,576]{2,1,0:T(8,128)} %get-tuple-element.96) | copy-start | bytes 995332
  573.5 91.2 %copy-start.6 = (f32[2,72,576]{2,1,0:T(8,128)S(1)}, f32[2,72,576]{2,1,0:T(8,128)}, u32[]{:S(2)}) copy-start(f32[2,72,576]{2,1,0:T(8,128)} %get-tuple-element.95) | copy-start | bytes 995332
  664.6 4.0 copy-start.15
  666.3 6.8 copy-start.5
  668.8 5.8 copy-start
  674.5 2.5 copy-start.8
  674.5 7.4 %copy-start.2 = (f32[72,3456]{1,0:T(8,128)S(1)}, f32[72,3456]{1,0:T(8,128)}, u32[]{:S(2)}) copy-start(f32[72,3456]{1,0:T(8,128)} %get-tuple-element.140) | copy-start | bytes 2985988
